TPU v7x, 32 devices: a whole 2x2x4 slice. The times are simulated.
32 devices in a mesh: dp: 4 (over y, core), cuts: 8 (over z, x).
Axes of the slice: x: 2, y: 2, z: 4, core: 2. Of those that a mesh axis runs over, the one named last changes fastest.
Arguments:
- hidden: bfloat16 [4, 256, 8192], P('dp', None, 'cuts'), may hold values from -6 to 6
- down_weight: bfloat16 [4, 8192, 3072], P('dp', 'cuts'), may hold values from -0.0625 to 0.0625
- expert_ids: int32 [512, 2], P('dp'), may hold values from 0 to 7, all different within a row; in each aligned block of 128 rows (0 to 127, 128 to 255, ...) at most 64 rows name the same one
- combine: float32 [512, 2], P('dp'), may hold values from 0.1 to 1
- out_grad: bfloat16 [512, 3072], P('dp', 'cuts'), may hold values from -6 to 6
Outputs:
- mixed: bfloat16 [512, 3072], P('dp', 'cuts')
- hidden_grad: bfloat16 [4, 256, 8192], P('dp', None, 'cuts')
- weight_grad: bfloat16 [4, 8192, 3072], P('dp', 'cuts')
Inputs may be any that keep to these rules, and one draw needn't show every extreme that they name: `expert_ids`: the two ids of a row differ. Among the 256 pairs of one index of dp, no expert is named more than 64 times, a bound that some block reaches.
All inputs are finite; a program needn't handle non-finite values.
Results may differ from a plain program's by a relative error of at most 0.0049.
Values may be sent and summed in bfloat16 or wider, within the bound.
No kernel may reach another device: no remote copies, remote signals or barrier semaphores. Data moves between devices by JAX's collectives and lax.ppermute only.
A program may use at most 64 MiB of HBM per device.

v0:
```python
import jax
import jax.numpy as jnp
from jax import lax
from jax.sharding import PartitionSpec as P


def local(hidden, down_weight, expert_ids, combine, out_grad):
    dp_count = lax.axis_size("dp")
    tok_rows = expert_ids.shape[0]
    capacity = 2 * tok_rows // dp_count
    slot_count = dp_count * capacity
    feat_share = out_grad.shape[1]
    width = down_weight.shape[2]
    flat_ids = expert_ids.reshape(-1)
    labels = jnp.arange(dp_count, dtype=jnp.int32)
    onehot = (flat_ids[:, None] == labels[None, :]).astype(jnp.int32)
    pair_rank = jnp.sum((jnp.cumsum(onehot, axis=0) - 1) * onehot, axis=1)
    inside = flat_ids < dp_count
    target = jnp.where(inside, flat_ids * capacity + pair_rank, dp_count * capacity)
    weights = combine.reshape(-1)
    full_grad = lax.all_gather(out_grad, "cuts", axis=1, tiled=True)
    scaled = (weights[:, None] * jnp.repeat(full_grad, 2, axis=0).astype(jnp.float32)).astype(
        jnp.bfloat16
    )
    outgoing = (
        jnp.zeros((dp_count * capacity, width), jnp.bfloat16).at[target].set(scaled, mode="drop")
    )
    incoming = lax.all_to_all(
        outgoing.reshape(dp_count, capacity, width), "dp", split_axis=0, concat_axis=0, tiled=True
    )
    grad_rows = incoming.reshape(slot_count, width)
    hidden_rows = hidden[0]
    weight = down_weight[0]
    own_share = lax.psum_scatter(
        lax.dot_general(
            weight, hidden_rows, (((0,), (1,)), ((), ())), preferred_element_type=jnp.float32
        ),
        "cuts",
        scatter_dimension=0,
        tiled=True,
    )
    hid_grad = lax.dot_general(
        grad_rows, weight, (((1,), (1,)), ((), ())), preferred_element_type=jnp.float32
    ).astype(jnp.bfloat16)
    down_grad = lax.dot_general(
        hidden_rows, grad_rows, (((0,), (0,)), ((), ())), preferred_element_type=jnp.float32
    ).astype(jnp.bfloat16)
    returned = lax.all_to_all(
        own_share.astype(jnp.bfloat16), "dp", split_axis=1, concat_axis=1, tiled=True
    )
    pick_index = jnp.minimum(target, dp_count * capacity - 1)
    picked = jnp.take(returned, pick_index, axis=1).astype(jnp.float32)
    pair_coef = jnp.where(inside, weights, jnp.zeros_like(weights))
    summed = jnp.sum((picked * pair_coef[None, :]).reshape(feat_share, tok_rows, 2), axis=2)
    mixed = summed.T.astype(jnp.bfloat16)
    return (mixed, hid_grad[None], down_grad[None])


def solution(mesh):
    return jax.shard_map(
        local,
        mesh=mesh,
        in_specs=(
            P("dp", None, "cuts"),
            P("dp", "cuts", None),
            P("dp", None),
            P("dp", None),
            P("dp", "cuts"),
        ),
        out_specs=(P("dp", "cuts"), P("dp", None, "cuts"), P("dp", "cuts", None)),
        check_vma=False,
    )
```

profile of v0, /device:TPU:0, one launch (start us, length us, event | category | flops | bytes accessed | tf_op | source)
XLA Modules:
  0.0 128.0 jit_solution(8152011908300580976)
XLA Ops:
  7.2 1.0 copy-done
  8.2 6.3 %fusion.2 = f32[3072,256]{1,0:T(8,128)} fusion(bf16[1,1024,3072]{2,1,0:T(8,128)(2,1)} %param.6, bf16[1,256,1024]{2,1,0:T(8,128)(2,1)S(1)} %copy-done), kind=kOutput, calls=%fused_computation.4 | convolution fusion | flops 1610612736 | bytes 9961472 | tf_op jit(solution)/shard_map/dot_general | solution.py:35
  14.6 0.6 copy-done.2
  15.2 0.1 copy.24
  15.3 0.1 eq.26
  15.5 0.1 reshape.132
  15.6 0.1 copy.34
  15.7 0.1 copy.31
  15.9 0.1 lt.64
  16.0 0.1 copy.32
  16.2 0.1 mul.48
  16.3 1.2 reduce-window.6
  17.6 0.1 copy.26
  17.9 0.1 mul.51
  18.0 37.5 %all_gather.3 = bf16[128,3072]{1,0:T(8,128)(2,1)S(1)} all-gather(bf16[128,384]{1,0:T(8,128)(2,1)S(1)} %copy-done.1), channel_id=1, replica_groups=mesh['dp'=4,'cuts'=8] {'cuts'}, dimensions={1}, use_global_device_ids=true | all-gather | bytes 884736 | tf_op jit(solution)/shard_map/all_gather | solution.py:21
  55.5 2.5 %broadcast_in_dim.40 = f32[128,2,3072]{2,1,0:T(2,128)} broadcast(bf16[128,3072]{1,0:T(8,128)(2,1)S(1)} %all_gather.3), dimensions={0,2} | broadcast | bytes 3932160 | tf_op jit(solution)/shard_map/broadcast_in_dim | solution.py:22
  58.0 5.3 %convert_element_type.43 = f32[256,3072]{1,0:T(8,128)} reshape(f32[128,2,3072]{2,1,0:T(2,128)} %broadcast_in_dim.40) | data formatting | bytes 6291456 | tf_op jit(solution)/shard_map/convert_element_type | solution.py:22
  63.4 5.4 %scatter_custom_fusion = bf16[256,3072]{1,0:T(8,128)(2,1)} fusion(s32[256]{0:T(256)S(1)} %bitcast.60, f32[256,3072]{1,0:T(8,128)} %convert_element_type.43, f32[256]{0:T(256)S(1)} %mul.51, bf16[]{:T(256)} %constant.36.clone.1), kind=kCustom, calls=%fused_computation.8 | custom fusion | flops 1572864 | bytes 4719618 | tf_op jit(solution)/shard_map/scatter | solution.py:26
  68.8 3.6 %all-to-all-start.1 = ((bf16[4,64,3072]{2,1,0:T(8,128)(2,1)}), bf16[4,64,3072]{2,1,0:T(8,128)(2,1)S(1)}, u32[]{:S(2)}, u32[]{:S(2)}) async-start(bf16[4,64,3072]{2,1,0:T(8,128)(2,1)} %bitcast.54), calls=%async_computation.2 | async-start | bytes 3145728 | tf_op jit(solution)/shard_map/all_to_all | solution.py:28
  72.4 0.1 reduce_sum.23
  72.5 0.1 copy.33
  72.7 0.1 copy.29
  72.9 19.5 %all-to-all-done.1 = bf16[4,64,3072]{2,1,0:T(8,128)(2,1)S(1)} async-done(((bf16[4,64,3072]{2,1,0:T(8,128)(2,1)}), bf16[4,64,3072]{2,1,0:T(8,128)(2,1)S(1)}, u32[]{:S(2)}, u32[]{:S(2)}) %all-to-all-start.1) | async-done | bytes 1572896 | tf_op jit(solution)/shard_map/all_to_all | solution.py:28
  92.4 5.5 %fusion.9 = bf16[1,256,1024]{2,1,0:T(8,128)(2,1)} fusion(bf16[256,3072]{1,0:T(8,128)(2,1)S(1)} %bitcast.52, bf16[1,1024,3072]{2,1,0:T(8,128)(2,1)} %param.6), kind=kOutput, calls=%fused_computation.11 | convolution fusion | flops 1610874880 | bytes 8388608 | tf_op jit(solution)/shard_map/dot_general | solution.py:42
  97.9 2.2 %reduce-scatter.2.cloned.1.call-done = f32[384,256]{1,0:T(8,128)} async-done(((f32[3072,256]{1,0:T(8,128)}), f32[384,256]{1,0:T(8,128)}) %reduce-scatter.2.cloned.1.call-update) | async-done | bytes 393232 | tf_op jit(solution)/shard_map/reduce_scatter | solution.py:34
  100.1 1.0 convert_element_type.38
  101.1 0.8 copy.30
  101.9 3.5 %all-to-all-start = ((bf16[384,4,64]{0,2,1:T(8,128)(2,1)}), bf16[384,4,64]{0,2,1:T(8,128)(2,1)S(1)}, u32[]{:S(2)}, u32[]{:S(2)}) async-start(bf16[384,4,64]{0,2,1:T(8,128)(2,1)} %bitcast.4), calls=%async_computation.1 | async-start | bytes 393216 | tf_op jit(solution)/shard_map/all_to_all | solution.py:48
  105.5 4.5 %convert_bitcast_fusion = bf16[1,1024,3072]{1,2,0:T(8,128)(2,1)} fusion(bf16[256,3072]{1,0:T(8,128)(2,1)S(1)} %bitcast.53, bf16[1,256,1024]{2,1,0:T(8,128)(2,1)S(1)} %copy-done), kind=kOutput, calls=%fused_computation.6 | convolution fusion | flops 1613758464 | bytes 8388608 | tf_op jit(solution)/shard_map/dot_general | solution.py:45
  110.0 8.6 %copy.35 = bf16[1,1024,3072]{2,1,0:T(8,128)(2,1)} copy(bf16[1,1024,3072]{1,2,0:T(8,128)(2,1)} %convert_bitcast_fusion) | data formatting | bytes 12582912
  118.6 1.2 gather_fusion
  119.9 1.3 %multiply_reduce_fusion = bf16[384,128]{0,1:T(8,128)(2,1)} fusion(bf16[384,128,2]{0,2,1:T(2,128)(2,1)S(1)} %gather.7, pred[128,2]{1,0:T(8,128)(4,1)S(1)} %copy.29, f32[128,2]{1,0:T(8,128)S(1)} %copy.33), kind=kLoop, calls=%fused_computation.15 | loop fusion | flops 344064 | bytes 296192 | tf_op jit(solution)/shard_map/reduce_sum | solution.py:54
  (23 shorter events, 0.6 us)
Async XLA Ops:
  7.2 1.0 copy-start
  7.2 92.9 %reduce-scatter.2.cloned.1.call-start = ((), (), s32[]{:S(2)}) async-start(), calls=%async_computation.3 | async-start | bytes 3538944 | tf_op jit(solution)/shard_map/reduce_scatter | solution.py:34
  14.5 0.7 copy-start.2
  14.5 1.1 copy-start.3
  14.5 3.5 %copy-start.1 = (bf16[128,384]{1,0:T(8,128)(2,1)S(1)}, bf16[128,384]{1,0:T(8,128)(2,1)}, u32[]{:S(2)}) copy-start(bf16[128,384]{1,0:T(8,128)(2,1)} %param.9) | copy-start | bytes 294916
  68.8 23.6 %all-to-all-start.1 = ((bf16[4,64,3072]{2,1,0:T(8,128)(2,1)}), bf16[4,64,3072]{2,1,0:T(8,128)(2,1)S(1)}, u32[]{:S(2)}, u32[]{:S(2)}) async-start(bf16[4,64,3072]{2,1,0:T(8,128)(2,1)} %bitcast.54), calls=%async_computation.2 | async-start | bytes 3145728 | tf_op jit(solution)/shard_map/all_to_all | solution.py:28
  101.9 16.7 %all-to-all-start = ((bf16[384,4,64]{0,2,1:T(8,128)(2,1)}), bf16[384,4,64]{0,2,1:T(8,128)(2,1)S(1)}, u32[]{:S(2)}, u32[]{:S(2)}) async-start(bf16[384,4,64]{0,2,1:T(8,128)(2,1)} %bitcast.4), calls=%async_computation.1 | async-start | bytes 393216 | tf_op jit(solution)/shard_map/all_to_all | solution.py:48
Sparse Core Ops, SparseCore 0:
  14.7 85.3 reduce-scatter.1
where the time goes:
time: 129 us; the launch traced here: 128 us
  blocking collectives  37.5 us (29%)
  local copies, waits for them, and re-layouts  22 us (17%)
  waiting for transfers between devices  21.8 us (17%)
  matrix products  16.3 us (13%)
  between operations  14.1 us (11%)
  other arithmetic  9.16 us (7%)
  starting transfers between devices  7.15 us (6%)
    all_gather x1, blocking collectives, local(): full_grad = lax.all_gather(out_grad, 'cuts', axis=1, tiled=True)  37.5 us
    all_to_all x1, waiting for transfers between devices, local(): lax.all_to_all(outgoing.reshape(dp_count, capacity, width), 'dp', split_a...  19.5 us
    unnamed x11, local copies, waits for them, and re-layouts  10.5 us
    dot_general x1, matrix products, local(): lax.dot_general(weight, hidden_rows, (((0,), (1,)), ((), ())), preferred_...  6.32 us
    dot_general x1, matrix products, local(): lax.dot_general(grad_rows, weight, (((1,), (1,)), ((), ())), preferred_el...  5.48 us
    scatter x1, other arithmetic, local(): jnp.zeros((dp_count * capacity, width), jnp.bfloat16).at[target]  5.42 us
    convert_element_type x1, local copies, waits for them, and re-layouts, local(): jnp.repeat(full_grad, 2, axis=0).astype(jnp.float32)  5.28 us
    dot_general x1, matrix products, local(): lax.dot_general(hidden_rows, grad_rows, (((0,), (0,)), ((), ())), preferr...  4.5 us
  transfers between devices with their start and end apart: 3, of which 2 were waited for; matrix products, arithmetic and copies ran while one was open for 27% of the time, Pallas kernels for 0%

commit v1 on v0

v1 whole, which is shorter than its diff:
```python
import functools

import jax
import jax.numpy as jnp
from jax import lax
from jax.experimental import pallas as pl
from jax.experimental.pallas import tpu as pltpu
from jax.sharding import PartitionSpec as P

BF, F32 = jnp.bfloat16, jnp.float32


def routed(hidden, down_weight, expert_ids, combine, out_grad):
    dp_count = lax.axis_size("dp")
    tok_rows = expert_ids.shape[0]
    capacity = 2 * tok_rows // dp_count
    slot_count = dp_count * capacity
    feat_share = out_grad.shape[1]
    width = down_weight.shape[2]
    flat_ids = expert_ids.reshape(-1)
    labels = jnp.arange(dp_count, dtype=jnp.int32)
    onehot = (flat_ids[:, None] == labels[None, :]).astype(jnp.int32)
    pair_rank = jnp.sum((jnp.cumsum(onehot, axis=0) - 1) * onehot, axis=1)
    inside = flat_ids < dp_count
    target = jnp.where(inside, flat_ids * capacity + pair_rank, dp_count * capacity)
    weights = combine.reshape(-1)
    full_grad = lax.all_gather(out_grad, "cuts", axis=1, tiled=True)
    scaled = (weights[:, None] * jnp.repeat(full_grad, 2, axis=0).astype(F32)).astype(BF)
    outgoing = jnp.zeros((dp_count * capacity, width), BF).at[target].set(scaled, mode="drop")
    incoming = lax.all_to_all(
        outgoing.reshape(dp_count, capacity, width), "dp", split_axis=0, concat_axis=0, tiled=True
    )
    grad_rows = incoming.reshape(slot_count, width)
    hidden_rows = hidden[0]
    weight = down_weight[0]
    own_share = lax.psum_scatter(
        lax.dot_general(weight, hidden_rows, (((0,), (1,)), ((), ())), preferred_element_type=F32),
        "cuts",
        scatter_dimension=0,
        tiled=True,
    )
    hid_grad = lax.dot_general(
        grad_rows, weight, (((1,), (1,)), ((), ())), preferred_element_type=F32
    ).astype(BF)
    down_grad = lax.dot_general(
        hidden_rows, grad_rows, (((0,), (0,)), ((), ())), preferred_element_type=F32
    ).astype(BF)
    returned = lax.all_to_all(
        own_share.astype(BF), "dp", split_axis=1, concat_axis=1, tiled=True
    )
    pick_index = jnp.minimum(target, dp_count * capacity - 1)
    picked = jnp.take(returned, pick_index, axis=1).astype(F32)
    pair_coef = jnp.where(inside, weights, jnp.zeros_like(weights))
    summed = jnp.sum((picked * pair_coef[None, :]).reshape(feat_share, tok_rows, 2), axis=2)
    mixed = summed.T.astype(BF)
    return (mixed, hid_grad[None], down_grad[None])


def routing(meta, expert, capacity):
    tok = meta.shape[1]
    label = jnp.full((1, tok), expert).astype(F32)
    first, second = meta[0:1] == label, meta[1:2] == label
    named = jnp.where(first, 1.0, jnp.where(second, 1.0, 0.0))
    weight = jnp.where(first, meta[2:3], jnp.where(second, meta[3:4], 0.0))
    earlier = lax.broadcasted_iota(jnp.int32, (tok, tok), 0) < lax.broadcasted_iota(
        jnp.int32, (tok, tok), 1
    )
    rank = jnp.dot(
        jnp.broadcast_to(named, (8, tok)).astype(BF),
        jnp.where(earlier, 1.0, 0.0).astype(BF),
        preferred_element_type=F32,
    )[0:1]
    slot = lax.broadcasted_iota(jnp.int32, (capacity, tok), 0).astype(F32)
    hot = jnp.where(slot == rank, named, 0.0)
    return hot, weight


def forward_kernel(capacity, hidden_ref, weight_ref, keep_ref, send_ref, rows_ref):
    me = lax.axis_index("dp")
    rows_ref[...] = jnp.dot(hidden_ref[0], weight_ref[0], preferred_element_type=F32)
    for dy in range(2):
        for dc, out in ((0, keep_ref), (1, send_ref)):
            source = me ^ (2 * dy + dc)
            at = pl.multiple_of(source * capacity, capacity)
            out[0, dy] = rows_ref[pl.ds(at, capacity), :].astype(BF)


def forward(hidden, weight, feat, dp_count):
    _, slots, ff = hidden.shape
    width = weight.shape[2]
    chunks, capacity = width // feat, slots // dp_count
    part = jax.ShapeDtypeStruct((chunks, 2, capacity, feat), BF)
    spec = pl.BlockSpec((1, 2, capacity, feat), lambda c: (c, 0, 0, 0))
    return pl.pallas_call(
        functools.partial(forward_kernel, capacity),
        grid=(chunks,),
        in_specs=[
            pl.BlockSpec((1, slots, ff), lambda c: (0, 0, 0)),
            pl.BlockSpec((1, ff, feat), lambda c: (0, 0, c)),
        ],
        out_specs=[spec, spec],
        out_shape=[part, part],
        scratch_shapes=[pltpu.VMEM((slots, feat), F32)],
        compiler_params=pltpu.CompilerParams(vmem_limit_bytes=24 << 20),
        cost_estimate=pl.CostEstimate(
            flops=2 * slots * ff * width, bytes_accessed=2 * (ff * width + slots * (ff + width)), transcendentals=0
        ),
        name="forward_rows",
    )(hidden, weight)


def spread_kernel(capacity, own_ref, near_ref, keep_ref, got_ref, *refs):
    outs, hots, cols = refs[:4], refs[4], refs[5]
    me, x = lax.axis_index("dp"), lax.axis_index("cuts") % 2

    @pl.when(pl.program_id(0) == 0)
    def _():
        for dy, meta_ref in enumerate((own_ref, near_ref)):
            for dc in range(2):
                hot, weight = routing(meta_ref[...], me ^ dc, capacity)
                tok = hot.shape[1]
                hots[dy, dc] = hot.astype(BF)
                cols[dy, dc] = jnp.broadcast_to(weight, (tok, tok)).T

    for dy in range(2):
        for dx in range(2):
            total = None
            for dc, rows in ((0, keep_ref), (1, got_ref)):
                picked = lax.dot_general(
                    hots[dy, dc], rows[0, x ^ dx, dy], (((0,), (0,)), ((), ())), preferred_element_type=F32
                )
                term = picked * cols[dy, dc][:, 0:1]
                total = term if total is None else total + term
            outs[2 * dy + dx][0] = total.astype(BF)


def spread(own, near, keep, got, nz):
    chunks, _, capacity, feat = keep.shape
    tok = own.shape[1]
    keep, got = (a.reshape(nz, 2, 2, capacity, feat) for a in (keep, got))
    rows = pl.BlockSpec((1, 2, 2, capacity, feat), lambda k: (k, 0, 0, 0, 0))
    meta = pl.BlockSpec((8, tok), lambda k: (0, 0))
    return pl.pallas_call(
        functools.partial(spread_kernel, capacity),
        grid=(nz,),
        in_specs=[meta, meta, rows, rows],
        out_specs=[pl.BlockSpec((1, tok, feat), lambda k: (k, 0, 0))] * 4,
        out_shape=[jax.ShapeDtypeStruct((nz, tok, feat), BF)] * 4,
        scratch_shapes=[pltpu.VMEM((2, 2, capacity, tok), BF), pltpu.VMEM((2, 2, tok, tok), F32)],
        compiler_params=pltpu.CompilerParams(vmem_limit_bytes=16 << 20),
        cost_estimate=pl.CostEstimate(
            flops=16 * tok * capacity * chunks * feat, bytes_accessed=24 * tok * chunks * feat, transcendentals=0
        ),
        name="spread_rows",
    )(own, near, keep, got)


def plane_sum_kernel(nz, a_ref, b_ref, c_ref, d_ref, *outs):
    z = lax.axis_index("cuts") // 2
    for k in range(nz):
        at = lax.rem(z + k, nz)
        total = (a_ref[at].astype(F32) + b_ref[at].astype(F32)) + (c_ref[at].astype(F32) + d_ref[at].astype(F32))
        outs[k][...] = total.astype(outs[k].dtype)


def plane_sum(parts):
    nz, tok, feat = parts[0].shape
    return pl.pallas_call(
        functools.partial(plane_sum_kernel, nz),
        out_shape=[jax.ShapeDtypeStruct((tok, feat), F32 if k == 0 else BF) for k in range(nz)],
        compiler_params=pltpu.CompilerParams(vmem_limit_bytes=16 << 20),
        name="plane_sum",
    )(*parts)


def backward_kernel(nz, capacity, pos_ref, hidden_ref, weight_ref, *refs):
    metas, grads, (hid_ref, down_ref), (hots, cols, turned, rows_ref, total) = (
        refs[:4], refs[4:12], refs[12:14], refs[14:],
    )
    step, me = pl.program_id(0), pos_ref[0]

    @pl.when(step == 0)
    def _():
        turned[...] = hidden_ref[0].T
        for q in range(4):
            hot, weight = routing(metas[q][...], me, capacity)
            hots[q] = hot.astype(BF)
            cols[q] = jnp.broadcast_to(jnp.sum(hot * weight, axis=1, keepdims=True), cols.shape[1:])

    def rows_of(dx):
        for q in range(4):
            picked = jnp.dot(hots[q], grads[4 * dx + q][0], preferred_element_type=F32)
            at = pl.multiple_of((me ^ q) * capacity, capacity)
            rows_ref[pl.ds(at, capacity), :] = (picked * cols[q][:, 0:1]).astype(BF)

    @pl.when(step < nz)
    def _():
        rows_of(0)

    @pl.when(step >= nz)
    def _():
        rows_of(1)

    rows = rows_ref[...]
    down_ref[0] = jnp.dot(turned[...], rows, preferred_element_type=F32).astype(BF)
    part = lax.dot_general(rows, weight_ref[0], (((1,), (1,)), ((), ())), preferred_element_type=F32)

    @pl.when(step == 0)
    def _():
        total[...] = part

    @pl.when(step > 0)
    def _():
        total[...] += part

    @pl.when(step == 2 * nz - 1)
    def _():
        hid_ref[0] = total[...].astype(BF)


def backward(pos, hidden, weight, metas, grads):
    nz, tok, feat = grads[0].shape
    _, slots, ff = hidden.shape
    width = weight.shape[2]
    capacity = slots // 4

    def column(g, pos):
        z = lax.rem(pos[2] - lax.rem(g, nz) + nz, nz)
        return (0, 0, 2 * z + (pos[1] ^ (g // nz)))

    first = pl.BlockSpec((1, tok, feat), lambda g, pos: (jnp.minimum(g, nz - 1), 0, 0))
    second = pl.BlockSpec((1, tok, feat), lambda g, pos: (jnp.maximum(g - nz, 0), 0, 0))
    whole = pl.BlockSpec((1, slots, ff), lambda g, pos: (0, 0, 0))
    return pl.pallas_call(
        functools.partial(backward_kernel, nz, capacity),
        grid_spec=pltpu.PrefetchScalarGridSpec(
            num_scalar_prefetch=1,
            grid=(2 * nz,),
            in_specs=[whole, pl.BlockSpec((1, ff, feat), column)]
            + [pl.BlockSpec((8, tok), lambda g, pos: (0, 0))] * 4
            + [first] * 4
            + [second] * 4,
            out_specs=[whole, pl.BlockSpec((1, ff, feat), column)],
            scratch_shapes=[
                pltpu.VMEM((4, capacity, tok), BF),
                pltpu.VMEM((4, capacity, 128), F32),
                pltpu.VMEM((ff, slots), BF),
                pltpu.VMEM((slots, feat), BF),
                pltpu.VMEM((slots, ff), F32),
            ],
        ),
        out_shape=[jax.ShapeDtypeStruct(hidden.shape, BF), jax.ShapeDtypeStruct(weight.shape, BF)],
        compiler_params=pltpu.CompilerParams(vmem_limit_bytes=32 << 20),
        cost_estimate=pl.CostEstimate(
            flops=4 * slots * ff * width,
            bytes_accessed=4 * ff * width + 4 * slots * ff + 8 * tok * width,
            transcendentals=0,
        ),
        name="backward_rows",
    )(pos, hidden, weight, *metas, *grads)


def shared(hidden, down_weight, expert_ids, combine, out_grad):
    dp_count, cut_count = lax.axis_size("dp"), lax.axis_size("cuts")
    nz = cut_count // 2
    tok, feat = out_grad.shape

    def send(value, dp_flip, cut_flip):
        pairs = [
            (d * cut_count + c, (d ^ dp_flip) * cut_count + (c ^ cut_flip))
            for d in range(dp_count)
            for c in range(cut_count)
        ]
        return lax.ppermute(value, ("dp", "cuts"), pairs)

    def along(value, k):
        return lax.ppermute(value, "cuts", [(c, (c + 2 * k) % cut_count) for c in range(cut_count)])

    pos = jnp.stack([lax.axis_index("dp"), lax.axis_index("cuts") % 2, lax.axis_index("cuts") // 2]).astype(jnp.int32)
    own = jnp.concatenate([expert_ids.T.astype(F32), combine.T, jnp.zeros((4, tok), F32)])
    near = send(own, 2, 0)
    blocks = jnp.stack([out_grad] + [along(out_grad, k) for k in range(1, nz)])

    keep, away = forward(hidden, down_weight, feat, dp_count)
    got = send(away, 1, 0)
    mine, by_x, by_y, by_xy = spread(own, near, keep, got, nz)
    by_xy, by_x, by_y = send(by_xy, 2, 1), send(by_x, 0, 1), send(by_y, 2, 0)

    metas = (own, send(own, 1, 0), near, send(near, 1, 0))
    grads = []
    for dx in range(2):
        for dy in range(2):
            part = blocks if dx == dy == 0 else send(blocks, 2 * dy, dx)
            grads += [part, send(part, 1, 0)]

    terms = plane_sum((mine, by_x, by_y, by_xy))
    total = terms[0]
    for k in range(1, nz):
        total = total + along(terms[k], k).astype(F32)
    mixed = total.astype(BF)

    hid_grad, down_grad = backward(pos, hidden, down_weight, metas, grads)
    return (mixed, hid_grad, down_grad)


def local(hidden, down_weight, expert_ids, combine, out_grad):
    dp_count, cut_count = lax.axis_size("dp"), lax.axis_size("cuts")
    few = dp_count == 4 and cut_count % 2 == 0 and dp_count * expert_ids.shape[0] <= 2 * hidden.shape[1]
    return (shared if few else routed)(hidden, down_weight, expert_ids, combine, out_grad)


def solution(mesh):
    return jax.shard_map(
        local,
        mesh=mesh,
        in_specs=(
            P("dp", None, "cuts"),
            P("dp", "cuts", None),
            P("dp", None),
            P("dp", None),
            P("dp", "cuts"),
        ),
        out_specs=(P("dp", "cuts"), P("dp", None, "cuts"), P("dp", "cuts", None)),
        check_vma=False,
    )
```

time: 129 us -> 86 us (0.67)
  blocking collectives: 37.5 us -> 0 us
  Pallas kernels: 0 us -> 20.4 us
  matrix products: 16.3 us -> 0 us
  local copies, waits for them, and re-layouts: 22 us -> 6.69 us
  waiting for transfers between devices: 21.8 us -> 36.9 us
  between operations: 14.1 us -> 0.71 us
  starting transfers between devices: 7.15 us -> 20.1 us
  other arithmetic: 9.16 us -> 0.9 us
    all_gather x1 -> x0, blocking collectives: 37.5 us -> none  [local(): full_grad = lax.all_gather(out_grad, 'cuts', axis=1, tiled=True)]
    ppermute x0 -> x20, waiting for transfers between devices: none -> 36.9 us  [the longest x14 28 us: send(): return lax.ppermute(value, ('dp', 'cuts'), pairs)]
    pallas_call x0 -> x4, Pallas kernels: none -> 20.4 us  [the longest x1 12.8 us: backward(): pl.pallas_call(functools.partial(backward_kernel, nz, capacity), grid_spe...]
    ppermute x0 -> x20, starting transfers between devices: none -> 20.1 us  [the longest x14 10.6 us: send(): return lax.ppermute(value, ('dp', 'cuts'), pairs)]
    all_to_all x2 -> x0, waiting for transfers between devices: 19.5 us -> none  [the longest x1 19.5 us: local(): lax.all_to_all(outgoing.reshape(dp_count, capacity, width), 'dp', split_a...]
    dot_general x3 -> x0, matrix products: 16.3 us -> none  [the longest x1 6.32 us: local(): lax.dot_general(weight, hidden_rows, (((0,), (1,)), ((), ())), preferred_...]
    all_to_all x2 -> x0, starting transfers between devices: 7.11 us -> none  [the longest x1 3.57 us: local(): lax.all_to_all(outgoing.reshape(dp_count, capacity, width), 'dp', split_a...]
    convert_element_type x2 -> x0, local copies, waits for them, and re-layouts: 6.09 us -> none  [the longest x1 5.28 us: local(): jnp.repeat(full_grad, 2, axis=0).astype(jnp.float32)]
  transfers between devices with their start and end apart: 3 -> 20, of which waited for: 2 -> 8; matrix products, arithmetic and copies ran while one was open for 27% -> 0% of each run, Pallas kernels for 0% -> 18%
where the time goes in v1:
time: 86 us; the launch traced here: 85.8 us
  waiting for transfers between devices  36.9 us (43%)
  Pallas kernels  20.4 us (24%)
  starting transfers between devices  20.1 us (23%)
  local copies, waits for them, and re-layouts  6.69 us (8%)
  other arithmetic  0.9 us (1%)
    ppermute x14, waiting for transfers between devices, send(): return lax.ppermute(value, ('dp', 'cuts'), pairs)  28 us
    pallas_call x1, Pallas kernels, backward(): pl.pallas_call(functools.partial(backward_kernel, nz, capacity), grid_spe...  12.8 us
    ppermute x14, starting transfers between devices, send(): return lax.ppermute(value, ('dp', 'cuts'), pairs)  10.6 us
    ppermute x6, starting transfers between devices, along(): lax.ppermute(value, 'cuts', [(c, (c + 2 * k) % cut_count) for c in range(...  9.56 us
    ppermute x6, waiting for transfers between devices, along(): lax.ppermute(value, 'cuts', [(c, (c + 2 * k) % cut_count) for c in range(...  8.88 us
    unnamed x14, local copies, waits for them, and re-layouts  6.62 us
    pallas_call x1, Pallas kernels, forward(): pl.pallas_call(functools.partial(forward_kernel, capacity), grid=(chunks,...  4.7 us
    pallas_call x1, Pallas kernels, spread(): pl.pallas_call(functools.partial(spread_kernel, capacity), grid=(nz,), in...  2.73 us
  transfers between devices with their start and end apart: 20, of which 8 were waited for; matrix products, arithmetic and copies ran while one was open for 0% of the time, Pallas kernels for 18%

profile of v1, /device:TPU:0, one launch (start us, length us, event | category | flops | bytes accessed | tf_op | source)
XLA Modules:
  0.0 85.8 jit_solution(5518298394572203949)
XLA Ops:
  0.6 2.8 %copy-done = bf16[1,1024,3072]{2,1,0:T(8,128)(2,1)S(1)} copy-done((bf16[1,1024,3072]{2,1,0:T(8,128)(2,1)S(1)}, bf16[1,1024,3072]{2,1,0:T(8,128)(2,1)}, u32[]{:S(2)}) %copy-start) | copy-done | bytes 6291480
  3.4 1.0 %copy-done.2 = bf16[1,256,1024]{2,1,0:T(8,128)(2,1)S(1)} copy-done((bf16[1,256,1024]{2,1,0:T(8,128)(2,1)S(1)}, bf16[1,256,1024]{2,1,0:T(8,128)(2,1)}, u32[]{:S(2)}) %copy-start.2) | copy-done | bytes 524312
  4.5 4.7 %forward_rows.1 = (bf16[8,2,64,384]{3,2,1,0:T(8,128)(2,1)S(1)}, bf16[8,2,64,384]{3,2,1,0:T(8,128)(2,1)S(1)}) custom-call(bf16[1,256,1024]{2,1,0:T(8,128)(2,1)S(1)} %copy-done.2, bf16[1,1024,3072]{2,1,0:T(8,128)(2,1)S(1)} %copy-done), custom_call_target="tpu_custom_call" | custom-call | flops 1610612736 | bytes 8388608 | tf_op jit(solution)/shard_map/forward_rows/pallas_call | solution.py:94
  9.2 0.5 collective-permute-start.1
  9.7 4.7 %collective-permute-start.12 = (bf16[128,384]{1,0:T(8,128)(2,1)S(1)}, bf16[128,384]{1,0:T(8,128)(2,1)S(1)}, u32[]{:S(2)}, u32[]{:S(2)}) collective-permute-start(bf16[128,384]{1,0:T(8,128)(2,1)S(1)} %copy-done.4), channel_id=1, source_target_pairs={{0,6},{1,7},{2,0},{3,1},{4,2},{5,3},{6,4},{7,5},{8,14},{9,15},{10,... | collective-permute-start | bytes 294920 | tf_op jit(solution)/shard_map/ppermute | solution.py:277
  14.4 1.0 %collective-permute-start.11 = (bf16[128,384]{1,0:T(8,128)(2,1)S(1)}, bf16[128,384]{1,0:T(8,128)(2,1)S(1)}, u32[]{:S(2)}, u32[]{:S(2)}) collective-permute-start(bf16[128,384]{1,0:T(8,128)(2,1)S(1)} %copy-done.4), channel_id=1, source_target_pairs={{0,4},{1,5},{2,6},{3,7},{4,0},{5,1},{6,2},{7,3},{8,12},{9,13},{10,... | collective-permute-start | bytes 294920 | tf_op jit(solution)/shard_map/ppermute | solution.py:277
  15.4 0.1 pad.9.clone
  15.5 2.1 %collective-permute-done.12 = bf16[128,384]{1,0:T(8,128)(2,1)S(1)} collective-permute-done((bf16[128,384]{1,0:T(8,128)(2,1)S(1)}, bf16[128,384]{1,0:T(8,128)(2,1)S(1)}, u32[]{:S(2)}, u32[]{:S(2)}) %collective-permute-start.12) | collective-permute-done | bytes 98336 | tf_op jit(solution)/shard_map/ppermute | solution.py:277
  17.5 4.4 %collective-permute-done.10 = bf16[128,384]{1,0:T(8,128)(2,1)S(1)} collective-permute-done((bf16[128,384]{1,0:T(8,128)(2,1)S(1)}, bf16[128,384]{1,0:T(8,128)(2,1)S(1)}, u32[]{:S(2)}, u32[]{:S(2)}) %collective-permute-start.10) | collective-permute-done | bytes 98336 | tf_op jit(solution)/shard_map/ppermute | solution.py:277
  21.9 2.4 %collective-permute-done.11 = bf16[128,384]{1,0:T(8,128)(2,1)S(1)} collective-permute-done((bf16[128,384]{1,0:T(8,128)(2,1)S(1)}, bf16[128,384]{1,0:T(8,128)(2,1)S(1)}, u32[]{:S(2)}, u32[]{:S(2)}) %collective-permute-start.11) | collective-permute-done | bytes 98336 | tf_op jit(solution)/shard_map/ppermute | solution.py:277
  24.4 1.6 %collective-permute-start.14 = (bf16[4,128,384]{2,1,0:T(8,128)(2,1)S(1)}, bf16[4,128,384]{2,1,0:T(8,128)(2,1)S(1)}, u32[]{:S(2)}, u32[]{:S(2)}) collective-permute-start(bf16[4,128,384]{2,1,0:T(8,128)(2,1)S(1)} %pad_maximum_fusion.refs_4_), channel_id=1, source_target_pairs={{0,16},{1,17},{2,18},{3,19},{4,20},{5,21},{6,22},{7,23},{8,24},{9,... | collective-permute-start | bytes 1179656 | tf_op jit(solution)/shard_map/ppermute | solution.py:274
  26.0 0.1 maximum_maximum_fusion.own_ref.refs_0_
  26.1 0.5 collective-permute-start
  26.6 1.5 %collective-permute-start.16 = (bf16[4,128,384]{2,1,0:T(8,128)(2,1)S(1)}, bf16[4,128,384]{2,1,0:T(8,128)(2,1)S(1)}, u32[]{:S(2)}, u32[]{:S(2)}) collective-permute-start(bf16[4,128,384]{2,1,0:T(8,128)(2,1)S(1)} %pad_maximum_fusion.refs_4_), channel_id=1, source_target_pairs={{0,1},{1,0},{2,3},{3,2},{4,5},{5,4},{6,7},{7,6},{8,9},{9,8},{10,11... | collective-permute-start | bytes 1179656 | tf_op jit(solution)/shard_map/ppermute | solution.py:274
  28.1 6.8 %collective-permute-done.near_ref.refs_2_ = f32[8,128]{1,0:T(8,128)S(1)} collective-permute-done((f32[8,128]{1,0:T(8,128)S(1)}, f32[8,128]{1,0:T(8,128)S(1)}, u32[]{:S(2)}, u32[]{:S(2)}) %collective-permute-start) | collective-permute-done | bytes 4128 | tf_op jit(solution)/shard_map/ppermute | solution.py:274
  34.9 2.4 %collective-permute-start.18 = (bf16[4,128,384]{2,1,0:T(8,128)(2,1)S(1)}, bf16[4,128,384]{2,1,0:T(8,128)(2,1)}, u32[]{:S(2)}, u32[]{:S(2)}) collective-permute-start(bf16[4,128,384]{2,1,0:T(8,128)(2,1)S(1)} %pad_maximum_fusion.refs_4_), channel_id=1, source_target_pairs={{0,17},{1,16},{2,19},{3,18},{4,21},{5,20},{6,23},{7,22},{8,25},{9,... | collective-permute-start | bytes 1179656 | tf_op jit(solution)/shard_map/ppermute | solution.py:274
  37.4 2.7 %spread_rows.1 = (bf16[4,128,384]{2,1,0:T(8,128)(2,1)S(1)}, bf16[4,128,384]{2,1,0:T(8,128)(2,1)S(1)}, bf16[4,128,384]{2,1,0:T(8,128)(2,1)S(1)}, bf16[4,128,384]{2,1,0:T(8,128)(2,1)}) custom-call(f32[8,128]{1,0:T(8,128)S(1)} %maximum_maximum_fusion.own_ref.refs_0_, f32[8,128]{1,0:T(8,128)S(1)} %collective-permute-done.near_ref.refs_2_, ...), custom_call_target="tpu_custom_call" | custom-call | flops 402653184 | bytes 9437184 | tf_op jit(solution)/shard_map/spread_rows/pallas_call | solution.py:143
  40.1 0.5 collective-permute-start.2
  40.6 0.5 collective-permute-start.3
  41.1 2.5 %collective-permute-start.4 = (bf16[4,128,384]{2,1,0:T(8,128)(2,1)}, bf16[4,128,384]{2,1,0:T(8,128)(2,1)S(1)}, u32[]{:S(2)}, u32[]{:S(2)}) collective-permute-start(bf16[4,128,384]{2,1,0:T(8,128)(2,1)} %get-tuple-element.20), channel_id=1, source_target_pairs={{0,17},{1,16},{2,19},{3,18},{4,21},{5,20},{6,23},{7,22},{8,25},{9,... | collective-permute-start | bytes 1179656 | tf_op jit(solution)/shard_map/ppermute | solution.py:274
  43.6 4.4 %collective-permute-done.18.refs_10_ = bf16[4,128,384]{2,1,0:T(8,128)(2,1)} collective-permute-done((bf16[4,128,384]{2,1,0:T(8,128)(2,1)S(1)}, bf16[4,128,384]{2,1,0:T(8,128)(2,1)}, u32[]{:S(2)}, u32[]{:S(2)}) %collective-permute-start.18) | collective-permute-done | bytes 393248 | tf_op jit(solution)/shard_map/ppermute | solution.py:274
  48.0 8.4 %collective-permute-done.2.b_ref = bf16[4,128,384]{2,1,0:T(8,128)(2,1)S(1)} collective-permute-done((bf16[4,128,384]{2,1,0:T(8,128)(2,1)S(1)}, bf16[4,128,384]{2,1,0:T(8,128)(2,1)S(1)}, u32[]{:S(2)}, u32[]{:S(2)}) %collective-permute-start.2) | collective-permute-done | bytes 393248 | tf_op jit(solution)/shard_map/ppermute | solution.py:274
  56.4 0.5 collective-permute-start.19
  56.9 7.5 %collective-permute-done.4.d_ref = bf16[4,128,384]{2,1,0:T(8,128)(2,1)S(1)} collective-permute-done((bf16[4,128,384]{2,1,0:T(8,128)(2,1)}, bf16[4,128,384]{2,1,0:T(8,128)(2,1)S(1)}, u32[]{:S(2)}, u32[]{:S(2)}) %collective-permute-start.4) | collective-permute-done | bytes 393248 | tf_op jit(solution)/shard_map/ppermute | solution.py:274
  64.4 0.1 pad_add_fusion.pos_ref
  64.5 0.2 plane_sum.1
  64.7 0.9 %collective-permute-done.9.refs_3_ = f32[8,128]{1,0:T(8,128)S(1)} collective-permute-done((f32[8,128]{1,0:T(8,128)S(1)}, f32[8,128]{1,0:T(8,128)S(1)}, u32[]{:S(2)}, u32[]{:S(2)}) %collective-permute-start.9) | collective-permute-done | bytes 4128 | tf_op jit(solution)/shard_map/ppermute | solution.py:274
  65.6 2.1 %collective-permute-start.6 = (bf16[128,384]{1,0:T(8,128)(2,1)S(1)}, bf16[128,384]{1,0:T(8,128)(2,1)S(1)}, u32[]{:S(2)}, u32[]{:S(2)}) collective-permute-start(bf16[128,384]{1,0:T(8,128)(2,1)S(1)} %get-tuple-element.23), channel_id=1, source_target_pairs={{0,4},{1,5},{2,6},{3,7},{4,0},{5,1},{6,2},{7,3},{8,12},{9,13},{10,... | collective-permute-start | bytes 294920 | tf_op jit(solution)/shard_map/ppermute | solution.py:277
  67.7 1.8 %collective-permute-start.7 = (bf16[128,384]{1,0:T(8,128)(2,1)S(1)}, bf16[128,384]{1,0:T(8,128)(2,1)S(1)}, u32[]{:S(2)}, u32[]{:S(2)}) collective-permute-start(bf16[128,384]{1,0:T(8,128)(2,1)S(1)} %get-tuple-element.24), channel_id=1, source_target_pairs={{0,6},{1,7},{2,0},{3,1},{4,2},{5,3},{6,4},{7,5},{8,14},{9,15},{10,... | collective-permute-start | bytes 294920 | tf_op jit(solution)/shard_map/ppermute | solution.py:277
  69.5 2.8 %copy-done.1 = bf16[1,1024,3072]{2,1,0:T(8,128)(2,1)S(1)} copy-done((bf16[1,1024,3072]{2,1,0:T(8,128)(2,1)S(1)}, bf16[1,1024,3072]{2,1,0:T(8,128)(2,1)}, u32[]{:S(2)}) %copy-start.1) | copy-done | bytes 6291480
  72.2 12.8 %backward_rows.1 = (bf16[1,256,1024]{2,1,0:T(8,128)(2,1)}, bf16[1,1024,3072]{2,1,0:T(8,128)(2,1)}) custom-call(s32[3]{0:T(128)S(1)} %pad_add_fusion.pos_ref, bf16[1,256,1024]{2,1,0:T(8,128)(2,1)S(1)} %copy-done.3, bf16[1,1024,3072]{2,1,0:T(8,128)(2,1)S(1)} %copy-done.1, f32[8,128]{1,0:T(8,128)S(1)} %maximum_maximum_fusion.own_ref.refs_0_, ...), custom_call_target="tpu_custom_call" | custom-call | flops 3221225472 | bytes 16777216 | tf_op jit(solution)/shard_map/backward_rows/pallas_call | solution.py:234
  85.1 0.7 add_convert_fusion
  (33 shorter events, 0.1 us)
Async XLA Ops:
  0.6 2.8 %copy-start = (bf16[1,1024,3072]{2,1,0:T(8,128)(2,1)S(1)}, bf16[1,1024,3072]{2,1,0:T(8,128)(2,1)}, u32[]{:S(2)}) copy-start(bf16[1,1024,3072]{2,1,0:T(8,128)(2,1)} %weight_ref.3) | copy-start | bytes 18874372
  3.4 1.0 %copy-start.2 = (bf16[1,256,1024]{2,1,0:T(8,128)(2,1)S(1)}, bf16[1,256,1024]{2,1,0:T(8,128)(2,1)}, u32[]{:S(2)}) copy-start(bf16[1,256,1024]{2,1,0:T(8,128)(2,1)} %hidden_ref.3) | copy-start | bytes 1572868
  4.5 5.2 %copy-start.4 = (bf16[128,384]{1,0:T(8,128)(2,1)S(1)}, bf16[128,384]{1,0:T(8,128)(2,1)}, u32[]{:S(2)}) copy-start(bf16[128,384]{1,0:T(8,128)(2,1)} %param.9) | copy-start | bytes 294916
  4.5 10.9 %copy-start.5 = (s32[128,2]{0,1:T(2,128)S(1)}, s32[128,2]{0,1:T(2,128)}, u32[]{:S(2)}) copy-start(s32[128,2]{0,1:T(2,128)} %param.7) | copy-start | bytes 3076
  4.5 21.5 %copy-start.6 = (f32[128,2]{0,1:T(2,128)S(1)}, f32[128,2]{0,1:T(2,128)}, u32[]{:S(2)}) copy-start(f32[128,2]{0,1:T(2,128)} %param.8) | copy-start | bytes 3076
  4.5 65.0 %copy-start.3 = (bf16[1,256,1024]{2,1,0:T(8,128)(2,1)S(1)}, bf16[1,256,1024]{2,1,0:T(8,128)(2,1)}, u32[]{:S(2)}) copy-start(bf16[1,256,1024]{2,1,0:T(8,128)(2,1)} %hidden_ref.3) | copy-start | bytes 1572868
  9.2 28.2 %collective-permute-start.1 = (bf16[8,2,64,384]{3,2,1,0:T(8,128)(2,1)S(1)}, bf16[8,2,64,384]{3,2,1,0:T(8,128)(2,1)S(1)}, u32[]{:S(2)}, u32[]{:S(2)}) collective-permute-start(bf16[8,2,64,384]{3,2,1,0:T(8,128)(2,1)S(1)} %get-tuple-element.16), channel_id=1, source_target_pairs={{0,8},{1,9},{2,10},{3,11},{4,12},{5,13},{6,14},{7,15},{8,0},{9,1},... | collective-permute-start | bytes 2359304 | tf_op jit(solution)/shard_map/ppermute | solution.py:274
  9.7 7.8 %collective-permute-start.12 = (bf16[128,384]{1,0:T(8,128)(2,1)S(1)}, bf16[128,384]{1,0:T(8,128)(2,1)S(1)}, u32[]{:S(2)}, u32[]{:S(2)}) collective-permute-start(bf16[128,384]{1,0:T(8,128)(2,1)S(1)} %copy-done.4), channel_id=1, source_target_pairs={{0,6},{1,7},{2,0},{3,1},{4,2},{5,3},{6,4},{7,5},{8,14},{9,15},{10,... | collective-permute-start | bytes 294920 | tf_op jit(solution)/shard_map/ppermute | solution.py:277
  14.4 7.5 %collective-permute-start.10 = (bf16[128,384]{1,0:T(8,128)(2,1)S(1)}, bf16[128,384]{1,0:T(8,128)(2,1)S(1)}, u32[]{:S(2)}, u32[]{:S(2)}) collective-permute-start(bf16[128,384]{1,0:T(8,128)(2,1)S(1)} %copy-done.4), channel_id=1, source_target_pairs={{0,2},{1,3},{2,4},{3,5},{4,6},{5,7},{6,0},{7,1},{8,10},{9,11},{10,... | collective-permute-start | bytes 294920 | tf_op jit(solution)/shard_map/ppermute | solution.py:277
  14.4 10.0 %collective-permute-start.11 = (bf16[128,384]{1,0:T(8,128)(2,1)S(1)}, bf16[128,384]{1,0:T(8,128)(2,1)S(1)}, u32[]{:S(2)}, u32[]{:S(2)}) collective-permute-start(bf16[128,384]{1,0:T(8,128)(2,1)S(1)} %copy-done.4), channel_id=1, source_target_pairs={{0,4},{1,5},{2,6},{3,7},{4,0},{5,1},{6,2},{7,3},{8,12},{9,13},{10,... | collective-permute-start | bytes 294920 | tf_op jit(solution)/shard_map/ppermute | solution.py:277
  24.4 16.7 %collective-permute-start.14 = (bf16[4,128,384]{2,1,0:T(8,128)(2,1)S(1)}, bf16[4,128,384]{2,1,0:T(8,128)(2,1)S(1)}, u32[]{:S(2)}, u32[]{:S(2)}) collective-permute-start(bf16[4,128,384]{2,1,0:T(8,128)(2,1)S(1)} %pad_maximum_fusion.refs_4_), channel_id=1, source_target_pairs={{0,16},{1,17},{2,18},{3,19},{4,20},{5,21},{6,22},{7,23},{8,24},{9,... | collective-permute-start | bytes 1179656 | tf_op jit(solution)/shard_map/ppermute | solution.py:274
  26.1 8.8 %collective-permute-start = (f32[8,128]{1,0:T(8,128)S(1)}, f32[8,128]{1,0:T(8,128)S(1)}, u32[]{:S(2)}, u32[]{:S(2)}) collective-permute-start(f32[8,128]{1,0:T(8,128)S(1)} %maximum_maximum_fusion.own_ref.refs_0_), channel_id=1, source_target_pairs={{0,16},{1,17},{2,18},{3,19},{4,20},{5,21},{6,22},{7,23},{8,24},{9,... | collective-permute-start | bytes 12296 | tf_op jit(solution)/shard_map/ppermute | solution.py:274
  26.6 14.0 %collective-permute-start.8 = (f32[8,128]{1,0:T(8,128)S(1)}, f32[8,128]{1,0:T(8,128)S(1)}, u32[]{:S(2)}, u32[]{:S(2)}) collective-permute-start(f32[8,128]{1,0:T(8,128)S(1)} %maximum_maximum_fusion.own_ref.refs_0_), channel_id=1, source_target_pairs={{0,8},{1,9},{2,10},{3,11},{4,12},{5,13},{6,14},{7,15},{8,0},{9,1},... | collective-permute-start | bytes 12296 | tf_op jit(solution)/shard_map/ppermute | solution.py:274
  26.6 17.0 %collective-permute-start.16 = (bf16[4,128,384]{2,1,0:T(8,128)(2,1)S(1)}, bf16[4,128,384]{2,1,0:T(8,128)(2,1)S(1)}, u32[]{:S(2)}, u32[]{:S(2)}) collective-permute-start(bf16[4,128,384]{2,1,0:T(8,128)(2,1)S(1)} %pad_maximum_fusion.refs_4_), channel_id=1, source_target_pairs={{0,1},{1,0},{2,3},{3,2},{4,5},{5,4},{6,7},{7,6},{8,9},{9,8},{10,11... | collective-permute-start | bytes 1179656 | tf_op jit(solution)/shard_map/ppermute | solution.py:274
  34.9 13.1 %collective-permute-start.18 = (bf16[4,128,384]{2,1,0:T(8,128)(2,1)S(1)}, bf16[4,128,384]{2,1,0:T(8,128)(2,1)}, u32[]{:S(2)}, u32[]{:S(2)}) collective-permute-start(bf16[4,128,384]{2,1,0:T(8,128)(2,1)S(1)} %pad_maximum_fusion.refs_4_), channel_id=1, source_target_pairs={{0,17},{1,16},{2,19},{3,18},{4,21},{5,20},{6,23},{7,22},{8,25},{9,... | collective-permute-start | bytes 1179656 | tf_op jit(solution)/shard_map/ppermute | solution.py:274
  40.1 16.3 %collective-permute-start.2 = (bf16[4,128,384]{2,1,0:T(8,128)(2,1)S(1)}, bf16[4,128,384]{2,1,0:T(8,128)(2,1)S(1)}, u32[]{:S(2)}, u32[]{:S(2)}) collective-permute-start(bf16[4,128,384]{2,1,0:T(8,128)(2,1)S(1)} %get-tuple-element.18), channel_id=1, source_target_pairs={{0,1},{1,0},{2,3},{3,2},{4,5},{5,4},{6,7},{7,6},{8,9},{9,8},{10,11... | collective-permute-start | bytes 1179656 | tf_op jit(solution)/shard_map/ppermute | solution.py:274
  40.6 15.8 %collective-permute-start.3 = (bf16[4,128,384]{2,1,0:T(8,128)(2,1)S(1)}, bf16[4,128,384]{2,1,0:T(8,128)(2,1)S(1)}, u32[]{:S(2)}, u32[]{:S(2)}) collective-permute-start(bf16[4,128,384]{2,1,0:T(8,128)(2,1)S(1)} %get-tuple-element.19), channel_id=1, source_target_pairs={{0,16},{1,17},{2,18},{3,19},{4,20},{5,21},{6,22},{7,23},{8,24},{9,... | collective-permute-start | bytes 1179656 | tf_op jit(solution)/shard_map/ppermute | solution.py:274
  41.1 23.3 %collective-permute-start.4 = (bf16[4,128,384]{2,1,0:T(8,128)(2,1)}, bf16[4,128,384]{2,1,0:T(8,128)(2,1)S(1)}, u32[]{:S(2)}, u32[]{:S(2)}) collective-permute-start(bf16[4,128,384]{2,1,0:T(8,128)(2,1)} %get-tuple-element.20), channel_id=1, source_target_pairs={{0,17},{1,16},{2,19},{3,18},{4,21},{5,20},{6,23},{7,22},{8,25},{9,... | collective-permute-start | bytes 1179656 | tf_op jit(solution)/shard_map/ppermute | solution.py:274
  43.6 22.0 %collective-permute-start.13 = (bf16[4,128,384]{2,1,0:T(8,128)(2,1)S(1)}, bf16[4,128,384]{2,1,0:T(8,128)(2,1)}, u32[]{:S(2)}, u32[]{:S(2)}) collective-permute-start(bf16[4,128,384]{2,1,0:T(8,128)(2,1)S(1)} %pad_maximum_fusion.refs_4_), channel_id=1, source_target_pairs={{0,8},{1,9},{2,10},{3,11},{4,12},{5,13},{6,14},{7,15},{8,0},{9,1},... | collective-permute-start | bytes 1179656 | tf_op jit(solution)/shard_map/ppermute | solution.py:274
  48.0 19.7 %collective-permute-start.15 = (bf16[4,128,384]{2,1,0:T(8,128)(2,1)S(1)}, bf16[4,128,384]{2,1,0:T(8,128)(2,1)}, u32[]{:S(2)}, u32[]{:S(2)}) collective-permute-start(bf16[4,128,384]{2,1,0:T(8,128)(2,1)S(1)} %collective-permute-done.14.refs_6_), channel_id=1, source_target_pairs={{0,8},{1,9},{2,10},{3,11},{4,12},{5,13},{6,14},{7,15},{8,0},{9,1},... | collective-permute-start | bytes 1179656 | tf_op jit(solution)/shard_map/ppermute | solution.py:274
  56.4 13.1 %collective-permute-start.17 = (bf16[4,128,384]{2,1,0:T(8,128)(2,1)S(1)}, bf16[4,128,384]{2,1,0:T(8,128)(2,1)}, u32[]{:S(2)}, u32[]{:S(2)}) collective-permute-start(bf16[4,128,384]{2,1,0:T(8,128)(2,1)S(1)} %collective-permute-done.16.refs_8_), channel_id=1, source_target_pairs={{0,8},{1,9},{2,10},{3,11},{4,12},{5,13},{6,14},{7,15},{8,0},{9,1},... | collective-permute-start | bytes 1179656 | tf_op jit(solution)/shard_map/ppermute | solution.py:274
  56.4 13.1 %collective-permute-start.19 = (bf16[4,128,384]{2,1,0:T(8,128)(2,1)}, bf16[4,128,384]{2,1,0:T(8,128)(2,1)}, u32[]{:S(2)}, u32[]{:S(2)}) collective-permute-start(bf16[4,128,384]{2,1,0:T(8,128)(2,1)} %collective-permute-done.18.refs_10_), channel_id=1, source_target_pairs={{0,8},{1,9},{2,10},{3,11},{4,12},{5,13},{6,14},{7,15},{8,0},{9,1},... | collective-permute-start | bytes 1179656 | tf_op jit(solution)/shard_map/ppermute | solution.py:274
  64.4 1.2 %collective-permute-start.9 = (f32[8,128]{1,0:T(8,128)S(1)}, f32[8,128]{1,0:T(8,128)S(1)}, u32[]{:S(2)}, u32[]{:S(2)}) collective-permute-start(f32[8,128]{1,0:T(8,128)S(1)} %collective-permute-done.near_ref.refs_2_), channel_id=1, source_target_pairs={{0,8},{1,9},{2,10},{3,11},{4,12},{5,13},{6,14},{7,15},{8,0},{9,1},... | collective-permute-start | bytes 12296 | tf_op jit(solution)/shard_map/ppermute | solution.py:274
  65.6 19.5 %collective-permute-start.5 = (bf16[128,384]{1,0:T(8,128)(2,1)S(1)}, bf16[128,384]{1,0:T(8,128)(2,1)S(1)}, u32[]{:S(2)}, u32[]{:S(2)}) collective-permute-start(bf16[128,384]{1,0:T(8,128)(2,1)S(1)} %get-tuple-element.22), channel_id=1, source_target_pairs={{0,2},{1,3},{2,4},{3,5},{4,6},{5,7},{6,0},{7,1},{8,10},{9,11},{10,... | collective-permute-start | bytes 294920 | tf_op jit(solution)/shard_map/ppermute | solution.py:277
  65.6 19.5 %collective-permute-start.6 = (bf16[128,384]{1,0:T(8,128)(2,1)S(1)}, bf16[128,384]{1,0:T(8,128)(2,1)S(1)}, u32[]{:S(2)}, u32[]{:S(2)}) collective-permute-start(bf16[128,384]{1,0:T(8,128)(2,1)S(1)} %get-tuple-element.23), channel_id=1, source_target_pairs={{0,4},{1,5},{2,6},{3,7},{4,0},{5,1},{6,2},{7,3},{8,12},{9,13},{10,... | collective-permute-start | bytes 294920 | tf_op jit(solution)/shard_map/ppermute | solution.py:277
  67.7 17.4 %collective-permute-start.7 = (bf16[128,384]{1,0:T(8,128)(2,1)S(1)}, bf16[128,384]{1,0:T(8,128)(2,1)S(1)}, u32[]{:S(2)}, u32[]{:S(2)}) collective-permute-start(bf16[128,384]{1,0:T(8,128)(2,1)S(1)} %get-tuple-element.24), channel_id=1, source_target_pairs={{0,6},{1,7},{2,0},{3,1},{4,2},{5,3},{6,4},{7,5},{8,14},{9,15},{10,... | collective-permute-start | bytes 294920 | tf_op jit(solution)/shard_map/ppermute | solution.py:277
  69.5 2.8 %copy-start.1 = (bf16[1,1024,3072]{2,1,0:T(8,128)(2,1)S(1)}, bf16[1,1024,3072]{2,1,0:T(8,128)(2,1)}, u32[]{:S(2)}) copy-start(bf16[1,1024,3072]{2,1,0:T(8,128)(2,1)} %weight_ref.3) | copy-start | bytes 18874372

commit v2 on v0

v2 whole, which is shorter than its diff:
```python
import functools

import jax
import jax.numpy as jnp
from jax import lax
from jax.experimental import pallas as pl
from jax.experimental.pallas import tpu as pltpu
from jax.sharding import PartitionSpec as P

BF, F32 = jnp.bfloat16, jnp.float32


def routed(hidden, down_weight, expert_ids, combine, out_grad):
    dp_count = lax.axis_size("dp")
    tok_rows = expert_ids.shape[0]
    capacity = 2 * tok_rows // dp_count
    slot_count = dp_count * capacity
    feat_share = out_grad.shape[1]
    width = down_weight.shape[2]
    flat_ids = expert_ids.reshape(-1)
    labels = jnp.arange(dp_count, dtype=jnp.int32)
    onehot = (flat_ids[:, None] == labels[None, :]).astype(jnp.int32)
    pair_rank = jnp.sum((jnp.cumsum(onehot, axis=0) - 1) * onehot, axis=1)
    inside = flat_ids < dp_count
    target = jnp.where(inside, flat_ids * capacity + pair_rank, dp_count * capacity)
    weights = combine.reshape(-1)
    full_grad = lax.all_gather(out_grad, "cuts", axis=1, tiled=True)
    scaled = (weights[:, None] * jnp.repeat(full_grad, 2, axis=0).astype(F32)).astype(BF)
    outgoing = jnp.zeros((dp_count * capacity, width), BF).at[target].set(scaled, mode="drop")
    incoming = lax.all_to_all(
        outgoing.reshape(dp_count, capacity, width), "dp", split_axis=0, concat_axis=0, tiled=True
    )
    grad_rows = incoming.reshape(slot_count, width)
    hidden_rows = hidden[0]
    weight = down_weight[0]
    own_share = lax.psum_scatter(
        lax.dot_general(weight, hidden_rows, (((0,), (1,)), ((), ())), preferred_element_type=F32),
        "cuts",
        scatter_dimension=0,
        tiled=True,
    )
    hid_grad = lax.dot_general(
        grad_rows, weight, (((1,), (1,)), ((), ())), preferred_element_type=F32
    ).astype(BF)
    down_grad = lax.dot_general(
        hidden_rows, grad_rows, (((0,), (0,)), ((), ())), preferred_element_type=F32
    ).astype(BF)
    returned = lax.all_to_all(
        own_share.astype(BF), "dp", split_axis=1, concat_axis=1, tiled=True
    )
    pick_index = jnp.minimum(target, dp_count * capacity - 1)
    picked = jnp.take(returned, pick_index, axis=1).astype(F32)
    pair_coef = jnp.where(inside, weights, jnp.zeros_like(weights))
    summed = jnp.sum((picked * pair_coef[None, :]).reshape(feat_share, tok_rows, 2), axis=2)
    mixed = summed.T.astype(BF)
    return (mixed, hid_grad[None], down_grad[None])


def routing(meta, expert, capacity):
    tok = meta.shape[1]
    label = jnp.full((1, tok), expert).astype(F32)
    first, second = meta[0:1] == label, meta[1:2] == label
    named = jnp.where(first, 1.0, jnp.where(second, 1.0, 0.0))
    weight = jnp.where(first, meta[2:3], jnp.where(second, meta[3:4], 0.0))
    earlier = lax.broadcasted_iota(jnp.int32, (tok, tok), 0) < lax.broadcasted_iota(
        jnp.int32, (tok, tok), 1
    )
    rank = jnp.dot(
        jnp.broadcast_to(named, (8, tok)).astype(BF),
        jnp.where(earlier, 1.0, 0.0).astype(BF),
        preferred_element_type=F32,
    )[0:1]
    slot = lax.broadcasted_iota(jnp.int32, (capacity, tok), 0).astype(F32)
    hot = jnp.where(slot == rank, named, 0.0)
    return hot, weight


def forward_kernel(nz, capacity, ids_ref, coef_ref, hidden_ref, weight_ref, keep_ref, send_ref, meta_ref, *scratch):
    ids, held, wide, rows_ref, sems = scratch
    me = lax.axis_index("dp")
    feat = keep_ref.shape[-1]
    copies = [pltpu.make_async_copy(hidden_ref.at[0], held, sems.at[nz])]
    for z in range(nz):
        part = weight_ref.at[0, :, pl.ds(2 * z * feat, 2 * feat)]
        copies.append(pltpu.make_async_copy(part, wide.at[z], sems.at[z]))
    small = pltpu.make_async_copy(ids_ref, ids, sems.at[nz + 1])
    small.start()
    coefs = pltpu.make_async_copy(coef_ref, meta_ref.at[2:4], sems.at[nz + 2])
    coefs.start()
    for copy in copies:
        copy.start()
    small.wait()
    meta_ref[0:2] = ids[...].astype(F32)
    coefs.wait()
    copies[0].wait()
    for z in range(nz):
        copies[z + 1].wait()
        rows_ref[...] = jnp.dot(held[...], wide[z], preferred_element_type=F32).astype(BF)
        for dy in range(2):
            for dc, out in ((0, keep_ref), (1, send_ref)):
                source = me ^ (2 * dy + dc)
                at = pl.multiple_of(source * capacity, capacity)
                for x in range(2):
                    out[z, x, dy] = rows_ref[pl.ds(at, capacity), x * feat : (x + 1) * feat]


def forward(ids, coefs, hidden, weight, feat, dp_count):
    _, slots, ff = hidden.shape
    width = weight.shape[2]
    nz, capacity = width // (2 * feat), slots // dp_count
    part = jax.ShapeDtypeStruct((nz, 2, 2, capacity, feat), BF)
    hbm, vmem = pl.BlockSpec(memory_space=pltpu.HBM), pl.BlockSpec(memory_space=pltpu.VMEM)
    return pl.pallas_call(
        functools.partial(forward_kernel, nz, capacity),
        in_specs=[hbm] * 4,
        out_specs=[vmem] * 3,
        out_shape=[part, part, jax.ShapeDtypeStruct((4, ids.shape[1]), F32)],
        scratch_shapes=[
            pltpu.VMEM(ids.shape, jnp.int32),
            pltpu.VMEM((slots, ff), BF),
            pltpu.VMEM((nz, ff, 2 * feat), BF),
            pltpu.VMEM((slots, 2 * feat), BF),
            pltpu.SemaphoreType.DMA((nz + 3,)),
        ],
        compiler_params=pltpu.CompilerParams(vmem_limit_bytes=58 << 20),
        cost_estimate=pl.CostEstimate(
            flops=2 * slots * ff * width, bytes_accessed=2 * (ff * width + slots * (ff + width)), transcendentals=0
        ),
        name="forward_rows",
    )(ids, coefs, hidden, weight)


def spread_kernel(nz, capacity, own_ref, near_ref, keep_ref, got_ref, *refs):
    (to_x, by_x, to_y, by_y), hots, cols = refs[:4], refs[4], refs[5]
    step, me, x = pl.program_id(0), lax.axis_index("dp"), lax.axis_index("cuts") % 2

    @pl.when(step == 0)
    def _():
        for dy, meta_ref in enumerate((own_ref, near_ref)):
            for dc in range(2):
                hot, weight = routing(meta_ref[...], me ^ dc, capacity)
                tok = hot.shape[1]
                hots[dy, dc] = hot.astype(BF)
                cols[dy, dc] = jnp.broadcast_to(weight, (tok, tok)).T

    def block(dy, dx):
        total = None
        for dc, rows in ((0, keep_ref), (1, got_ref)):
            picked = lax.dot_general(
                hots[dy, dc], rows[0, x ^ dx, dy], (((0,), (0,)), ((), ())), preferred_element_type=F32
            )
            term = picked * cols[dy, dc][:, 0:1]
            total = term if total is None else total + term
        return total

    @pl.when(step < nz // 2)
    def _():
        for dy in range(2):
            to_x[dy, 0] = block(dy, 1).astype(BF)
            by_x[dy, 0] = block(dy, 0)

    @pl.when(step >= nz // 2)
    def _():
        for dx in range(2):
            to_y[dx, 0] = block(1, dx).astype(BF)
            by_y[dx, 0] = block(0, dx)


def spread(own, near, keep, got):
    nz, _, _, capacity, feat = keep.shape
    tok, half = own.shape[1], nz // 2
    rows = pl.BlockSpec((1, 2, 2, capacity, feat), lambda k: (k, 0, 0, 0, 0))
    meta = pl.BlockSpec((4, tok), lambda k: (0, 0))
    first = pl.BlockSpec((2, 1, tok, feat), lambda k: (0, jnp.minimum(k, half - 1), 0, 0))
    second = pl.BlockSpec((2, 1, tok, feat), lambda k: (0, jnp.maximum(k - half, 0), 0, 0))
    shape = (2, half, tok, feat)
    return pl.pallas_call(
        functools.partial(spread_kernel, nz, capacity),
        grid=(nz,),
        in_specs=[meta, meta, rows, rows],
        out_specs=[first, first, second, second],
        out_shape=[jax.ShapeDtypeStruct(shape, t) for t in (BF, F32, BF, F32)],
        scratch_shapes=[pltpu.VMEM((2, 2, capacity, tok), BF), pltpu.VMEM((2, 2, tok, tok), F32)],
        compiler_params=pltpu.CompilerParams(vmem_limit_bytes=16 << 20),
        cost_estimate=pl.CostEstimate(
            flops=32 * tok * capacity * nz * feat, bytes_accessed=48 * tok * nz * feat, transcendentals=0
        ),
        name="spread_rows",
    )(own, near, keep, got)


def first_sum_kernel(kept_ref, got_ref, keep_out, send_out):
    keep_out[...] = kept_ref[0] + got_ref[0].astype(F32)
    send_out[...] = (kept_ref[1] + got_ref[1].astype(F32)).astype(BF)


def first_sum(kept, got):
    shape = kept.shape[1:]
    return pl.pallas_call(
        first_sum_kernel,
        out_shape=[jax.ShapeDtypeStruct(shape, F32), jax.ShapeDtypeStruct(shape, BF)],
        compiler_params=pltpu.CompilerParams(vmem_limit_bytes=16 << 20),
        name="first_sum",
    )(kept, got)


def second_sum_kernel(nz, a_ref, a_got, b_ref, b_got, *refs):
    outs, total = refs[:nz], refs[nz]
    z, half = lax.axis_index("cuts") // 2, nz // 2
    total[:half] = a_ref[...] + a_got[...].astype(F32)
    total[half:] = b_ref[...] + b_got[...].astype(F32)
    for k in range(nz):
        outs[k][...] = total[lax.rem(z + k, nz)].astype(outs[k].dtype)


def second_sum(a, a_got, b, b_got):
    half, tok, feat = a.shape
    nz = 2 * half
    return pl.pallas_call(
        functools.partial(second_sum_kernel, nz),
        out_shape=[jax.ShapeDtypeStruct((tok, feat), F32 if k == 0 else BF) for k in range(nz)],
        scratch_shapes=[pltpu.VMEM((nz, tok, feat), F32)],
        compiler_params=pltpu.CompilerParams(vmem_limit_bytes=16 << 20),
        name="second_sum",
    )(a, a_got, b, b_got)


def stack_kernel(_, *refs):
    for k, ref in enumerate(refs[:-1]):
        refs[-1][k] = ref[...]


def stack(parts, after):
    vmem = pl.BlockSpec(memory_space=pltpu.VMEM)
    return pl.pallas_call(
        stack_kernel,
        in_specs=[pl.BlockSpec(memory_space=pl.ANY)] + [vmem] * len(parts),
        out_specs=vmem,
        out_shape=jax.ShapeDtypeStruct((len(parts), *parts[0].shape), parts[0].dtype),
        compiler_params=pltpu.CompilerParams(vmem_limit_bytes=16 << 20),
        name="stack_blocks",
    )(after, *parts)


def backward_kernel(nz, capacity, *refs):
    hidden_ref, weight_ref = refs[:2]
    metas, grads, (hid_out, down_out, mark) = refs[2:6], refs[6:16], refs[16:19]
    made, rows_ref, turned, total, done, hots, cols, sems = refs[19:]
    me, x, z = lax.axis_index("dp"), lax.axis_index("cuts") % 2, lax.axis_index("cuts") // 2
    feat, half = grads[0].shape[-1], nz // 2

    for q in range(4):
        hot, weight = routing(metas[q][...], me, capacity)
        hots[q] = hot.astype(BF)
        cols[q] = jnp.broadcast_to(jnp.sum(hot * weight, axis=1, keepdims=True), cols.shape[1:])
    turned[...] = hidden_ref[0].T

    def put(dx, q, rows):
        lane = pl.multiple_of((x ^ dx) * feat, feat)
        at = pl.multiple_of((me ^ q) * capacity, capacity)
        picked = jnp.dot(hots[q], rows, preferred_element_type=F32)
        rows_ref[pl.ds(at, capacity), pl.ds(lane, feat)] = (picked * cols[q][:, 0:1]).astype(BF)

    leaving = []
    for k in range(nz):
        for dc in range(2):
            own, by_x, by_y, low, high = grads[5 * dc : 5 * dc + 5]
            put(0, dc, own[k])
            put(1, dc, by_x[k])
            put(0, 2 + dc, by_y[k])
            put(1, 2 + dc, low[k] if k < half else high[k - half])
        rows = rows_ref[...]
        column = pl.ds(pl.multiple_of(lax.rem(z - k + nz, nz) * 2 * feat, 2 * feat), 2 * feat)
        part = lax.dot_general(rows, weight_ref[0, :, column], (((1,), (1,)), ((), ())), preferred_element_type=F32)
        total[...] = part if k == 0 else total[...] + part
        if k == nz - 1:
            done[...] = total[...].astype(BF)
            last = pltpu.make_async_copy(done, hid_out.at[0], sems.at[2])
            last.start()
        if k >= 2:
            leaving[k - 2].wait()
        made[k % 2] = jnp.dot(turned[...], rows, preferred_element_type=F32).astype(BF)
        leaving.append(pltpu.make_async_copy(made.at[k % 2], down_out.at[0, :, column], sems.at[k % 2]))
        leaving[k].start()
    for copy in leaving[-2:]:
        copy.wait()
    last.wait()
    mark[...] = jnp.zeros_like(mark)


def backward(hidden, weight, metas, grads):
    nz, tok, feat = grads[0].shape
    _, slots, ff = hidden.shape
    width = weight.shape[2]
    capacity = slots // 4
    anywhere, vmem = pl.BlockSpec(memory_space=pl.ANY), pl.BlockSpec(memory_space=pltpu.VMEM)
    return pl.pallas_call(
        functools.partial(backward_kernel, nz, capacity),
        in_specs=[vmem] * 16,
        out_specs=[anywhere, anywhere, vmem],
        scratch_shapes=[
            pltpu.VMEM((2, ff, 2 * feat), BF),
            pltpu.VMEM((slots, 2 * feat), BF),
            pltpu.VMEM((ff, slots), BF),
            pltpu.VMEM((slots, ff), F32),
            pltpu.VMEM((slots, ff), BF),
            pltpu.VMEM((4, capacity, tok), BF),
            pltpu.VMEM((4, capacity, 128), F32),
            pltpu.SemaphoreType.DMA((3,)),
        ],
        out_shape=[
            jax.ShapeDtypeStruct(hidden.shape, BF),
            jax.ShapeDtypeStruct(weight.shape, BF),
            jax.ShapeDtypeStruct((8, 128), F32),
        ],
        compiler_params=pltpu.CompilerParams(vmem_limit_bytes=32 << 20),
        cost_estimate=pl.CostEstimate(
            flops=4 * slots * ff * width,
            bytes_accessed=4 * ff * width + 4 * slots * ff + 8 * tok * width,
            transcendentals=0,
        ),
        name="backward_rows",
    )(hidden, weight, *metas, *grads)


def last_sum_kernel(_, first_ref, *refs):
    total = first_ref[...]
    for ref in refs[:-1]:
        total = total + ref[...].astype(F32)
    refs[-1][...] = total.astype(BF)


def last_sum(parts, after):
    vmem = pl.BlockSpec(memory_space=pltpu.VMEM)
    return pl.pallas_call(
        last_sum_kernel,
        in_specs=[pl.BlockSpec(memory_space=pl.ANY)] + [vmem] * len(parts),
        out_specs=vmem,
        out_shape=jax.ShapeDtypeStruct(parts[0].shape, BF),
        compiler_params=pltpu.CompilerParams(vmem_limit_bytes=16 << 20),
        name="last_sum",
    )(after, *parts)


def shared(hidden, down_weight, expert_ids, combine, out_grad):
    dp_count, cut_count = lax.axis_size("dp"), lax.axis_size("cuts")
    nz = cut_count // 2
    tok, feat = out_grad.shape

    def send(value, dp_flip, cut_flip):
        pairs = [
            (d * cut_count + c, (d ^ dp_flip) * cut_count + (c ^ cut_flip))
            for d in range(dp_count)
            for c in range(cut_count)
        ]
        return lax.ppermute(value, ("dp", "cuts"), pairs)

    def along(value, k):
        return lax.ppermute(value, "cuts", [(c, (c + 2 * k) % cut_count) for c in range(cut_count)])

    half = nz // 2
    keep, away, own = forward(expert_ids.T, combine.T, hidden, down_weight, feat, dp_count)
    near = send(own, 2, 0)
    got = send(away, 1, 0)
    to_x, by_x, to_y, by_y = spread(own, near, keep, got)
    mine, _ = lax.optimization_barrier((out_grad, by_x))
    blocks = [mine] + [along(mine, k) for k in range(1, nz)]
    a, a_send = first_sum(by_x, send(to_x, 0, 1))
    b, b_send = first_sum(by_y, send(to_y, 2, 0))
    terms = second_sum(a, send(a_send, 2, 0), b, send(b_send, 0, 1))
    blocks = stack(blocks, a)
    from_x, from_y = send(blocks, 0, 1), send(blocks, 2, 0)
    parts = [blocks, from_x, from_y, send(from_x[:half], 2, 0), send(from_y[half:], 0, 1)]
    grads = parts + [send(p, 1, 0) for p in parts]
    metas = (own, send(own, 1, 0), near, send(near, 1, 0))
    hid_grad, down_grad, mark = backward(hidden, down_weight, metas, grads)
    mixed = last_sum([terms[0]] + [along(terms[k], k) for k in range(1, nz)], mark)
    return (mixed, hid_grad, down_grad)


def local(hidden, down_weight, expert_ids, combine, out_grad):
    dp_count, cut_count = lax.axis_size("dp"), lax.axis_size("cuts")
    few = dp_count == 4 and cut_count % 4 == 0 and dp_count * expert_ids.shape[0] <= 2 * hidden.shape[1]
    return (shared if few else routed)(hidden, down_weight, expert_ids, combine, out_grad)


def solution(mesh):
    return jax.shard_map(
        local,
        mesh=mesh,
        in_specs=(
            P("dp", None, "cuts"),
            P("dp", "cuts", None),
            P("dp", None),
            P("dp", None),
            P("dp", "cuts"),
        ),
        out_specs=(P("dp", "cuts"), P("dp", None, "cuts"), P("dp", "cuts", None)),
        check_vma=False,
    )
```

time: 129 us -> 63.6 us (0.49)
  blocking collectives: 37.5 us -> 0 us
  local copies, waits for them, and re-layouts: 22 us -> 1.87 us
  matrix products: 16.3 us -> 0 us
  Pallas kernels: 0 us -> 15.3 us
  starting transfers between devices: 7.15 us -> 21.8 us
  between operations: 14.1 us -> 0.81 us
  other arithmetic: 9.16 us -> 0 us
  waiting for transfers between devices: 21.8 us -> 23.6 us
    all_gather x1 -> x0, blocking collectives: 37.5 us -> none  [local(): full_grad = lax.all_gather(out_grad, 'cuts', axis=1, tiled=True)]
    ppermute x0 -> x23, waiting for transfers between devices: none -> 23.6 us  [the longest x17 18.9 us: send(): return lax.ppermute(value, ('dp', 'cuts'), pairs)]
    ppermute x0 -> x23, starting transfers between devices: none -> 21.8 us  [the longest x17 12.6 us: send(): return lax.ppermute(value, ('dp', 'cuts'), pairs)]
    all_to_all x2 -> x0, waiting for transfers between devices: 19.5 us -> none  [the longest x1 19.5 us: local(): lax.all_to_all(outgoing.reshape(dp_count, capacity, width), 'dp', split_a...]
    dot_general x3 -> x0, matrix products: 16.3 us -> none  [the longest x1 6.32 us: local(): lax.dot_general(weight, hidden_rows, (((0,), (1,)), ((), ())), preferred_...]
    pallas_call x0 -> x8, Pallas kernels: none -> 15.3 us  [the longest x1 6.25 us: backward(): pl.pallas_call(functools.partial(backward_kernel, nz, capacity), in_specs...]
    unnamed x11 -> x12, local copies, waits for them, and re-layouts: 10.5 us -> 1.83 us
    all_to_all x2 -> x0, starting transfers between devices: 7.11 us -> none  [the longest x1 3.57 us: local(): lax.all_to_all(outgoing.reshape(dp_count, capacity, width), 'dp', split_a...]
  transfers between devices with their start and end apart: 3 -> 23, of which waited for: 2 -> 8; matrix products, arithmetic and copies ran while one was open for 27% -> 0% of each run, Pallas kernels for 0% -> 10%
where the time goes in v2:
time: 63.6 us; the launch traced here: 63.4 us
  waiting for transfers between devices  23.6 us (37%)
  starting transfers between devices  21.8 us (34%)
  Pallas kernels  15.3 us (24%)
  local copies, waits for them, and re-layouts  1.87 us (3%)
  between operations  0.81 us (1%)
    ppermute x17, waiting for transfers between devices, send(): return lax.ppermute(value, ('dp', 'cuts'), pairs)  18.9 us
    ppermute x17, starting transfers between devices, send(): return lax.ppermute(value, ('dp', 'cuts'), pairs)  12.6 us
    ppermute x6, starting transfers between devices, along(): lax.ppermute(value, 'cuts', [(c, (c + 2 * k) % cut_count) for c in range(...  9.17 us
    pallas_call x1, Pallas kernels, backward(): pl.pallas_call(functools.partial(backward_kernel, nz, capacity), in_specs...  6.25 us
    pallas_call x1, Pallas kernels, forward(): pl.pallas_call(functools.partial(forward_kernel, nz, capacity), in_specs=...  5.81 us
    ppermute x6, waiting for transfers between devices, along(): lax.ppermute(value, 'cuts', [(c, (c + 2 * k) % cut_count) for c in range(...  4.61 us
    pallas_call x1, Pallas kernels, spread(): pl.pallas_call(functools.partial(spread_kernel, nz, capacity), grid=(nz,)...  2.22 us
    unnamed x12, local copies, waits for them, and re-layouts  1.83 us
  transfers between devices with their start and end apart: 23, of which 8 were waited for; matrix products, arithmetic and copies ran while one was open for 0% of the time, Pallas kernels for 10%

profile of v2, /device:TPU:0, one launch (start us, length us, event | category | flops | bytes accessed | tf_op | source)
XLA Modules:
  0.0 63.4 jit_solution(457339399605145455)
XLA Ops:
  0.7 5.8 %forward_rows.1 = (bf16[4,2,2,64,384]{4,3,2,1,0:T(8,128)(2,1)}, bf16[4,2,2,64,384]{4,3,2,1,0:T(8,128)(2,1)}, f32[4,128]{1,0:T(4,128)}) custom-call(s32[2,128]{1,0:T(2,128)} %bitcast.2, f32[2,128]{1,0:T(2,128)} %bitcast.3, bf16[1,256,1024]{2,1,0:T(8,128)(2,1)} %refs_0_.2, bf16[1,1024,3072]{2,1,0:T(8,128)(2,1)} %refs_1_.1), custom_call_target="tpu_custom_call" | custom-call | flops 1610612736 | bytes 8388608 | tf_op jit(solution)/shard_map/forward_rows/pallas_call | solution.py:113
  6.5 0.5 collective-permute-start.3
  7.0 2.6 %collective-permute-start.1 = (f32[4,128]{1,0:T(4,128)}, f32[4,128]{1,0:T(4,128)S(1)}, u32[]{:S(2)}, u32[]{:S(2)}) collective-permute-start(f32[4,128]{1,0:T(4,128)} %get-tuple-element.22.own_ref.refs_2_), channel_id=1, source_target_pairs={{0,16},{1,17},{2,18},{3,19},{4,20},{5,21},{6,22},{7,23},{8,24},{9,... | collective-permute-start | bytes 6152 | tf_op jit(solution)/shard_map/ppermute | solution.py:356
  9.6 1.8 %collective-permute-done.1.near_ref.refs_4_ = f32[4,128]{1,0:T(4,128)S(1)} collective-permute-done((f32[4,128]{1,0:T(4,128)}, f32[4,128]{1,0:T(4,128)S(1)}, u32[]{:S(2)}, u32[]{:S(2)}) %collective-permute-start.1) | collective-permute-done | bytes 2080 | tf_op jit(solution)/shard_map/ppermute | solution.py:356
  11.4 1.1 %copy-done.1 = bf16[4,2,2,64,384]{4,3,2,1,0:T(8,128)(2,1)S(1)} copy-done((bf16[4,2,2,64,384]{4,3,2,1,0:T(8,128)(2,1)S(1)}, bf16[4,2,2,64,384]{4,3,2,1,0:T(8,128)(2,1)}, u32[]{:S(2)}) %copy-start.1) | copy-done | bytes 786456
  12.5 0.7 %copy-done.4 = f32[4,128]{1,0:T(4,128)S(1)} copy-done((f32[4,128]{1,0:T(4,128)S(1)}, f32[4,128]{1,0:T(4,128)}, u32[]{:S(2)}) %copy-start.4) | copy-done | bytes 2072
  13.2 2.2 %spread_rows.1 = (bf16[2,2,128,384]{3,2,1,0:T(8,128)(2,1)S(1)}, f32[2,2,128,384]{3,2,1,0:T(8,128)S(1)}, bf16[2,2,128,384]{3,2,1,0:T(8,128)(2,1)S(1)}, f32[2,2,128,384]{3,2,1,0:T(8,128)S(1)}) custom-call(f32[4,128]{1,0:T(4,128)S(1)} %copy-done.4, f32[4,128]{1,0:T(4,128)S(1)} %collective-permute-done.1.near_ref.refs_4_, ...), custom_call_target="tpu_custom_call" | custom-call | flops 402653184 | bytes 9437184 | tf_op jit(solution)/shard_map/spread_rows/pallas_call | solution.py:177
  15.4 2.1 %collective-permute-start.4 = (bf16[2,2,128,384]{3,2,1,0:T(8,128)(2,1)S(1)}, bf16[2,2,128,384]{3,2,1,0:T(8,128)(2,1)S(1)}, u32[]{:S(2)}, u32[]{:S(2)}) collective-permute-start(bf16[2,2,128,384]{3,2,1,0:T(8,128)(2,1)S(1)} %get-tuple-element.26), channel_id=1, source_target_pairs={{0,1},{1,0},{2,3},{3,2},{4,5},{5,4},{6,7},{7,6},{8,9},{9,8},{10,11... | collective-permute-start | bytes 1179656 | tf_op jit(solution)/shard_map/ppermute | solution.py:356
  17.5 1.5 %collective-permute-start.18 = (bf16[2,2,128,384]{3,2,1,0:T(8,128)(2,1)S(1)}, bf16[2,2,128,384]{3,2,1,0:T(8,128)(2,1)S(1)}, u32[]{:S(2)}, u32[]{:S(2)}) collective-permute-start(bf16[2,2,128,384]{3,2,1,0:T(8,128)(2,1)S(1)} %get-tuple-element.32), channel_id=1, source_target_pairs={{0,16},{1,17},{2,18},{3,19},{4,20},{5,21},{6,22},{7,23},{8,24},{9,... | collective-permute-start | bytes 1179656 | tf_op jit(solution)/shard_map/ppermute | solution.py:356
  19.0 3.6 %collective-permute-start.7 = (bf16[128,384]{1,0:T(8,128)(2,1)S(1)}, bf16[128,384]{1,0:T(8,128)(2,1)S(1)}, u32[]{:S(2)}, u32[]{:S(2)}) collective-permute-start(bf16[128,384]{1,0:T(8,128)(2,1)S(1)} %copy-done.3), channel_id=1, source_target_pairs={{0,6},{1,7},{2,0},{3,1},{4,2},{5,3},{6,4},{7,5},{8,14},{9,15},{10,... | collective-permute-start | bytes 294920 | tf_op jit(solution)/shard_map/ppermute | solution.py:359
  22.6 1.0 %collective-permute-start.5 = (bf16[128,384]{1,0:T(8,128)(2,1)S(1)}, bf16[128,384]{1,0:T(8,128)(2,1)S(1)}, u32[]{:S(2)}, u32[]{:S(2)}) collective-permute-start(bf16[128,384]{1,0:T(8,128)(2,1)S(1)} %copy-done.3), channel_id=1, source_target_pairs={{0,2},{1,3},{2,4},{3,5},{4,6},{5,7},{6,0},{7,1},{8,10},{9,11},{10,... | collective-permute-start | bytes 294920 | tf_op jit(solution)/shard_map/ppermute | solution.py:359
  23.6 2.5 %collective-permute-done.4.got_ref = bf16[2,2,128,384]{3,2,1,0:T(8,128)(2,1)S(1)} collective-permute-done((bf16[2,2,128,384]{3,2,1,0:T(8,128)(2,1)S(1)}, bf16[2,2,128,384]{3,2,1,0:T(8,128)(2,1)S(1)}, u32[]{:S(2)}, u32[]{:S(2)}) %collective-permute-start.4) | collective-permute-done | bytes 393248 | tf_op jit(solution)/shard_map/ppermute | solution.py:356
  26.1 0.1 first_sum.2
  26.2 4.6 %collective-permute-done.6.refs_2_ = bf16[128,384]{1,0:T(8,128)(2,1)S(1)} collective-permute-done((bf16[128,384]{1,0:T(8,128)(2,1)S(1)}, bf16[128,384]{1,0:T(8,128)(2,1)S(1)}, u32[]{:S(2)}, u32[]{:S(2)}) %collective-permute-start.6) | collective-permute-done | bytes 98336 | tf_op jit(solution)/shard_map/ppermute | solution.py:359
  30.8 0.6 collective-permute-start.9
  31.4 0.5 collective-permute-start.8
  31.9 1.5 %collective-permute-start.17 = (bf16[2,128,384]{2,1,0:T(8,128)(2,1)S(1)}, bf16[2,128,384]{2,1,0:T(8,128)(2,1)S(1)}, u32[]{:S(2)}, u32[]{:S(2)}) collective-permute-start(bf16[2,128,384]{2,1,0:T(8,128)(2,1)S(1)} %get-tuple-element.30), channel_id=1, source_target_pairs={{0,16},{1,17},{2,18},{3,19},{4,20},{5,21},{6,22},{7,23},{8,24},{9,... | collective-permute-start | bytes 589832 | tf_op jit(solution)/shard_map/ppermute | solution.py:356
  33.6 1.6 %collective-permute-start.19 = (bf16[2,128,384]{2,1,0:T(8,128)(2,1)S(1)}, bf16[2,128,384]{2,1,0:T(8,128)(2,1)S(1)}, u32[]{:S(2)}, u32[]{:S(2)}) collective-permute-start(bf16[2,128,384]{2,1,0:T(8,128)(2,1)S(1)} %get-tuple-element.34), channel_id=1, source_target_pairs={{0,1},{1,0},{2,3},{3,2},{4,5},{5,4},{6,7},{7,6},{8,9},{9,8},{10,11... | collective-permute-start | bytes 589832 | tf_op jit(solution)/shard_map/ppermute | solution.py:356
  35.1 7.8 %collective-permute-done.9.refs_8_ = bf16[4,128,384]{2,1,0:T(8,128)(2,1)S(1)} collective-permute-done((bf16[4,128,384]{2,1,0:T(8,128)(2,1)S(1)}, bf16[4,128,384]{2,1,0:T(8,128)(2,1)S(1)}, u32[]{:S(2)}, u32[]{:S(2)}) %collective-permute-start.9) | collective-permute-done | bytes 393248 | tf_op jit(solution)/shard_map/ppermute | solution.py:356
  43.0 0.6 collective-permute-start.12
  43.6 0.5 collective-permute-start.11
  44.1 0.1 collective-permute-start.14
  44.3 1.0 %collective-permute-done.17.a_got = bf16[2,128,384]{2,1,0:T(8,128)(2,1)S(1)} collective-permute-done((bf16[2,128,384]{2,1,0:T(8,128)(2,1)S(1)}, bf16[2,128,384]{2,1,0:T(8,128)(2,1)S(1)}, u32[]{:S(2)}, u32[]{:S(2)}) %collective-permute-start.17) | collective-permute-done | bytes 196640 | tf_op jit(solution)/shard_map/ppermute | solution.py:356
  45.3 0.5 collective-permute-start.10
  45.8 4.7 %collective-permute-done.11.refs_10_ = bf16[2,128,384]{2,1,0:T(8,128)(2,1)S(1)} collective-permute-done((bf16[2,128,384]{2,1,0:T(8,128)(2,1)S(1)}, bf16[2,128,384]{2,1,0:T(8,128)(2,1)S(1)}, u32[]{:S(2)}, u32[]{:S(2)}) %collective-permute-start.11) | collective-permute-done | bytes 196640 | tf_op jit(solution)/shard_map/ppermute | solution.py:356
  50.4 1.1 %collective-permute-done.10.refs_9_ = bf16[2,128,384]{2,1,0:T(8,128)(2,1)S(1)} collective-permute-done((bf16[2,128,384]{2,1,0:T(8,128)(2,1)S(1)}, bf16[2,128,384]{2,1,0:T(8,128)(2,1)S(1)}, u32[]{:S(2)}, u32[]{:S(2)}) %collective-permute-start.10) | collective-permute-done | bytes 196640 | tf_op jit(solution)/shard_map/ppermute | solution.py:356
  51.5 0.1 second_sum.1
  51.7 0.2 collective-permute-done.16.refs_15_
  51.9 1.7 %collective-permute-start.21 = (bf16[128,384]{1,0:T(8,128)(2,1)S(1)}, bf16[128,384]{1,0:T(8,128)(2,1)S(1)}, u32[]{:S(2)}, u32[]{:S(2)}) collective-permute-start(bf16[128,384]{1,0:T(8,128)(2,1)S(1)} %get-tuple-element.37), channel_id=1, source_target_pairs={{0,4},{1,5},{2,6},{3,7},{4,0},{5,1},{6,2},{7,3},{8,12},{9,13},{10,... | collective-permute-start | bytes 294920 | tf_op jit(solution)/shard_map/ppermute | solution.py:359
  53.6 2.8 %collective-permute-start.22 = (bf16[128,384]{1,0:T(8,128)(2,1)S(1)}, bf16[128,384]{1,0:T(8,128)(2,1)S(1)}, u32[]{:S(2)}, u32[]{:S(2)}) collective-permute-start(bf16[128,384]{1,0:T(8,128)(2,1)S(1)} %get-tuple-element.38), channel_id=1, source_target_pairs={{0,6},{1,7},{2,0},{3,1},{4,2},{5,3},{6,4},{7,5},{8,14},{9,15},{10,... | collective-permute-start | bytes 294920 | tf_op jit(solution)/shard_map/ppermute | solution.py:359
  56.4 6.2 %backward_rows.1 = (bf16[1,256,1024]{2,1,0:T(8,128)(2,1)}, bf16[1,1024,3072]{2,1,0:T(8,128)(2,1)}, f32[8,128]{1,0:T(8,128)S(1)}) custom-call(bf16[1,256,1024]{2,1,0:T(8,128)(2,1)S(1)} %copy-done.2, bf16[1,1024,3072]{2,1,0:T(8,128)(2,1)S(1)} %copy-done, f32[4,128]{1,0:T(4,128)S(1)} %copy-done.5, f32[4,128]{1,0:T(4,128)S(1)} %collective-permute-done.refs_3_, ...), custom_call_target="tpu_custom_call" | custom-call | flops 3221225472 | bytes 16777216 | tf_op jit(solution)/shard_map/backward_rows/pallas_call | solution.py:297
  62.7 0.7 %last_sum.1 = bf16[128,384]{1,0:T(8,128)(2,1)} custom-call(f32[8,128]{1,0:T(8,128)S(1)} %get-tuple-element.29._, f32[128,384]{1,0:T(8,128)S(1)} %get-tuple-element.35.first_ref, bf16[128,384]{1,0:T(8,128)(2,1)S(1)} %collective-permute-done.20.refs_0_, bf16[128,384]{1,0:T(8,128)(2,1)S(1)} %collective-permute-done.21.refs_1_, ...), custom_call_target="tpu_custom_call" | custom-call | tf_op jit(solution)/shard_map/last_sum/pallas_call | solution.py:335
  (36 shorter events, 0.3 us)
Async XLA Ops:
  0.6 18.4 %copy-start.3 = (bf16[128,384]{1,0:T(8,128)(2,1)S(1)}, bf16[128,384]{1,0:T(8,128)(2,1)}, u32[]{:S(2)}) copy-start(bf16[128,384]{1,0:T(8,128)(2,1)} %refs_0_.1) | copy-start | bytes 294916
  0.6 55.8 %copy-start.2 = (bf16[1,256,1024]{2,1,0:T(8,128)(2,1)S(1)}, bf16[1,256,1024]{2,1,0:T(8,128)(2,1)}, u32[]{:S(2)}) copy-start(bf16[1,256,1024]{2,1,0:T(8,128)(2,1)} %refs_0_.2) | copy-start | bytes 1572868
  6.5 49.9 %copy-start = (bf16[1,1024,3072]{2,1,0:T(8,128)(2,1)S(1)}, bf16[1,1024,3072]{2,1,0:T(8,128)(2,1)}, u32[]{:S(2)}) copy-start(bf16[1,1024,3072]{2,1,0:T(8,128)(2,1)} %refs_1_.1) | copy-start | bytes 18874372
  6.5 4.9 %collective-permute-start.3 = (bf16[4,2,2,64,384]{4,3,2,1,0:T(8,128)(2,1)}, bf16[4,2,2,64,384]{4,3,2,1,0:T(8,128)(2,1)S(1)}, u32[]{:S(2)}, u32[]{:S(2)}) collective-permute-start(bf16[4,2,2,64,384]{4,3,2,1,0:T(8,128)(2,1)} %get-tuple-element.24), channel_id=1, source_target_pairs={{0,8},{1,9},{2,10},{3,11},{4,12},{5,13},{6,14},{7,15},{8,0},{9,1},... | collective-permute-start | bytes 2359304 | tf_op jit(solution)/shard_map/ppermute | solution.py:356
  7.0 4.4 %collective-permute-start.1 = (f32[4,128]{1,0:T(4,128)}, f32[4,128]{1,0:T(4,128)S(1)}, u32[]{:S(2)}, u32[]{:S(2)}) collective-permute-start(f32[4,128]{1,0:T(4,128)} %get-tuple-element.22.own_ref.refs_2_), channel_id=1, source_target_pairs={{0,16},{1,17},{2,18},{3,19},{4,20},{5,21},{6,22},{7,23},{8,24},{9,... | collective-permute-start | bytes 6152 | tf_op jit(solution)/shard_map/ppermute | solution.py:356
  11.4 1.1 %copy-start.1 = (bf16[4,2,2,64,384]{4,3,2,1,0:T(8,128)(2,1)S(1)}, bf16[4,2,2,64,384]{4,3,2,1,0:T(8,128)(2,1)}, u32[]{:S(2)}) copy-start(bf16[4,2,2,64,384]{4,3,2,1,0:T(8,128)(2,1)} %get-tuple-element.23.keep_ref) | copy-start | bytes 2359300
  12.5 0.7 %copy-start.4 = (f32[4,128]{1,0:T(4,128)S(1)}, f32[4,128]{1,0:T(4,128)}, u32[]{:S(2)}) copy-start(f32[4,128]{1,0:T(4,128)} %get-tuple-element.22.own_ref.refs_2_) | copy-start | bytes 6148
  13.2 43.2 %copy-start.5 = (f32[4,128]{1,0:T(4,128)S(1)}, f32[4,128]{1,0:T(4,128)}, u32[]{:S(2)}) copy-start(f32[4,128]{1,0:T(4,128)} %get-tuple-element.22.own_ref.refs_2_) | copy-start | bytes 6148
  15.4 10.6 %collective-permute-start.4 = (bf16[2,2,128,384]{3,2,1,0:T(8,128)(2,1)S(1)}, bf16[2,2,128,384]{3,2,1,0:T(8,128)(2,1)S(1)}, u32[]{:S(2)}, u32[]{:S(2)}) collective-permute-start(bf16[2,2,128,384]{3,2,1,0:T(8,128)(2,1)S(1)} %get-tuple-element.26), channel_id=1, source_target_pairs={{0,1},{1,0},{2,3},{3,2},{4,5},{5,4},{6,7},{7,6},{8,9},{9,8},{10,11... | collective-permute-start | bytes 1179656 | tf_op jit(solution)/shard_map/ppermute | solution.py:356
  17.5 16.0 %collective-permute-start.18 = (bf16[2,2,128,384]{3,2,1,0:T(8,128)(2,1)S(1)}, bf16[2,2,128,384]{3,2,1,0:T(8,128)(2,1)S(1)}, u32[]{:S(2)}, u32[]{:S(2)}) collective-permute-start(bf16[2,2,128,384]{3,2,1,0:T(8,128)(2,1)S(1)} %get-tuple-element.32), channel_id=1, source_target_pairs={{0,16},{1,17},{2,18},{3,19},{4,20},{5,21},{6,22},{7,23},{8,24},{9,... | collective-permute-start | bytes 1179656 | tf_op jit(solution)/shard_map/ppermute | solution.py:356
  19.0 7.2 %collective-permute-start.7 = (bf16[128,384]{1,0:T(8,128)(2,1)S(1)}, bf16[128,384]{1,0:T(8,128)(2,1)S(1)}, u32[]{:S(2)}, u32[]{:S(2)}) collective-permute-start(bf16[128,384]{1,0:T(8,128)(2,1)S(1)} %copy-done.3), channel_id=1, source_target_pairs={{0,6},{1,7},{2,0},{3,1},{4,2},{5,3},{6,4},{7,5},{8,14},{9,15},{10,... | collective-permute-start | bytes 294920 | tf_op jit(solution)/shard_map/ppermute | solution.py:359
  22.6 8.2 %collective-permute-start.6 = (bf16[128,384]{1,0:T(8,128)(2,1)S(1)}, bf16[128,384]{1,0:T(8,128)(2,1)S(1)}, u32[]{:S(2)}, u32[]{:S(2)}) collective-permute-start(bf16[128,384]{1,0:T(8,128)(2,1)S(1)} %copy-done.3), channel_id=1, source_target_pairs={{0,4},{1,5},{2,6},{3,7},{4,0},{5,1},{6,2},{7,3},{8,12},{9,13},{10,... | collective-permute-start | bytes 294920 | tf_op jit(solution)/shard_map/ppermute | solution.py:359
  22.6 8.2 %collective-permute-start.5 = (bf16[128,384]{1,0:T(8,128)(2,1)S(1)}, bf16[128,384]{1,0:T(8,128)(2,1)S(1)}, u32[]{:S(2)}, u32[]{:S(2)}) collective-permute-start(bf16[128,384]{1,0:T(8,128)(2,1)S(1)} %copy-done.3), channel_id=1, source_target_pairs={{0,2},{1,3},{2,4},{3,5},{4,6},{5,7},{6,0},{7,1},{8,10},{9,11},{10,... | collective-permute-start | bytes 294920 | tf_op jit(solution)/shard_map/ppermute | solution.py:359
  30.8 12.1 %collective-permute-start.9 = (bf16[4,128,384]{2,1,0:T(8,128)(2,1)S(1)}, bf16[4,128,384]{2,1,0:T(8,128)(2,1)S(1)}, u32[]{:S(2)}, u32[]{:S(2)}) collective-permute-start(bf16[4,128,384]{2,1,0:T(8,128)(2,1)S(1)} %stack_blocks.1.refs_6_), channel_id=1, source_target_pairs={{0,16},{1,17},{2,18},{3,19},{4,20},{5,21},{6,22},{7,23},{8,24},{9,... | collective-permute-start | bytes 1179656 | tf_op jit(solution)/shard_map/ppermute | solution.py:356
  31.4 12.2 %collective-permute-start.8 = (bf16[4,128,384]{2,1,0:T(8,128)(2,1)S(1)}, bf16[4,128,384]{2,1,0:T(8,128)(2,1)S(1)}, u32[]{:S(2)}, u32[]{:S(2)}) collective-permute-start(bf16[4,128,384]{2,1,0:T(8,128)(2,1)S(1)} %stack_blocks.1.refs_6_), channel_id=1, source_target_pairs={{0,1},{1,0},{2,3},{3,2},{4,5},{5,4},{6,7},{7,6},{8,9},{9,8},{10,11... | collective-permute-start | bytes 1179656 | tf_op jit(solution)/shard_map/ppermute | solution.py:356
  31.9 13.3 %collective-permute-start.17 = (bf16[2,128,384]{2,1,0:T(8,128)(2,1)S(1)}, bf16[2,128,384]{2,1,0:T(8,128)(2,1)S(1)}, u32[]{:S(2)}, u32[]{:S(2)}) collective-permute-start(bf16[2,128,384]{2,1,0:T(8,128)(2,1)S(1)} %get-tuple-element.30), channel_id=1, source_target_pairs={{0,16},{1,17},{2,18},{3,19},{4,20},{5,21},{6,22},{7,23},{8,24},{9,... | collective-permute-start | bytes 589832 | tf_op jit(solution)/shard_map/ppermute | solution.py:356
  33.6 12.2 %collective-permute-start.19 = (bf16[2,128,384]{2,1,0:T(8,128)(2,1)S(1)}, bf16[2,128,384]{2,1,0:T(8,128)(2,1)S(1)}, u32[]{:S(2)}, u32[]{:S(2)}) collective-permute-start(bf16[2,128,384]{2,1,0:T(8,128)(2,1)S(1)} %get-tuple-element.34), channel_id=1, source_target_pairs={{0,1},{1,0},{2,3},{3,2},{4,5},{5,4},{6,7},{7,6},{8,9},{9,8},{10,11... | collective-permute-start | bytes 589832 | tf_op jit(solution)/shard_map/ppermute | solution.py:356
  35.1 7.9 %collective-permute-start = (f32[4,128]{1,0:T(4,128)S(1)}, f32[4,128]{1,0:T(4,128)S(1)}, u32[]{:S(2)}, u32[]{:S(2)}) collective-permute-start(f32[4,128]{1,0:T(4,128)S(1)} %copy-done.4), channel_id=1, source_target_pairs={{0,8},{1,9},{2,10},{3,11},{4,12},{5,13},{6,14},{7,15},{8,0},{9,1},... | collective-permute-start | bytes 6152 | tf_op jit(solution)/shard_map/ppermute | solution.py:356
  42.9 1.2 %collective-permute-start.2 = (f32[4,128]{1,0:T(4,128)S(1)}, f32[4,128]{1,0:T(4,128)S(1)}, u32[]{:S(2)}, u32[]{:S(2)}) collective-permute-start(f32[4,128]{1,0:T(4,128)S(1)} %collective-permute-done.1.near_ref.refs_4_), channel_id=1, source_target_pairs={{0,8},{1,9},{2,10},{3,11},{4,12},{5,13},{6,14},{7,15},{8,0},{9,1},... | collective-permute-start | bytes 6152 | tf_op jit(solution)/shard_map/ppermute | solution.py:356
  43.0 8.7 %collective-permute-start.12 = (bf16[4,128,384]{2,1,0:T(8,128)(2,1)S(1)}, bf16[4,128,384]{2,1,0:T(8,128)(2,1)S(1)}, u32[]{:S(2)}, u32[]{:S(2)}) collective-permute-start(bf16[4,128,384]{2,1,0:T(8,128)(2,1)S(1)} %stack_blocks.1.refs_6_), channel_id=1, source_target_pairs={{0,8},{1,9},{2,10},{3,11},{4,12},{5,13},{6,14},{7,15},{8,0},{9,1},... | collective-permute-start | bytes 1179656 | tf_op jit(solution)/shard_map/ppermute | solution.py:356
  43.6 6.9 %collective-permute-start.11 = (bf16[2,128,384]{2,1,0:T(8,128)(2,1)S(1)}, bf16[2,128,384]{2,1,0:T(8,128)(2,1)S(1)}, u32[]{:S(2)}, u32[]{:S(2)}) collective-permute-start(bf16[2,128,384]{2,1,0:T(8,128)(2,1)S(1)} %slice.9), channel_id=1, source_target_pairs={{0,1},{1,0},{2,3},{3,2},{4,5},{5,4},{6,7},{7,6},{8,9},{9,8},{10,11... | collective-permute-start | bytes 589832 | tf_op jit(solution)/shard_map/ppermute | solution.py:356
  44.1 9.5 %collective-permute-start.14 = (bf16[4,128,384]{2,1,0:T(8,128)(2,1)S(1)}, bf16[4,128,384]{2,1,0:T(8,128)(2,1)S(1)}, u32[]{:S(2)}, u32[]{:S(2)}) collective-permute-start(bf16[4,128,384]{2,1,0:T(8,128)(2,1)S(1)} %collective-permute-done.9.refs_8_), channel_id=1, source_target_pairs={{0,8},{1,9},{2,10},{3,11},{4,12},{5,13},{6,14},{7,15},{8,0},{9,1},... | collective-permute-start | bytes 1179656 | tf_op jit(solution)/shard_map/ppermute | solution.py:356
  45.3 6.2 %collective-permute-start.10 = (bf16[2,128,384]{2,1,0:T(8,128)(2,1)S(1)}, bf16[2,128,384]{2,1,0:T(8,128)(2,1)S(1)}, u32[]{:S(2)}, u32[]{:S(2)}) collective-permute-start(bf16[2,128,384]{2,1,0:T(8,128)(2,1)S(1)} %slice.8), channel_id=1, source_target_pairs={{0,16},{1,17},{2,18},{3,19},{4,20},{5,21},{6,22},{7,23},{8,24},{9,... | collective-permute-start | bytes 589832 | tf_op jit(solution)/shard_map/ppermute | solution.py:356
  45.8 10.6 %collective-permute-start.13 = (bf16[4,128,384]{2,1,0:T(8,128)(2,1)S(1)}, bf16[4,128,384]{2,1,0:T(8,128)(2,1)S(1)}, u32[]{:S(2)}, u32[]{:S(2)}) collective-permute-start(bf16[4,128,384]{2,1,0:T(8,128)(2,1)S(1)} %collective-permute-done.8.refs_7_), channel_id=1, source_target_pairs={{0,8},{1,9},{2,10},{3,11},{4,12},{5,13},{6,14},{7,15},{8,0},{9,1},... | collective-permute-start | bytes 1179656 | tf_op jit(solution)/shard_map/ppermute | solution.py:356
  50.4 1.4 %collective-permute-start.16 = (bf16[2,128,384]{2,1,0:T(8,128)(2,1)S(1)}, bf16[2,128,384]{2,1,0:T(8,128)(2,1)S(1)}, u32[]{:S(2)}, u32[]{:S(2)}) collective-permute-start(bf16[2,128,384]{2,1,0:T(8,128)(2,1)S(1)} %collective-permute-done.11.refs_10_), channel_id=1, source_target_pairs={{0,8},{1,9},{2,10},{3,11},{4,12},{5,13},{6,14},{7,15},{8,0},{9,1},... | collective-permute-start | bytes 589832 | tf_op jit(solution)/shard_map/ppermute | solution.py:356
  51.5 4.9 %collective-permute-start.15 = (bf16[2,128,384]{2,1,0:T(8,128)(2,1)S(1)}, bf16[2,128,384]{2,1,0:T(8,128)(2,1)S(1)}, u32[]{:S(2)}, u32[]{:S(2)}) collective-permute-start(bf16[2,128,384]{2,1,0:T(8,128)(2,1)S(1)} %collective-permute-done.10.refs_9_), channel_id=1, source_target_pairs={{0,8},{1,9},{2,10},{3,11},{4,12},{5,13},{6,14},{7,15},{8,0},{9,1},... | collective-permute-start | bytes 589832 | tf_op jit(solution)/shard_map/ppermute | solution.py:356
  51.7 11.0 %collective-permute-start.20 = (bf16[128,384]{1,0:T(8,128)(2,1)S(1)}, bf16[128,384]{1,0:T(8,128)(2,1)S(1)}, u32[]{:S(2)}, u32[]{:S(2)}) collective-permute-start(bf16[128,384]{1,0:T(8,128)(2,1)S(1)} %get-tuple-element.36), channel_id=1, source_target_pairs={{0,2},{1,3},{2,4},{3,5},{4,6},{5,7},{6,0},{7,1},{8,10},{9,11},{10,... | collective-permute-start | bytes 294920 | tf_op jit(solution)/shard_map/ppermute | solution.py:359
  51.9 10.8 %collective-permute-start.21 = (bf16[128,384]{1,0:T(8,128)(2,1)S(1)}, bf16[128,384]{1,0:T(8,128)(2,1)S(1)}, u32[]{:S(2)}, u32[]{:S(2)}) collective-permute-start(bf16[128,384]{1,0:T(8,128)(2,1)S(1)} %get-tuple-element.37), channel_id=1, source_target_pairs={{0,4},{1,5},{2,6},{3,7},{4,0},{5,1},{6,2},{7,3},{8,12},{9,13},{10,... | collective-permute-start | bytes 294920 | tf_op jit(solution)/shard_map/ppermute | solution.py:359
  53.6 9.1 %collective-permute-start.22 = (bf16[128,384]{1,0:T(8,128)(2,1)S(1)}, bf16[128,384]{1,0:T(8,128)(2,1)S(1)}, u32[]{:S(2)}, u32[]{:S(2)}) collective-permute-start(bf16[128,384]{1,0:T(8,128)(2,1)S(1)} %get-tuple-element.38), channel_id=1, source_target_pairs={{0,6},{1,7},{2,0},{3,1},{4,2},{5,3},{6,4},{7,5},{8,14},{9,15},{10,... | collective-permute-start | bytes 294920 | tf_op jit(solution)/shard_map/ppermute | solution.py:359

commit v3 on v2

--- a/solution.py
+++ b/solution.py
@@ -76,32 +76,36 @@
 
 
 def forward_kernel(nz, capacity, ids_ref, coef_ref, hidden_ref, weight_ref, keep_ref, send_ref, meta_ref, *scratch):
-    ids, held, wide, rows_ref, sems = scratch
+    ids, held, wide, part, rows, sems = scratch
     me = lax.axis_index("dp")
     feat = keep_ref.shape[-1]
-    copies = [pltpu.make_async_copy(hidden_ref.at[0], held, sems.at[nz])]
-    for z in range(nz):
-        part = weight_ref.at[0, :, pl.ds(2 * z * feat, 2 * feat)]
-        copies.append(pltpu.make_async_copy(part, wide.at[z], sems.at[z]))
-    small = pltpu.make_async_copy(ids_ref, ids, sems.at[nz + 1])
-    small.start()
-    coefs = pltpu.make_async_copy(coef_ref, meta_ref.at[2:4], sems.at[nz + 2])
-    coefs.start()
-    for copy in copies:
+    ff = wide.shape[0]
+    mid = ff // 2
+    small = pltpu.make_async_copy(ids_ref, ids, sems.at[0])
+    coefs = pltpu.make_async_copy(coef_ref, meta_ref.at[2:4], sems.at[1])
+    first = pltpu.make_async_copy(hidden_ref.at[0], held, sems.at[2])
+    low = pltpu.make_async_copy(weight_ref.at[0, pl.ds(0, mid)], wide.at[pl.ds(0, mid)], sems.at[3])
+    high = pltpu.make_async_copy(weight_ref.at[0, pl.ds(mid, mid)], wide.at[pl.ds(mid, mid)], sems.at[4])
+    for copy in (small, coefs, first, low, high):
         copy.start()
     small.wait()
     meta_ref[0:2] = ids[...].astype(F32)
     coefs.wait()
-    copies[0].wait()
+    first.wait()
+    low.wait()
     for z in range(nz):
-        copies[z + 1].wait()
-        rows_ref[...] = jnp.dot(held[...], wide[z], preferred_element_type=F32).astype(BF)
+        columns = slice(2 * z * feat, 2 * (z + 1) * feat)
+        part[z] = jnp.dot(held[:, :mid], wide[:mid, columns], preferred_element_type=F32)
+    high.wait()
+    for z in range(nz):
+        columns = slice(2 * z * feat, 2 * (z + 1) * feat)
+        rest = jnp.dot(held[:, mid:], wide[mid:, columns], preferred_element_type=F32)
+        rows[...] = (part[z] + rest).astype(BF)
         for dy in range(2):
             for dc, out in ((0, keep_ref), (1, send_ref)):
-                source = me ^ (2 * dy + dc)
-                at = pl.multiple_of(source * capacity, capacity)
+                at = pl.multiple_of((me ^ (2 * dy + dc)) * capacity, capacity)
                 for x in range(2):
-                    out[z, x, dy] = rows_ref[pl.ds(at, capacity), x * feat : (x + 1) * feat]
+                    out[z, x, dy] = rows[pl.ds(at, capacity), x * feat : (x + 1) * feat]
 
 
 def forward(ids, coefs, hidden, weight, feat, dp_count):
@@ -118,11 +122,12 @@
         scratch_shapes=[
             pltpu.VMEM(ids.shape, jnp.int32),
             pltpu.VMEM((slots, ff), BF),
-            pltpu.VMEM((nz, ff, 2 * feat), BF),
+            pltpu.VMEM((ff, width), BF),
+            pltpu.VMEM((nz, slots, 2 * feat), F32),
             pltpu.VMEM((slots, 2 * feat), BF),
-            pltpu.SemaphoreType.DMA((nz + 3,)),
+            pltpu.SemaphoreType.DMA((5,)),
         ],
-        compiler_params=pltpu.CompilerParams(vmem_limit_bytes=58 << 20),
+        compiler_params=pltpu.CompilerParams(vmem_limit_bytes=50 << 20),
         cost_estimate=pl.CostEstimate(
             flops=2 * slots * ff * width, bytes_accessed=2 * (ff * width + slots * (ff + width)), transcendentals=0
         ),
@@ -130,99 +135,104 @@
     )(ids, coefs, hidden, weight)
 
 
-def spread_kernel(nz, capacity, own_ref, near_ref, keep_ref, got_ref, *refs):
-    (to_x, by_x, to_y, by_y), hots, cols = refs[:4], refs[4], refs[5]
-    step, me, x = pl.program_id(0), lax.axis_index("dp"), lax.axis_index("cuts") % 2
-
-    @pl.when(step == 0)
-    def _():
-        for dy, meta_ref in enumerate((own_ref, near_ref)):
-            for dc in range(2):
-                hot, weight = routing(meta_ref[...], me ^ dc, capacity)
-                tok = hot.shape[1]
-                hots[dy, dc] = hot.astype(BF)
-                cols[dy, dc] = jnp.broadcast_to(weight, (tok, tok)).T
-
-    def block(dy, dx):
-        total = None
-        for dc, rows in ((0, keep_ref), (1, got_ref)):
-            picked = lax.dot_general(
-                hots[dy, dc], rows[0, x ^ dx, dy], (((0,), (0,)), ((), ())), preferred_element_type=F32
-            )
-            term = picked * cols[dy, dc][:, 0:1]
-            total = term if total is None else total + term
-        return total
-
-    @pl.when(step < nz // 2)
-    def _():
-        for dy in range(2):
-            to_x[dy, 0] = block(dy, 1).astype(BF)
-            by_x[dy, 0] = block(dy, 0)
-
-    @pl.when(step >= nz // 2)
-    def _():
-        for dx in range(2):
-            to_y[dx, 0] = block(1, dx).astype(BF)
-            by_y[dx, 0] = block(0, dx)
-
-
-def spread(own, near, keep, got):
-    nz, _, _, capacity, feat = keep.shape
-    tok, half = own.shape[1], nz // 2
-    rows = pl.BlockSpec((1, 2, 2, capacity, feat), lambda k: (k, 0, 0, 0, 0))
-    meta = pl.BlockSpec((4, tok), lambda k: (0, 0))
-    first = pl.BlockSpec((2, 1, tok, feat), lambda k: (0, jnp.minimum(k, half - 1), 0, 0))
-    second = pl.BlockSpec((2, 1, tok, feat), lambda k: (0, jnp.maximum(k - half, 0), 0, 0))
-    shape = (2, half, tok, feat)
+def spread_kernel(nz, capacity, own_ref, near_ref, keep_ref, got_ref, grad_ref, *refs):
+    to_x, by_x, to_y, by_y = refs
+    me, x = lax.axis_index("dp"), lax.axis_index("cuts") % 2
+    tok = grad_ref.shape[0]
+    half = nz // 2
+    to_x[nz] = grad_ref[...]
+    to_y[nz] = grad_ref[...]
+    for dy, meta_ref in enumerate((own_ref, near_ref)):
+        hots, cols = [], []
+        for dc in range(2):
+            hot, weight = routing(meta_ref[...], me ^ dc, capacity)
+            hots.append(hot.astype(BF))
+            cols.append(jnp.broadcast_to(weight, (tok, tok)).T[:, 0:1])
+
+        def block(z, dx):
+            total = None
+            for dc, rows in ((0, keep_ref), (1, got_ref)):
+                picked = lax.dot_general(
+                    hots[dc], rows[z, x ^ dx, dy], (((0,), (0,)), ((), ())), preferred_element_type=F32
+                )
+                term = picked * cols[dc]
+                total = term if total is None else total + term
+            return total
+
+        for z in range(half):
+            to_x[half * dy + z] = block(z, 1).astype(BF)
+            by_x[half * dy + z] = block(z, 0)
+            for dx in range(2):
+                if dy:
+                    to_y[half * dx + z] = block(half + z, dx).astype(BF)
+                else:
+                    by_y[half * dx + z] = block(half + z, dx)
+
+
+def spread(own, near, keep, got, grad):
+    nz, _, _, capacity, _ = keep.shape
+    tok, feat = grad.shape
+    shapes = [jax.ShapeDtypeStruct((nz + 1, tok, feat), BF), jax.ShapeDtypeStruct((nz, tok, feat), F32)] * 2
     return pl.pallas_call(
         functools.partial(spread_kernel, nz, capacity),
-        grid=(nz,),
-        in_specs=[meta, meta, rows, rows],
-        out_specs=[first, first, second, second],
-        out_shape=[jax.ShapeDtypeStruct(shape, t) for t in (BF, F32, BF, F32)],
-        scratch_shapes=[pltpu.VMEM((2, 2, capacity, tok), BF), pltpu.VMEM((2, 2, tok, tok), F32)],
-        compiler_params=pltpu.CompilerParams(vmem_limit_bytes=16 << 20),
+        out_shape=shapes,
+        compiler_params=pltpu.CompilerParams(vmem_limit_bytes=24 << 20),
         cost_estimate=pl.CostEstimate(
             flops=32 * tok * capacity * nz * feat, bytes_accessed=48 * tok * nz * feat, transcendentals=0
         ),
         name="spread_rows",
-    )(own, near, keep, got)
-
-
-def first_sum_kernel(kept_ref, got_ref, keep_out, send_out):
-    keep_out[...] = kept_ref[0] + got_ref[0].astype(F32)
-    send_out[...] = (kept_ref[1] + got_ref[1].astype(F32)).astype(BF)
-
-
-def first_sum(kept, got):
-    shape = kept.shape[1:]
-    return pl.pallas_call(
-        first_sum_kernel,
-        out_shape=[jax.ShapeDtypeStruct(shape, F32), jax.ShapeDtypeStruct(shape, BF)],
+    )(own, near, keep, got, grad)
+
+
+def first_sum_kernel(half, _, x_kept, x_got, y_kept, y_got, *refs):
+    far, (x_keep, x_send, y_keep, y_send, own, stacked) = refs[:-6], refs[-6:]
+    for k, ref in enumerate(far):
+        stacked[k] = ref[...]
+    own[0] = x_got[2 * half]
+    own[1] = y_got[2 * half]
+    for kept, got, keep, send in ((x_kept, x_got, x_keep, x_send), (y_kept, y_got, y_keep, y_send)):
+        for z in range(half):
+            keep[z] = kept[z] + got[z].astype(F32)
+            send[z] = (kept[half + z] + got[half + z].astype(F32)).astype(BF)
+
+
+def first_sum(after, x_kept, x_got, y_kept, y_got, far):
+    nz, tok, feat = x_kept.shape
+    half = nz // 2
+    shapes = [
+        jax.ShapeDtypeStruct((half, tok, feat), F32),
+        jax.ShapeDtypeStruct((half, tok, feat), BF),
+    ]
+    return pl.pallas_call(
+        functools.partial(first_sum_kernel, half),
+        in_specs=[pl.BlockSpec(memory_space=pl.ANY)] + [pl.BlockSpec(memory_space=pltpu.VMEM)] * (4 + len(far)),
+        out_shape=shapes + shapes + [jax.ShapeDtypeStruct((n, tok, feat), BF) for n in (2, len(far))],
         compiler_params=pltpu.CompilerParams(vmem_limit_bytes=16 << 20),
+        cost_estimate=pl.CostEstimate(flops=1000_000_000, bytes_accessed=0, transcendentals=0),
         name="first_sum",
-    )(kept, got)
-
-
-def second_sum_kernel(nz, a_ref, a_got, b_ref, b_got, *refs):
+    )(after, x_kept, x_got, y_kept, y_got, *far)
+
+
+def second_sum_kernel(nz, x_kept, y_kept, by_y, by_x, *refs):
     outs, total = refs[:nz], refs[nz]
     z, half = lax.axis_index("cuts") // 2, nz // 2
-    total[:half] = a_ref[...] + a_got[...].astype(F32)
-    total[half:] = b_ref[...] + b_got[...].astype(F32)
+    total[:half] = x_kept[...] + by_y[...].astype(F32)
+    total[half:] = y_kept[...] + by_x[...].astype(F32)
     for k in range(nz):
         outs[k][...] = total[lax.rem(z + k, nz)].astype(outs[k].dtype)
 
 
-def second_sum(a, a_got, b, b_got):
-    half, tok, feat = a.shape
+def second_sum(x_kept, y_kept, by_y, by_x):
+    half, tok, feat = x_kept.shape
     nz = 2 * half
     return pl.pallas_call(
         functools.partial(second_sum_kernel, nz),
         out_shape=[jax.ShapeDtypeStruct((tok, feat), F32 if k == 0 else BF) for k in range(nz)],
         scratch_shapes=[pltpu.VMEM((nz, tok, feat), F32)],
         compiler_params=pltpu.CompilerParams(vmem_limit_bytes=16 << 20),
+        cost_estimate=pl.CostEstimate(flops=5000_000_000, bytes_accessed=0, transcendentals=0),
         name="second_sum",
-    )(a, a_got, b, b_got)
+    )(x_kept, y_kept, by_y, by_x)
 
 
 def stack_kernel(_, *refs):
@@ -238,16 +248,21 @@
         out_specs=vmem,
         out_shape=jax.ShapeDtypeStruct((len(parts), *parts[0].shape), parts[0].dtype),
         compiler_params=pltpu.CompilerParams(vmem_limit_bytes=16 << 20),
+        cost_estimate=pl.CostEstimate(flops=1000_000_000, bytes_accessed=0, transcendentals=0),
         name="stack_blocks",
     )(after, *parts)
 
 
+PER_CORE = 7
+
+
 def backward_kernel(nz, capacity, *refs):
     hidden_ref, weight_ref = refs[:2]
-    metas, grads, (hid_out, down_out, mark) = refs[2:6], refs[6:16], refs[16:19]
-    made, rows_ref, turned, total, done, hots, cols, sems = refs[19:]
+    metas, grads, refs = refs[2:6], refs[6 : 6 + 2 * PER_CORE], refs[-11:]
+    hid_out, down_out, mark = refs[:3]
+    made, rows_ref, turned, total, done, hots, cols, sems = refs[3:]
     me, x, z = lax.axis_index("dp"), lax.axis_index("cuts") % 2, lax.axis_index("cuts") // 2
-    feat, half = grads[0].shape[-1], nz // 2
+    feat = grads[0].shape[-1]
 
     for q in range(4):
         hot, weight = routing(metas[q][...], me, capacity)
@@ -264,11 +279,11 @@
     leaving = []
     for k in range(nz):
         for dc in range(2):
-            own, by_x, by_y, low, high = grads[5 * dc : 5 * dc + 5]
-            put(0, dc, own[k])
-            put(1, dc, by_x[k])
-            put(0, 2 + dc, by_y[k])
-            put(1, 2 + dc, low[k] if k < half else high[k - half])
+            own, cross, plane, far, far_x, far_y, far_xy = grads[PER_CORE * dc : PER_CORE * (dc + 1)]
+            put(0, dc, own[...] if k == 0 else far[k - 1])
+            put(1, dc, plane[0] if k == 0 else far_x[k - 1])
+            put(0, 2 + dc, plane[1] if k == 0 else far_y[k - 1])
+            put(1, 2 + dc, cross[...] if k == 0 else far_xy[k - 1])
         rows = rows_ref[...]
         column = pl.ds(pl.multiple_of(lax.rem(z - k + nz, nz) * 2 * feat, 2 * feat), 2 * feat)
         part = lax.dot_general(rows, weight_ref[0, :, column], (((1,), (1,)), ((), ())), preferred_element_type=F32)
@@ -288,15 +303,15 @@
     mark[...] = jnp.zeros_like(mark)
 
 
-def backward(hidden, weight, metas, grads):
-    nz, tok, feat = grads[0].shape
+def backward(hidden, weight, metas, grads, after):
+    tok, feat = grads[0].shape
     _, slots, ff = hidden.shape
     width = weight.shape[2]
-    capacity = slots // 4
+    nz, capacity = width // (2 * feat), slots // 4
     anywhere, vmem = pl.BlockSpec(memory_space=pl.ANY), pl.BlockSpec(memory_space=pltpu.VMEM)
     return pl.pallas_call(
         functools.partial(backward_kernel, nz, capacity),
-        in_specs=[vmem] * 16,
+        in_specs=[vmem] * (6 + 2 * PER_CORE) + [anywhere] * len(after),
         out_specs=[anywhere, anywhere, vmem],
         scratch_shapes=[
             pltpu.VMEM((2, ff, 2 * feat), BF),
@@ -314,13 +329,9 @@
             jax.ShapeDtypeStruct((8, 128), F32),
         ],
         compiler_params=pltpu.CompilerParams(vmem_limit_bytes=32 << 20),
-        cost_estimate=pl.CostEstimate(
-            flops=4 * slots * ff * width,
-            bytes_accessed=4 * ff * width + 4 * slots * ff + 8 * tok * width,
-            transcendentals=0,
-        ),
+        cost_estimate=pl.CostEstimate(flops=3000_000_000, bytes_accessed=0, transcendentals=0),
         name="backward_rows",
-    )(hidden, weight, *metas, *grads)
+    )(hidden, weight, *metas, *grads, *after)
 
 
 def last_sum_kernel(_, first_ref, *refs):
@@ -338,6 +349,7 @@
         out_specs=vmem,
         out_shape=jax.ShapeDtypeStruct(parts[0].shape, BF),
         compiler_params=pltpu.CompilerParams(vmem_limit_bytes=16 << 20),
+        cost_estimate=pl.CostEstimate(flops=1000_000_000, bytes_accessed=0, transcendentals=0),
         name="last_sum",
     )(after, *parts)
 
@@ -345,7 +357,7 @@
 def shared(hidden, down_weight, expert_ids, combine, out_grad):
     dp_count, cut_count = lax.axis_size("dp"), lax.axis_size("cuts")
     nz = cut_count // 2
-    tok, feat = out_grad.shape
+    feat = out_grad.shape[1]
 
     def send(value, dp_flip, cut_flip):
         pairs = [
@@ -358,23 +370,27 @@
     def along(value, k):
         return lax.ppermute(value, "cuts", [(c, (c + 2 * k) % cut_count) for c in range(cut_count)])
 
-    half = nz // 2
-    keep, away, own = forward(expert_ids.T, combine.T, hidden, down_weight, feat, dp_count)
+    keep, away, own = forward(expert_ids.T, combine.T, hidden, down_weight, out_grad.shape[1], dp_count)
     near = send(own, 2, 0)
     got = send(away, 1, 0)
-    to_x, by_x, to_y, by_y = spread(own, near, keep, got)
+    to_x, by_x, to_y, by_y = spread(own, near, keep, got, out_grad)
     mine, _ = lax.optimization_barrier((out_grad, by_x))
-    blocks = [mine] + [along(mine, k) for k in range(1, nz)]
-    a, a_send = first_sum(by_x, send(to_x, 0, 1))
-    b, b_send = first_sum(by_y, send(to_y, 2, 0))
-    terms = second_sum(a, send(a_send, 2, 0), b, send(b_send, 0, 1))
-    blocks = stack(blocks, a)
-    from_x, from_y = send(blocks, 0, 1), send(blocks, 2, 0)
-    parts = [blocks, from_x, from_y, send(from_x[:half], 2, 0), send(from_y[half:], 0, 1)]
-    grads = parts + [send(p, 1, 0) for p in parts]
+    far = [along(mine, k) for k in range(1, nz)]
+    cross = send(mine, 2, 1)
+    a, a_send, b, b_send, plane, far = first_sum(cross, by_x, send(to_x, 0, 1), by_y, send(to_y, 2, 0), far)
+    *terms, = second_sum(a, b, send(a_send, 2, 0), send(b_send, 0, 1))
+    sums = [terms[0]] + [along(terms[k], k) for k in range(1, nz)]
+
+    far_y, far_x = send(far, 2, 0), send(far, 0, 1)
+    far_xy = stack([along(cross, k) for k in range(1, nz)], a)
+    parts = [out_grad, cross, plane, far, far_x, far_y, far_xy]
+    after = [None, None, None, None, None, None, sums[1]]
+    grads = parts + [
+        send(p if held is None else lax.optimization_barrier((p, held))[0], 1, 0) for p, held in zip(parts, after)
+    ]
     metas = (own, send(own, 1, 0), near, send(near, 1, 0))
-    hid_grad, down_grad, mark = backward(hidden, down_weight, metas, grads)
-    mixed = last_sum([terms[0]] + [along(terms[k], k) for k in range(1, nz)], mark)
+    hid_grad, down_grad, mark = backward(hidden, down_weight, metas, grads, ())
+    mixed = last_sum(sums, mark)
     return (mixed, hid_grad, down_grad)
 
 

time: 63.6 us -> 61.1 us (0.961)
  waiting for transfers between devices: 23.6 us -> 15.3 us
  starting transfers between devices: 21.8 us -> 29.4 us
  Pallas kernels: 15.3 us -> 13 us
    ppermute x17 -> x18, waiting for transfers between devices: 18.9 us -> 5 us  [send(): return lax.ppermute(value, ('dp', 'cuts'), pairs)]
    ppermute x6 -> x9, waiting for transfers between devices: 4.61 us -> 10.3 us  [along(): lax.ppermute(value, 'cuts', [(c, (c + 2 * k) % cut_count) for c in range(...]
    ppermute x6 -> x9, starting transfers between devices: 9.17 us -> 14.4 us  [along(): lax.ppermute(value, 'cuts', [(c, (c + 2 * k) % cut_count) for c in range(...]
    ppermute x17 -> x18, starting transfers between devices: 12.6 us -> 15 us  [send(): return lax.ppermute(value, ('dp', 'cuts'), pairs)]
    pallas_call x1, Pallas kernels: 5.81 us -> 4.06 us  [forward(): pl.pallas_call(functools.partial(forward_kernel, nz, capacity), in_specs=...]
    pallas_call x3 -> x2, Pallas kernels: 2.42 us -> 1.84 us  [the longest x1 1.64 us: spread(): pl.pallas_call(functools.partial(spread_kernel, nz, capacity), out_shape=...]
  transfers between devices with their start and end apart: 23 -> 27, of which waited for: 8 -> 9; matrix products, arithmetic and copies ran while one was open for 0% -> 0% of each run, Pallas kernels for 10% -> 11%
where the time goes in v3:
time: 61.1 us; the launch traced here: 60.9 us
  starting transfers between devices  29.4 us (48%)
  waiting for transfers between devices  15.3 us (25%)
  Pallas kernels  13 us (21%)
  local copies, waits for them, and re-layouts  2.4 us (4%)
  between operations  0.76 us (1%)
    ppermute x18, starting transfers between devices, send(): return lax.ppermute(value, ('dp', 'cuts'), pairs)  15 us
    ppermute x9, starting transfers between devices, along(): lax.ppermute(value, 'cuts', [(c, (c + 2 * k) % cut_count) for c in range(...  14.4 us
    ppermute x9, waiting for transfers between devices, along(): lax.ppermute(value, 'cuts', [(c, (c + 2 * k) % cut_count) for c in range(...  10.3 us
    pallas_call x1, Pallas kernels, backward(): pl.pallas_call(functools.partial(backward_kernel, nz, capacity), in_specs...  6.25 us
    ppermute x18, waiting for transfers between devices, send(): return lax.ppermute(value, ('dp', 'cuts'), pairs)  5 us
    pallas_call x1, Pallas kernels, forward(): pl.pallas_call(functools.partial(forward_kernel, nz, capacity), in_specs=...  4.06 us
    unnamed x12, local copies, waits for them, and re-layouts  2.4 us
    pallas_call x1, Pallas kernels, spread(): pl.pallas_call(functools.partial(spread_kernel, nz, capacity), out_shape=...  1.64 us
  transfers between devices with their start and end apart: 27, of which 9 were waited for; matrix products, arithmetic and copies ran while one was open for 0% of the time, Pallas kernels for 11%

profile of v3, /device:TPU:0, one launch (start us, length us, event | category | flops | bytes accessed | tf_op | source)
XLA Modules:
  0.0 60.9 jit_solution(6893393995694623973)
XLA Ops:
  0.6 1.0 %copy-done = bf16[1,256,1024]{2,1,0:T(8,128)(2,1)S(1)} copy-done((bf16[1,256,1024]{2,1,0:T(8,128)(2,1)S(1)}, bf16[1,256,1024]{2,1,0:T(8,128)(2,1)}, u32[]{:S(2)}) %copy-start) | copy-done | bytes 524312
  1.7 0.7 %copy-done.2 = s32[128,2]{0,1:T(2,128)S(1)} copy-done((s32[128,2]{0,1:T(2,128)S(1)}, s32[128,2]{0,1:T(2,128)}, u32[]{:S(2)}) %copy-start.2) | copy-done | bytes 1048
  2.4 0.7 %copy-done.3 = f32[128,2]{0,1:T(2,128)S(1)} copy-done((f32[128,2]{0,1:T(2,128)S(1)}, f32[128,2]{0,1:T(2,128)}, u32[]{:S(2)}) %copy-start.3) | copy-done | bytes 1048
  3.0 4.1 %forward_rows.1 = (bf16[4,2,2,64,384]{4,3,2,1,0:T(8,128)(2,1)S(1)}, bf16[4,2,2,64,384]{4,3,2,1,0:T(8,128)(2,1)S(1)}, f32[4,128]{1,0:T(4,128)S(1)}) custom-call(s32[2,128]{1,0:T(2,128)S(1)} %bitcast.4, f32[2,128]{1,0:T(2,128)S(1)} %bitcast.5, bf16[1,256,1024]{2,1,0:T(8,128)(2,1)S(1)} %copy-done, bf16[1,1024,3072]{2,1,0:T(8,128)(2,1)} %refs_1_.1), custom_call_target="tpu_custom_call" | custom-call | flops 1610612736 | bytes 8388608 | tf_op jit(solution)/shard_map/forward_rows/pallas_call | solution.py:117
  7.1 0.5 collective-permute-start.3
  7.6 2.6 %collective-permute-start.1 = (f32[4,128]{1,0:T(4,128)S(1)}, f32[4,128]{1,0:T(4,128)S(1)}, u32[]{:S(2)}, u32[]{:S(2)}) collective-permute-start(f32[4,128]{1,0:T(4,128)S(1)} %get-tuple-element.25.own_ref.refs_2_), channel_id=1, source_target_pairs={{0,16},{1,17},{2,18},{3,19},{4,20},{5,21},{6,22},{7,23},{8,24},{9,... | collective-permute-start | bytes 6152 | tf_op jit(solution)/shard_map/ppermute | solution.py:368
  10.2 1.6 %collective-permute-done.1.near_ref.refs_4_ = f32[4,128]{1,0:T(4,128)S(1)} collective-permute-done((f32[4,128]{1,0:T(4,128)S(1)}, f32[4,128]{1,0:T(4,128)S(1)}, u32[]{:S(2)}, u32[]{:S(2)}) %collective-permute-start.1) | collective-permute-done | bytes 2080 | tf_op jit(solution)/shard_map/ppermute | solution.py:368
  11.8 1.6 %spread_rows.1 = (bf16[5,128,384]{2,1,0:T(8,128)(2,1)S(1)}, f32[4,128,384]{2,1,0:T(8,128)S(1)}, bf16[5,128,384]{2,1,0:T(8,128)(2,1)S(1)}, f32[4,128,384]{2,1,0:T(8,128)S(1)}) custom-call(f32[4,128]{1,0:T(4,128)S(1)} %get-tuple-element.25.own_ref.refs_2_, f32[4,128]{1,0:T(4,128)S(1)} %collective-permute-done.1.near_ref.refs_4_, ...), custom_call_target="tpu_custom_call" | custom-call | flops 402653184 | bytes 9437184 | tf_op jit(solution)/shard_map/spread_rows/pallas_call | solution.py:176
  13.4 2.1 %collective-permute-start.5 = (bf16[5,128,384]{2,1,0:T(8,128)(2,1)S(1)}, bf16[5,128,384]{2,1,0:T(8,128)(2,1)S(1)}, u32[]{:S(2)}, u32[]{:S(2)}) collective-permute-start(bf16[5,128,384]{2,1,0:T(8,128)(2,1)S(1)} %get-tuple-element.30), channel_id=1, source_target_pairs={{0,1},{1,0},{2,3},{3,2},{4,5},{5,4},{6,7},{7,6},{8,9},{9,8},{10,11... | collective-permute-start | bytes 1474568 | tf_op jit(solution)/shard_map/ppermute | solution.py:368
  15.5 1.5 %collective-permute-start.6 = (bf16[5,128,384]{2,1,0:T(8,128)(2,1)S(1)}, bf16[5,128,384]{2,1,0:T(8,128)(2,1)S(1)}, u32[]{:S(2)}, u32[]{:S(2)}) collective-permute-start(bf16[5,128,384]{2,1,0:T(8,128)(2,1)S(1)} %get-tuple-element.32), channel_id=1, source_target_pairs={{0,16},{1,17},{2,18},{3,19},{4,20},{5,21},{6,22},{7,23},{8,24},{9,... | collective-permute-start | bytes 1474568 | tf_op jit(solution)/shard_map/ppermute | solution.py:368
  17.0 3.6 %collective-permute-start.9 = (bf16[128,384]{1,0:T(8,128)(2,1)S(1)}, bf16[128,384]{1,0:T(8,128)(2,1)S(1)}, u32[]{:S(2)}, u32[]{:S(2)}) collective-permute-start(bf16[128,384]{1,0:T(8,128)(2,1)S(1)} %copy-done.1), channel_id=1, source_target_pairs={{0,6},{1,7},{2,0},{3,1},{4,2},{5,3},{6,4},{7,5},{8,14},{9,15},{10,... | collective-permute-start | bytes 294920 | tf_op jit(solution)/shard_map/ppermute | solution.py:371
  20.6 1.0 %collective-permute-start.7 = (bf16[128,384]{1,0:T(8,128)(2,1)S(1)}, bf16[128,384]{1,0:T(8,128)(2,1)S(1)}, u32[]{:S(2)}, u32[]{:S(2)}) collective-permute-start(bf16[128,384]{1,0:T(8,128)(2,1)S(1)} %copy-done.1), channel_id=1, source_target_pairs={{0,2},{1,3},{2,4},{3,5},{4,6},{5,7},{6,0},{7,1},{8,10},{9,11},{10,... | collective-permute-start | bytes 294920 | tf_op jit(solution)/shard_map/ppermute | solution.py:371
  21.6 2.1 %collective-permute-done.9.refs_2_ = bf16[128,384]{1,0:T(8,128)(2,1)S(1)} collective-permute-done((bf16[128,384]{1,0:T(8,128)(2,1)S(1)}, bf16[128,384]{1,0:T(8,128)(2,1)S(1)}, u32[]{:S(2)}, u32[]{:S(2)}) %collective-permute-start.9) | collective-permute-done | bytes 98336 | tf_op jit(solution)/shard_map/ppermute | solution.py:371
  23.7 0.5 collective-permute-start.4
  24.2 4.6 %collective-permute-done.8.refs_1_ = bf16[128,384]{1,0:T(8,128)(2,1)S(1)} collective-permute-done((bf16[128,384]{1,0:T(8,128)(2,1)S(1)}, bf16[128,384]{1,0:T(8,128)(2,1)S(1)}, u32[]{:S(2)}, u32[]{:S(2)}) %collective-permute-start.8) | collective-permute-done | bytes 98336 | tf_op jit(solution)/shard_map/ppermute | solution.py:371
  28.8 0.8 %collective-permute-done.4._.refs_7_ = bf16[128,384]{1,0:T(8,128)(2,1)S(1)} collective-permute-done((bf16[128,384]{1,0:T(8,128)(2,1)S(1)}, bf16[128,384]{1,0:T(8,128)(2,1)S(1)}, u32[]{:S(2)}, u32[]{:S(2)}) %collective-permute-start.4) | collective-permute-done | bytes 98336 | tf_op jit(solution)/shard_map/ppermute | solution.py:368
  29.9 1.6 %collective-permute-start.21 = (bf16[2,128,384]{2,1,0:T(8,128)(2,1)S(1)}, bf16[2,128,384]{2,1,0:T(8,128)(2,1)S(1)}, u32[]{:S(2)}, u32[]{:S(2)}) collective-permute-start(bf16[2,128,384]{2,1,0:T(8,128)(2,1)S(1)} %get-tuple-element.37), channel_id=1, source_target_pairs={{0,16},{1,17},{2,18},{3,19},{4,20},{5,21},{6,22},{7,23},{8,24},{9,... | collective-permute-start | bytes 589832 | tf_op jit(solution)/shard_map/ppermute | solution.py:368
  31.5 0.5 collective-permute-start.22
  32.1 3.6 %collective-permute-start.14 = (bf16[128,384]{1,0:T(8,128)(2,1)S(1)}, bf16[128,384]{1,0:T(8,128)(2,1)S(1)}, u32[]{:S(2)}, u32[]{:S(2)}) collective-permute-start(bf16[128,384]{1,0:T(8,128)(2,1)S(1)} %collective-permute-done.4._.refs_7_), channel_id=1, source_target_pairs={{0,6},{1,7},{2,0},{3,1},{4,2},{5,3},{6,4},{7,5},{8,14},{9,15},{10,... | collective-permute-start | bytes 294920 | tf_op jit(solution)/shard_map/ppermute | solution.py:371
  35.7 0.9 %collective-permute-start.13 = (bf16[128,384]{1,0:T(8,128)(2,1)S(1)}, bf16[128,384]{1,0:T(8,128)(2,1)S(1)}, u32[]{:S(2)}, u32[]{:S(2)}) collective-permute-start(bf16[128,384]{1,0:T(8,128)(2,1)S(1)} %collective-permute-done.4._.refs_7_), channel_id=1, source_target_pairs={{0,4},{1,5},{2,6},{3,7},{4,0},{5,1},{6,2},{7,3},{8,12},{9,13},{10,... | collective-permute-start | bytes 294920 | tf_op jit(solution)/shard_map/ppermute | solution.py:371
  36.7 1.4 %collective-permute-start.11 = (bf16[3,128,384]{2,1,0:T(8,128)(2,1)S(1)}, bf16[3,128,384]{2,1,0:T(8,128)(2,1)S(1)}, u32[]{:S(2)}, u32[]{:S(2)}) collective-permute-start(bf16[3,128,384]{2,1,0:T(8,128)(2,1)S(1)} %get-tuple-element.34.refs_9_), channel_id=1, source_target_pairs={{0,16},{1,17},{2,18},{3,19},{4,20},{5,21},{6,22},{7,23},{8,24},{9,... | collective-permute-start | bytes 884744 | tf_op jit(solution)/shard_map/ppermute | solution.py:368
  38.1 2.0 %collective-permute-start.10 = (bf16[3,128,384]{2,1,0:T(8,128)(2,1)S(1)}, bf16[3,128,384]{2,1,0:T(8,128)(2,1)S(1)}, u32[]{:S(2)}, u32[]{:S(2)}) collective-permute-start(bf16[3,128,384]{2,1,0:T(8,128)(2,1)S(1)} %get-tuple-element.34.refs_9_), channel_id=1, source_target_pairs={{0,1},{1,0},{2,3},{3,2},{4,5},{5,4},{6,7},{7,6},{8,9},{9,8},{10,11... | collective-permute-start | bytes 884744 | tf_op jit(solution)/shard_map/ppermute | solution.py:368
  40.3 2.3 %collective-permute-start.23 = (bf16[128,384]{1,0:T(8,128)(2,1)S(1)}, bf16[128,384]{1,0:T(8,128)(2,1)S(1)}, u32[]{:S(2)}, u32[]{:S(2)}) collective-permute-start(bf16[128,384]{1,0:T(8,128)(2,1)S(1)} %get-tuple-element.39), channel_id=1, source_target_pairs={{0,2},{1,3},{2,4},{3,5},{4,6},{5,7},{6,0},{7,1},{8,10},{9,11},{10,... | collective-permute-start | bytes 294920 | tf_op jit(solution)/shard_map/ppermute | solution.py:371
  42.6 1.0 %collective-permute-done.13.refs_1_ = bf16[128,384]{1,0:T(8,128)(2,1)S(1)} collective-permute-done((bf16[128,384]{1,0:T(8,128)(2,1)S(1)}, bf16[128,384]{1,0:T(8,128)(2,1)S(1)}, u32[]{:S(2)}, u32[]{:S(2)}) %collective-permute-start.13) | collective-permute-done | bytes 98336 | tf_op jit(solution)/shard_map/ppermute | solution.py:371
  43.6 0.5 collective-permute-start
  44.1 2.7 %collective-permute-done.23.refs_0_ = bf16[128,384]{1,0:T(8,128)(2,1)S(1)} collective-permute-done((bf16[128,384]{1,0:T(8,128)(2,1)S(1)}, bf16[128,384]{1,0:T(8,128)(2,1)S(1)}, u32[]{:S(2)}, u32[]{:S(2)}) %collective-permute-start.23) | collective-permute-done | bytes 98336 | tf_op jit(solution)/shard_map/ppermute | solution.py:371
  46.8 0.6 collective-permute-start.16
  47.4 0.5 collective-permute-done.2.refs_5_
  49.1 1.9 %collective-permute-done.17.refs_15_ = bf16[2,128,384]{2,1,0:T(8,128)(2,1)S(1)} collective-permute-done((bf16[2,128,384]{2,1,0:T(8,128)(2,1)S(1)}, bf16[2,128,384]{2,1,0:T(8,128)(2,1)S(1)}, u32[]{:S(2)}, u32[]{:S(2)}) %collective-permute-start.17) | collective-permute-done | bytes 196640 | tf_op jit(solution)/shard_map/ppermute | solution.py:368
  51.2 2.7 %collective-permute-start.26 = (bf16[128,384]{1,0:T(8,128)(2,1)S(1)}, bf16[128,384]{1,0:T(8,128)(2,1)S(1)}, u32[]{:S(2)}, u32[]{:S(2)}) collective-permute-start(bf16[128,384]{1,0:T(8,128)(2,1)S(1)} %get-tuple-element.44), channel_id=1, source_target_pairs={{0,6},{1,7},{2,0},{3,1},{4,2},{5,3},{6,4},{7,5},{8,14},{9,15},{10,... | collective-permute-start | bytes 294920 | tf_op jit(solution)/shard_map/ppermute | solution.py:371
  53.9 6.2 %backward_rows.1 = (bf16[1,256,1024]{2,1,0:T(8,128)(2,1)}, bf16[1,1024,3072]{2,1,0:T(8,128)(2,1)}, f32[8,128]{1,0:T(8,128)S(1)}) custom-call(bf16[1,256,1024]{2,1,0:T(8,128)(2,1)S(1)} %copy-done, bf16[1,1024,3072]{2,1,0:T(8,128)(2,1)S(1)} %bitcast.3, f32[4,128]{1,0:T(4,128)S(1)} %get-tuple-element.25.own_ref.refs_2_, ...), custom_call_target="tpu_custom_call" | custom-call | flops 3000000000 | tf_op jit(solution)/shard_map/backward_rows/pallas_call | solution.py:312
  60.2 0.7 %last_sum.1 = bf16[128,384]{1,0:T(8,128)(2,1)} custom-call(f32[8,128]{1,0:T(8,128)S(1)} %get-tuple-element.41._, f32[128,384]{1,0:T(8,128)S(1)} %get-tuple-element.42.first_ref, bf16[128,384]{1,0:T(8,128)(2,1)S(1)} %collective-permute-done.23.refs_0_, bf16[128,384]{1,0:T(8,128)(2,1)S(1)} %collective-permute-done.25.refs_1_, ...), custom_call_target="tpu_custom_call" | custom-call | flops 1000000000 | tf_op jit(solution)/shard_map/last_sum/pallas_call | solution.py:346
  (42 shorter events, 2.1 us)
Async XLA Ops:
  0.6 1.0 %copy-start = (bf16[1,256,1024]{2,1,0:T(8,128)(2,1)S(1)}, bf16[1,256,1024]{2,1,0:T(8,128)(2,1)}, u32[]{:S(2)}) copy-start(bf16[1,256,1024]{2,1,0:T(8,128)(2,1)} %refs_0_.1) | copy-start | bytes 1572868
  1.7 0.7 %copy-start.2 = (s32[128,2]{0,1:T(2,128)S(1)}, s32[128,2]{0,1:T(2,128)}, u32[]{:S(2)}) copy-start(s32[128,2]{0,1:T(2,128)} %param.7) | copy-start | bytes 3076
  3.0 8.8 %copy-start.1 = (bf16[128,384]{1,0:T(8,128)(2,1)S(1)}, bf16[128,384]{1,0:T(8,128)(2,1)}, u32[]{:S(2)}) copy-start(bf16[128,384]{1,0:T(8,128)(2,1)} %refs_6_.1) | copy-start | bytes 294916
  7.1 4.7 %collective-permute-start.3 = (bf16[4,2,2,64,384]{4,3,2,1,0:T(8,128)(2,1)S(1)}, bf16[4,2,2,64,384]{4,3,2,1,0:T(8,128)(2,1)S(1)}, u32[]{:S(2)}, u32[]{:S(2)}) collective-permute-start(bf16[4,2,2,64,384]{4,3,2,1,0:T(8,128)(2,1)S(1)} %get-tuple-element.27), channel_id=1, source_target_pairs={{0,8},{1,9},{2,10},{3,11},{4,12},{5,13},{6,14},{7,15},{8,0},{9,1},... | collective-permute-start | bytes 2359304 | tf_op jit(solution)/shard_map/ppermute | solution.py:368
  7.6 4.2 %collective-permute-start.1 = (f32[4,128]{1,0:T(4,128)S(1)}, f32[4,128]{1,0:T(4,128)S(1)}, u32[]{:S(2)}, u32[]{:S(2)}) collective-permute-start(f32[4,128]{1,0:T(4,128)S(1)} %get-tuple-element.25.own_ref.refs_2_), channel_id=1, source_target_pairs={{0,16},{1,17},{2,18},{3,19},{4,20},{5,21},{6,22},{7,23},{8,24},{9,... | collective-permute-start | bytes 6152 | tf_op jit(solution)/shard_map/ppermute | solution.py:368
  13.4 16.2 %collective-permute-start.5 = (bf16[5,128,384]{2,1,0:T(8,128)(2,1)S(1)}, bf16[5,128,384]{2,1,0:T(8,128)(2,1)S(1)}, u32[]{:S(2)}, u32[]{:S(2)}) collective-permute-start(bf16[5,128,384]{2,1,0:T(8,128)(2,1)S(1)} %get-tuple-element.30), channel_id=1, source_target_pairs={{0,1},{1,0},{2,3},{3,2},{4,5},{5,4},{6,7},{7,6},{8,9},{9,8},{10,11... | collective-permute-start | bytes 1474568 | tf_op jit(solution)/shard_map/ppermute | solution.py:368
  15.5 14.2 %collective-permute-start.6 = (bf16[5,128,384]{2,1,0:T(8,128)(2,1)S(1)}, bf16[5,128,384]{2,1,0:T(8,128)(2,1)S(1)}, u32[]{:S(2)}, u32[]{:S(2)}) collective-permute-start(bf16[5,128,384]{2,1,0:T(8,128)(2,1)S(1)} %get-tuple-element.32), channel_id=1, source_target_pairs={{0,16},{1,17},{2,18},{3,19},{4,20},{5,21},{6,22},{7,23},{8,24},{9,... | collective-permute-start | bytes 1474568 | tf_op jit(solution)/shard_map/ppermute | solution.py:368
  17.0 6.7 %collective-permute-start.9 = (bf16[128,384]{1,0:T(8,128)(2,1)S(1)}, bf16[128,384]{1,0:T(8,128)(2,1)S(1)}, u32[]{:S(2)}, u32[]{:S(2)}) collective-permute-start(bf16[128,384]{1,0:T(8,128)(2,1)S(1)} %copy-done.1), channel_id=1, source_target_pairs={{0,6},{1,7},{2,0},{3,1},{4,2},{5,3},{6,4},{7,5},{8,14},{9,15},{10,... | collective-permute-start | bytes 294920 | tf_op jit(solution)/shard_map/ppermute | solution.py:371
  20.6 8.2 %collective-permute-start.8 = (bf16[128,384]{1,0:T(8,128)(2,1)S(1)}, bf16[128,384]{1,0:T(8,128)(2,1)S(1)}, u32[]{:S(2)}, u32[]{:S(2)}) collective-permute-start(bf16[128,384]{1,0:T(8,128)(2,1)S(1)} %copy-done.1), channel_id=1, source_target_pairs={{0,4},{1,5},{2,6},{3,7},{4,0},{5,1},{6,2},{7,3},{8,12},{9,13},{10,... | collective-permute-start | bytes 294920 | tf_op jit(solution)/shard_map/ppermute | solution.py:371
  20.6 8.2 %collective-permute-start.7 = (bf16[128,384]{1,0:T(8,128)(2,1)S(1)}, bf16[128,384]{1,0:T(8,128)(2,1)S(1)}, u32[]{:S(2)}, u32[]{:S(2)}) collective-permute-start(bf16[128,384]{1,0:T(8,128)(2,1)S(1)} %copy-done.1), channel_id=1, source_target_pairs={{0,2},{1,3},{2,4},{3,5},{4,6},{5,7},{6,0},{7,1},{8,10},{9,11},{10,... | collective-permute-start | bytes 294920 | tf_op jit(solution)/shard_map/ppermute | solution.py:371
  23.7 5.9 %collective-permute-start.4 = (bf16[128,384]{1,0:T(8,128)(2,1)S(1)}, bf16[128,384]{1,0:T(8,128)(2,1)S(1)}, u32[]{:S(2)}, u32[]{:S(2)}) collective-permute-start(bf16[128,384]{1,0:T(8,128)(2,1)S(1)} %copy-done.1), channel_id=1, source_target_pairs={{0,17},{1,16},{2,19},{3,18},{4,21},{5,20},{6,23},{7,22},{8,25},{9,... | collective-permute-start | bytes 294920 | tf_op jit(solution)/shard_map/ppermute | solution.py:368
  29.7 24.2 %slice-start = ((s8[6291456]{0:T(1024)(128)(4,1)}), s8[4194304]{0:T(1024)(128)(4,1)S(1)}, s32[]{:S(2)}) async-start(s8[6291456]{0:T(1024)(128)(4,1)} %bitcast.2), calls=%async_computation | async-start | bytes 8388608
  29.9 6.7 %collective-permute-start.21 = (bf16[2,128,384]{2,1,0:T(8,128)(2,1)S(1)}, bf16[2,128,384]{2,1,0:T(8,128)(2,1)S(1)}, u32[]{:S(2)}, u32[]{:S(2)}) collective-permute-start(bf16[2,128,384]{2,1,0:T(8,128)(2,1)S(1)} %get-tuple-element.37), channel_id=1, source_target_pairs={{0,16},{1,17},{2,18},{3,19},{4,20},{5,21},{6,22},{7,23},{8,24},{9,... | collective-permute-start | bytes 589832 | tf_op jit(solution)/shard_map/ppermute | solution.py:368
  31.5 6.6 %collective-permute-start.22 = (bf16[2,128,384]{2,1,0:T(8,128)(2,1)S(1)}, bf16[2,128,384]{2,1,0:T(8,128)(2,1)S(1)}, u32[]{:S(2)}, u32[]{:S(2)}) collective-permute-start(bf16[2,128,384]{2,1,0:T(8,128)(2,1)S(1)} %get-tuple-element.38), channel_id=1, source_target_pairs={{0,1},{1,0},{2,3},{3,2},{4,5},{5,4},{6,7},{7,6},{8,9},{9,8},{10,11... | collective-permute-start | bytes 589832 | tf_op jit(solution)/shard_map/ppermute | solution.py:368
  32.1 8.2 %collective-permute-start.14 = (bf16[128,384]{1,0:T(8,128)(2,1)S(1)}, bf16[128,384]{1,0:T(8,128)(2,1)S(1)}, u32[]{:S(2)}, u32[]{:S(2)}) collective-permute-start(bf16[128,384]{1,0:T(8,128)(2,1)S(1)} %collective-permute-done.4._.refs_7_), channel_id=1, source_target_pairs={{0,6},{1,7},{2,0},{3,1},{4,2},{5,3},{6,4},{7,5},{8,14},{9,15},{10,... | collective-permute-start | bytes 294920 | tf_op jit(solution)/shard_map/ppermute | solution.py:371
  35.7 7.9 %collective-permute-start.13 = (bf16[128,384]{1,0:T(8,128)(2,1)S(1)}, bf16[128,384]{1,0:T(8,128)(2,1)S(1)}, u32[]{:S(2)}, u32[]{:S(2)}) collective-permute-start(bf16[128,384]{1,0:T(8,128)(2,1)S(1)} %collective-permute-done.4._.refs_7_), channel_id=1, source_target_pairs={{0,4},{1,5},{2,6},{3,7},{4,0},{5,1},{6,2},{7,3},{8,12},{9,13},{10,... | collective-permute-start | bytes 294920 | tf_op jit(solution)/shard_map/ppermute | solution.py:371
  36.6 7.0 %collective-permute-start.12 = (bf16[128,384]{1,0:T(8,128)(2,1)S(1)}, bf16[128,384]{1,0:T(8,128)(2,1)S(1)}, u32[]{:S(2)}, u32[]{:S(2)}) collective-permute-start(bf16[128,384]{1,0:T(8,128)(2,1)S(1)} %collective-permute-done.4._.refs_7_), channel_id=1, source_target_pairs={{0,2},{1,3},{2,4},{3,5},{4,6},{5,7},{6,0},{7,1},{8,10},{9,11},{10,... | collective-permute-start | bytes 294920 | tf_op jit(solution)/shard_map/ppermute | solution.py:371
  36.7 11.8 %collective-permute-start.11 = (bf16[3,128,384]{2,1,0:T(8,128)(2,1)S(1)}, bf16[3,128,384]{2,1,0:T(8,128)(2,1)S(1)}, u32[]{:S(2)}, u32[]{:S(2)}) collective-permute-start(bf16[3,128,384]{2,1,0:T(8,128)(2,1)S(1)} %get-tuple-element.34.refs_9_), channel_id=1, source_target_pairs={{0,16},{1,17},{2,18},{3,19},{4,20},{5,21},{6,22},{7,23},{8,24},{9,... | collective-permute-start | bytes 884744 | tf_op jit(solution)/shard_map/ppermute | solution.py:368
  38.1 10.5 %collective-permute-start.10 = (bf16[3,128,384]{2,1,0:T(8,128)(2,1)S(1)}, bf16[3,128,384]{2,1,0:T(8,128)(2,1)S(1)}, u32[]{:S(2)}, u32[]{:S(2)}) collective-permute-start(bf16[3,128,384]{2,1,0:T(8,128)(2,1)S(1)} %get-tuple-element.34.refs_9_), channel_id=1, source_target_pairs={{0,1},{1,0},{2,3},{3,2},{4,5},{5,4},{6,7},{7,6},{8,9},{9,8},{10,11... | collective-permute-start | bytes 884744 | tf_op jit(solution)/shard_map/ppermute | solution.py:368
  40.1 13.8 %slice-start.1 = ((s8[6291456]{0:T(1024)(128)(4,1)}), s8[2097152]{0:T(1024)(128)(4,1)S(1)}, s32[]{:S(2)}) async-start(s8[6291456]{0:T(1024)(128)(4,1)} %bitcast.2), calls=%async_computation.1 | async-start | bytes 4194304
  40.3 6.5 %collective-permute-start.23 = (bf16[128,384]{1,0:T(8,128)(2,1)S(1)}, bf16[128,384]{1,0:T(8,128)(2,1)S(1)}, u32[]{:S(2)}, u32[]{:S(2)}) collective-permute-start(bf16[128,384]{1,0:T(8,128)(2,1)S(1)} %get-tuple-element.39), channel_id=1, source_target_pairs={{0,2},{1,3},{2,4},{3,5},{4,6},{5,7},{6,0},{7,1},{8,10},{9,11},{10,... | collective-permute-start | bytes 294920 | tf_op jit(solution)/shard_map/ppermute | solution.py:371
  43.6 4.5 %collective-permute-start.15 = (bf16[128,384]{1,0:T(8,128)(2,1)S(1)}, bf16[128,384]{1,0:T(8,128)(2,1)S(1)}, u32[]{:S(2)}, u32[]{:S(2)}) collective-permute-start(bf16[128,384]{1,0:T(8,128)(2,1)S(1)} %copy-done.1), channel_id=1, source_target_pairs={{0,8},{1,9},{2,10},{3,11},{4,12},{5,13},{6,14},{7,15},{8,0},{9,1},... | collective-permute-start | bytes 294920 | tf_op jit(solution)/shard_map/ppermute | solution.py:368
  43.6 3.2 %collective-permute-start = (f32[4,128]{1,0:T(4,128)S(1)}, f32[4,128]{1,0:T(4,128)S(1)}, u32[]{:S(2)}, u32[]{:S(2)}) collective-permute-start(f32[4,128]{1,0:T(4,128)S(1)} %get-tuple-element.25.own_ref.refs_2_), channel_id=1, source_target_pairs={{0,8},{1,9},{2,10},{3,11},{4,12},{5,13},{6,14},{7,15},{8,0},{9,1},... | collective-permute-start | bytes 6152 | tf_op jit(solution)/shard_map/ppermute | solution.py:368
  46.8 1.2 %collective-permute-start.2 = (f32[4,128]{1,0:T(4,128)S(1)}, f32[4,128]{1,0:T(4,128)S(1)}, u32[]{:S(2)}, u32[]{:S(2)}) collective-permute-start(f32[4,128]{1,0:T(4,128)S(1)} %collective-permute-done.1.near_ref.refs_4_), channel_id=1, source_target_pairs={{0,8},{1,9},{2,10},{3,11},{4,12},{5,13},{6,14},{7,15},{8,0},{9,1},... | collective-permute-start | bytes 6152 | tf_op jit(solution)/shard_map/ppermute | solution.py:368
  46.8 2.1 %collective-permute-start.16 = (bf16[128,384]{1,0:T(8,128)(2,1)S(1)}, bf16[128,384]{1,0:T(8,128)(2,1)S(1)}, u32[]{:S(2)}, u32[]{:S(2)}) collective-permute-start(bf16[128,384]{1,0:T(8,128)(2,1)S(1)} %collective-permute-done.4._.refs_7_), channel_id=1, source_target_pairs={{0,8},{1,9},{2,10},{3,11},{4,12},{5,13},{6,14},{7,15},{8,0},{9,1},... | collective-permute-start | bytes 294920 | tf_op jit(solution)/shard_map/ppermute | solution.py:368
  47.9 3.3 %collective-permute-start.18 = (bf16[3,128,384]{2,1,0:T(8,128)(2,1)S(1)}, bf16[3,128,384]{2,1,0:T(8,128)(2,1)S(1)}, u32[]{:S(2)}, u32[]{:S(2)}) collective-permute-start(bf16[3,128,384]{2,1,0:T(8,128)(2,1)S(1)} %get-tuple-element.34.refs_9_), channel_id=1, source_target_pairs={{0,8},{1,9},{2,10},{3,11},{4,12},{5,13},{6,14},{7,15},{8,0},{9,1},... | collective-permute-start | bytes 884744 | tf_op jit(solution)/shard_map/ppermute | solution.py:368
  48.1 5.8 %collective-permute-start.24 = (bf16[3,128,384]{2,1,0:T(8,128)(2,1)S(1)}, bf16[3,128,384]{2,1,0:T(8,128)(2,1)S(1)}, u32[]{:S(2)}, u32[]{:S(2)}) collective-permute-start(bf16[3,128,384]{2,1,0:T(8,128)(2,1)S(1)} %stack_blocks.1.refs_12_), channel_id=1, source_target_pairs={{0,8},{1,9},{2,10},{3,11},{4,12},{5,13},{6,14},{7,15},{8,0},{9,1},... | collective-permute-start | bytes 884744 | tf_op jit(solution)/shard_map/ppermute | solution.py:368
  48.4 5.5 %collective-permute-start.20 = (bf16[3,128,384]{2,1,0:T(8,128)(2,1)S(1)}, bf16[3,128,384]{2,1,0:T(8,128)(2,1)S(1)}, u32[]{:S(2)}, u32[]{:S(2)}) collective-permute-start(bf16[3,128,384]{2,1,0:T(8,128)(2,1)S(1)} %collective-permute-done.11.refs_11_), channel_id=1, source_target_pairs={{0,8},{1,9},{2,10},{3,11},{4,12},{5,13},{6,14},{7,15},{8,0},{9,1},... | collective-permute-start | bytes 884744 | tf_op jit(solution)/shard_map/ppermute | solution.py:368
  48.6 5.3 %collective-permute-start.19 = (bf16[3,128,384]{2,1,0:T(8,128)(2,1)S(1)}, bf16[3,128,384]{2,1,0:T(8,128)(2,1)S(1)}, u32[]{:S(2)}, u32[]{:S(2)}) collective-permute-start(bf16[3,128,384]{2,1,0:T(8,128)(2,1)S(1)} %collective-permute-done.10.refs_10_), channel_id=1, source_target_pairs={{0,8},{1,9},{2,10},{3,11},{4,12},{5,13},{6,14},{7,15},{8,0},{9,1},... | collective-permute-start | bytes 884744 | tf_op jit(solution)/shard_map/ppermute | solution.py:368
  49.0 2.1 %collective-permute-start.17 = (bf16[2,128,384]{2,1,0:T(8,128)(2,1)S(1)}, bf16[2,128,384]{2,1,0:T(8,128)(2,1)S(1)}, u32[]{:S(2)}, u32[]{:S(2)}) collective-permute-start(bf16[2,128,384]{2,1,0:T(8,128)(2,1)S(1)} %get-tuple-element.33.refs_8_), channel_id=1, source_target_pairs={{0,8},{1,9},{2,10},{3,11},{4,12},{5,13},{6,14},{7,15},{8,0},{9,1},... | collective-permute-start | bytes 589832 | tf_op jit(solution)/shard_map/ppermute | solution.py:368
  51.0 9.1 %collective-permute-start.25 = (bf16[128,384]{1,0:T(8,128)(2,1)S(1)}, bf16[128,384]{1,0:T(8,128)(2,1)S(1)}, u32[]{:S(2)}, u32[]{:S(2)}) collective-permute-start(bf16[128,384]{1,0:T(8,128)(2,1)S(1)} %get-tuple-element.43), channel_id=1, source_target_pairs={{0,4},{1,5},{2,6},{3,7},{4,0},{5,1},{6,2},{7,3},{8,12},{9,13},{10,... | collective-permute-start | bytes 294920 | tf_op jit(solution)/shard_map/ppermute | solution.py:371
  51.2 9.0 %collective-permute-start.26 = (bf16[128,384]{1,0:T(8,128)(2,1)S(1)}, bf16[128,384]{1,0:T(8,128)(2,1)S(1)}, u32[]{:S(2)}, u32[]{:S(2)}) collective-permute-start(bf16[128,384]{1,0:T(8,128)(2,1)S(1)} %get-tuple-element.44), channel_id=1, source_target_pairs={{0,6},{1,7},{2,0},{3,1},{4,2},{5,3},{6,4},{7,5},{8,14},{9,15},{10,... | collective-permute-start | bytes 294920 | tf_op jit(solution)/shard_map/ppermute | solution.py:371
  (1 other events, 0.7 us)

commit v4 on v3

v4 whole, which is shorter than its diff:
```python
import functools

import jax
import jax.numpy as jnp
from jax import lax
from jax.experimental import pallas as pl
from jax.experimental.pallas import tpu as pltpu
from jax.sharding import PartitionSpec as P

BF, F32 = jnp.bfloat16, jnp.float32


def routed(hidden, down_weight, expert_ids, combine, out_grad):
    dp_count = lax.axis_size("dp")
    tok_rows = expert_ids.shape[0]
    capacity = 2 * tok_rows // dp_count
    slot_count = dp_count * capacity
    feat_share = out_grad.shape[1]
    width = down_weight.shape[2]
    flat_ids = expert_ids.reshape(-1)
    labels = jnp.arange(dp_count, dtype=jnp.int32)
    onehot = (flat_ids[:, None] == labels[None, :]).astype(jnp.int32)
    pair_rank = jnp.sum((jnp.cumsum(onehot, axis=0) - 1) * onehot, axis=1)
    inside = flat_ids < dp_count
    target = jnp.where(inside, flat_ids * capacity + pair_rank, dp_count * capacity)
    weights = combine.reshape(-1)
    full_grad = lax.all_gather(out_grad, "cuts", axis=1, tiled=True)
    scaled = (weights[:, None] * jnp.repeat(full_grad, 2, axis=0).astype(F32)).astype(BF)
    outgoing = jnp.zeros((dp_count * capacity, width), BF).at[target].set(scaled, mode="drop")
    incoming = lax.all_to_all(
        outgoing.reshape(dp_count, capacity, width), "dp", split_axis=0, concat_axis=0, tiled=True
    )
    grad_rows = incoming.reshape(slot_count, width)
    hidden_rows = hidden[0]
    weight = down_weight[0]
    own_share = lax.psum_scatter(
        lax.dot_general(weight, hidden_rows, (((0,), (1,)), ((), ())), preferred_element_type=F32),
        "cuts",
        scatter_dimension=0,
        tiled=True,
    )
    hid_grad = lax.dot_general(
        grad_rows, weight, (((1,), (1,)), ((), ())), preferred_element_type=F32
    ).astype(BF)
    down_grad = lax.dot_general(
        hidden_rows, grad_rows, (((0,), (0,)), ((), ())), preferred_element_type=F32
    ).astype(BF)
    returned = lax.all_to_all(
        own_share.astype(BF), "dp", split_axis=1, concat_axis=1, tiled=True
    )
    pick_index = jnp.minimum(target, dp_count * capacity - 1)
    picked = jnp.take(returned, pick_index, axis=1).astype(F32)
    pair_coef = jnp.where(inside, weights, jnp.zeros_like(weights))
    summed = jnp.sum((picked * pair_coef[None, :]).reshape(feat_share, tok_rows, 2), axis=2)
    mixed = summed.T.astype(BF)
    return (mixed, hid_grad[None], down_grad[None])


def routing(meta, expert, capacity):
    tok = meta.shape[1]
    label = jnp.full((1, tok), expert).astype(F32)
    first, second = meta[0:1] == label, meta[1:2] == label
    named = jnp.where(first, 1.0, jnp.where(second, 1.0, 0.0))
    weight = jnp.where(first, meta[2:3], jnp.where(second, meta[3:4], 0.0))
    earlier = lax.broadcasted_iota(jnp.int32, (tok, tok), 0) < lax.broadcasted_iota(
        jnp.int32, (tok, tok), 1
    )
    rank = jnp.dot(
        jnp.broadcast_to(named, (8, tok)).astype(BF),
        jnp.where(earlier, 1.0, 0.0).astype(BF),
        preferred_element_type=F32,
    )[0:1]
    slot = lax.broadcasted_iota(jnp.int32, (capacity, tok), 0).astype(F32)
    hot = jnp.where(slot == rank, named, 0.0)
    return hot, weight


def forward_kernel(nz, capacity, hidden_ref, weight_ref, keep_ref, send_ref, *scratch):
    held, wide, part, rows, sems = scratch
    me = lax.axis_index("dp")
    feat = keep_ref.shape[-1]
    ff = wide.shape[0]
    mid = ff // 2
    first = pltpu.make_async_copy(hidden_ref.at[0], held, sems.at[0])
    low = pltpu.make_async_copy(weight_ref.at[0, pl.ds(0, mid)], wide.at[pl.ds(0, mid)], sems.at[1])
    high = pltpu.make_async_copy(weight_ref.at[0, pl.ds(mid, mid)], wide.at[pl.ds(mid, mid)], sems.at[2])
    for copy in (first, low, high):
        copy.start()
    first.wait()
    low.wait()
    for z in range(nz):
        columns = slice(2 * z * feat, 2 * (z + 1) * feat)
        part[z] = jnp.dot(held[:, :mid], wide[:mid, columns], preferred_element_type=F32)
    high.wait()
    for z in range(nz):
        columns = slice(2 * z * feat, 2 * (z + 1) * feat)
        rest = jnp.dot(held[:, mid:], wide[mid:, columns], preferred_element_type=F32)
        rows[...] = (part[z] + rest).astype(BF)
        for dy in range(2):
            for dc, out in ((0, keep_ref), (1, send_ref)):
                at = pl.multiple_of((me ^ (2 * dy + dc)) * capacity, capacity)
                for x in range(2):
                    out[z, x, dy] = rows[pl.ds(at, capacity), x * feat : (x + 1) * feat]


def forward(hidden, weight, feat, dp_count):
    _, slots, ff = hidden.shape
    width = weight.shape[2]
    nz, capacity = width // (2 * feat), slots // dp_count
    part = jax.ShapeDtypeStruct((nz, 2, 2, capacity, feat), BF)
    hbm, vmem = pl.BlockSpec(memory_space=pltpu.HBM), pl.BlockSpec(memory_space=pltpu.VMEM)
    return pl.pallas_call(
        functools.partial(forward_kernel, nz, capacity),
        in_specs=[hbm] * 2,
        out_specs=[vmem] * 2,
        out_shape=[part, part],
        scratch_shapes=[
            pltpu.VMEM((slots, ff), BF),
            pltpu.VMEM((ff, width), BF),
            pltpu.VMEM((nz, slots, 2 * feat), F32),
            pltpu.VMEM((slots, 2 * feat), BF),
            pltpu.SemaphoreType.DMA((3,)),
        ],
        compiler_params=pltpu.CompilerParams(vmem_limit_bytes=50 << 20),
        cost_estimate=pl.CostEstimate(
            flops=2 * slots * ff * width, bytes_accessed=2 * (ff * width + slots * (ff + width)), transcendentals=0
        ),
        name="forward_rows",
    )(hidden, weight)


def by_token(meta, experts, capacity):
    tok = meta.shape[1]
    table = []
    for expert in experts:
        hot, weight = routing(meta, expert, capacity)
        table.append((hot.astype(BF), jnp.broadcast_to(weight, (tok, tok)).T[:, 0:1]))

    def add_up(first, second):
        terms = [
            lax.dot_general(hot, rows, (((0,), (0,)), ((), ())), preferred_element_type=F32) * weight
            for (hot, weight), rows in zip(table, (first, second))
        ]
        return terms[0] + terms[1]

    return add_up


def spread_kernel(nz, capacity, meta_ref, keep_ref, got_ref, grad_ref, to_x, by_x, to_y, by_y):
    me, x = lax.axis_index("dp"), lax.axis_index("cuts") % 2
    half = nz // 2
    to_x[nz] = grad_ref[...]
    to_y[nz] = grad_ref[...]
    add_up = by_token(meta_ref[...], (me, me ^ 1), capacity)
    for z in range(half):
        to_x[z] = add_up(keep_ref[z, x ^ 1, 0], got_ref[z, x ^ 1, 0]).astype(BF)
        by_x[z] = add_up(keep_ref[z, x, 0], got_ref[z, x, 0])
        to_x[half + z, :capacity] = keep_ref[z, x ^ 1, 1]
        to_x[half + z, capacity:] = got_ref[z, x ^ 1, 1]
        by_x[half + z, :capacity] = keep_ref[z, x, 1].astype(F32)
        by_x[half + z, capacity:] = got_ref[z, x, 1].astype(F32)
        for dx in range(2):
            by_y[half * dx + z] = add_up(keep_ref[half + z, x ^ dx, 0], got_ref[half + z, x ^ dx, 0])
            to_y[half * dx + z, :capacity] = keep_ref[half + z, x ^ dx, 1]
            to_y[half * dx + z, capacity:] = got_ref[half + z, x ^ dx, 1]


def spread(meta, keep, got, grad):
    nz, _, _, capacity, _ = keep.shape
    tok, feat = grad.shape
    shapes = [jax.ShapeDtypeStruct((nz + 1, tok, feat), BF), jax.ShapeDtypeStruct((nz, tok, feat), F32)] * 2
    return pl.pallas_call(
        functools.partial(spread_kernel, nz, capacity),
        out_shape=shapes,
        compiler_params=pltpu.CompilerParams(vmem_limit_bytes=24 << 20),
        cost_estimate=pl.CostEstimate(
            flops=16 * tok * capacity * nz * feat, bytes_accessed=24 * tok * nz * feat, transcendentals=0
        ),
        name="spread_rows",
    )(meta, keep, got, grad)


def first_sum_kernel(half, grad_ref, cross_ref, meta_ref, x_kept, x_got, y_kept, y_got, *refs):
    far, (x_keep, x_send, y_keep, y_send, near_by, stacked) = refs[:-6], refs[-6:]
    me, capacity = lax.axis_index("dp"), x_kept.shape[1] // 2
    for k, ref in enumerate(far):
        stacked[k] = ref[...]
    for i, rows in enumerate((grad_ref[...], x_got[2 * half], y_got[2 * half], cross_ref[...])):
        near_by[i] = rows
    add_up = by_token(meta_ref[...], (me ^ 2, me ^ 3), capacity)
    for z in range(half):
        x_keep[z] = x_kept[z] + x_got[z].astype(F32)
        x_send[z] = (x_kept[half + z] + x_got[half + z].astype(F32)).astype(BF)
        y_keep[z] = y_kept[z] + add_up(y_got[z, :capacity], y_got[z, capacity:])
        y_send[z] = (y_kept[half + z] + add_up(y_got[half + z, :capacity], y_got[half + z, capacity:])).astype(BF)


def first_sum(grad, cross, meta, x_kept, x_got, y_kept, y_got, far):
    nz, tok, feat = x_kept.shape
    half = nz // 2
    shapes = [
        jax.ShapeDtypeStruct((half, tok, feat), F32),
        jax.ShapeDtypeStruct((half, tok, feat), BF),
    ]
    return pl.pallas_call(
        functools.partial(first_sum_kernel, half),
        out_shape=shapes
        + shapes
        + [
            jax.ShapeDtypeStruct((4, tok, feat), BF),
            jax.ShapeDtypeStruct((len(far), tok, feat), BF),
        ],
        compiler_params=pltpu.CompilerParams(vmem_limit_bytes=16 << 20),
        cost_estimate=pl.CostEstimate(flops=1000_000_000, bytes_accessed=0, transcendentals=0),
        name="first_sum",
    )(grad, cross, meta, x_kept, x_got, y_kept, y_got, *far)


def second_sum_kernel(nz, meta_ref, x_kept, y_kept, by_y, by_x, *refs):
    outs, total = refs[:nz], refs[nz]
    me, z, half = lax.axis_index("dp"), lax.axis_index("cuts") // 2, nz // 2
    capacity = by_y.shape[1] // 2
    add_up = by_token(meta_ref[...], (me ^ 2, me ^ 3), capacity)
    for i in range(half):
        total[i] = x_kept[i] + add_up(by_y[i, :capacity], by_y[i, capacity:])
        total[half + i] = y_kept[i] + by_x[i].astype(F32)
    for k in range(nz):
        outs[k][...] = total[lax.rem(z + k, nz)].astype(outs[k].dtype)


def second_sum(meta, x_kept, y_kept, by_y, by_x):
    half, tok, feat = x_kept.shape
    nz = 2 * half
    return pl.pallas_call(
        functools.partial(second_sum_kernel, nz),
        out_shape=[jax.ShapeDtypeStruct((tok, feat), F32 if k == 0 else BF) for k in range(nz)],
        scratch_shapes=[pltpu.VMEM((nz, tok, feat), F32)],
        compiler_params=pltpu.CompilerParams(vmem_limit_bytes=16 << 20),
        cost_estimate=pl.CostEstimate(flops=5000_000_000, bytes_accessed=0, transcendentals=0),
        name="second_sum",
    )(meta, x_kept, y_kept, by_y, by_x)


def stack_kernel(_, meta_ref, near_ref, *refs):
    refs, (stacked, metas) = refs[:-2], refs[-2:]
    for k, ref in enumerate(refs):
        stacked[k] = ref[...]
    metas[0] = meta_ref[...]
    metas[1] = near_ref[...]


def stack(parts, meta, near, after):
    vmem = pl.BlockSpec(memory_space=pltpu.VMEM)
    return pl.pallas_call(
        stack_kernel,
        in_specs=[pl.BlockSpec(memory_space=pl.ANY)] + [vmem] * (2 + len(parts)),
        out_specs=[vmem] * 2,
        out_shape=[
            jax.ShapeDtypeStruct((len(parts), *parts[0].shape), BF),
            jax.ShapeDtypeStruct((2, *meta.shape), F32),
        ],
        compiler_params=pltpu.CompilerParams(vmem_limit_bytes=16 << 20),
        cost_estimate=pl.CostEstimate(flops=1000_000_000, bytes_accessed=0, transcendentals=0),
        name="stack_blocks",
    )(after, meta, near, *parts)


def backward_kernel(nz, capacity, hidden_ref, weight_ref, metas, other_metas, *refs):
    grads, refs = (refs[:5], refs[5:10]), refs[10:]
    hid_out, down_out, mark, made, rows_ref, turned, total, done, hots, cols, sems = refs[-11:]
    mark[...] = jnp.zeros_like(mark)
    me, x, z = lax.axis_index("dp"), lax.axis_index("cuts") % 2, lax.axis_index("cuts") // 2
    feat = rows_ref.shape[1] // 2

    for dy in range(2):
        for dc, ref in enumerate((metas, other_metas)):
            hot, weight = routing(ref[dy], me, capacity)
            hots[2 * dy + dc] = hot.astype(BF)
            cols[2 * dy + dc] = jnp.broadcast_to(jnp.sum(hot * weight, axis=1, keepdims=True), cols.shape[1:])
    turned[...] = hidden_ref[0].T

    def put(dx, q, rows):
        lane = pl.multiple_of((x ^ dx) * feat, feat)
        at = pl.multiple_of((me ^ q) * capacity, capacity)
        picked = jnp.dot(hots[q], rows, preferred_element_type=F32)
        rows_ref[pl.ds(at, capacity), pl.ds(lane, feat)] = (picked * cols[q][:, 0:1]).astype(BF)

    leaving = []
    for k in range(nz):
        for dc in range(2):
            near_by, far, far_x, far_y, far_xy = grads[dc]
            for j, ref in enumerate((far, far_x, far_y, far_xy)):
                put(j % 2, 2 * (j // 2) + dc, near_by[j] if k == 0 else ref[k - 1])
        rows = rows_ref[...]
        column = pl.ds(pl.multiple_of(lax.rem(z - k + nz, nz) * 2 * feat, 2 * feat), 2 * feat)
        part = lax.dot_general(rows, weight_ref[0, :, column], (((1,), (1,)), ((), ())), preferred_element_type=F32)
        if k:
            part = total[...] + part
        if k < nz - 1:
            total[...] = part
        else:
            done[...] = part.astype(BF)
            leaving.append(pltpu.make_async_copy(done, hid_out.at[0], sems.at[2]))
            leaving[-1].start()
        if k >= 2:
            leaving.pop(0).wait()
        made[k % 2] = jnp.dot(turned[...], rows, preferred_element_type=F32).astype(BF)
        leaving.append(pltpu.make_async_copy(made.at[k % 2], down_out.at[0, :, column], sems.at[k % 2]))
        leaving[-1].start()
    for copy in leaving:
        copy.wait()


def backward(hidden, weight, metas, other_metas, grads, after=()):
    tok, feat = grads[1].shape[1:]
    _, slots, ff = hidden.shape
    width = weight.shape[2]
    nz, capacity = width // (2 * feat), slots // 4
    anywhere, vmem = pl.BlockSpec(memory_space=pl.ANY), pl.BlockSpec(memory_space=pltpu.VMEM)
    return pl.pallas_call(
        functools.partial(backward_kernel, nz, capacity),
        in_specs=[vmem] * 14 + [anywhere] * len(after),
        out_specs=[anywhere, anywhere, vmem],
        scratch_shapes=[
            pltpu.VMEM((2, ff, 2 * feat), BF),
            pltpu.VMEM((slots, 2 * feat), BF),
            pltpu.VMEM((ff, slots), BF),
            pltpu.VMEM((slots, ff), F32),
            pltpu.VMEM((slots, ff), BF),
            pltpu.VMEM((4, capacity, tok), BF),
            pltpu.VMEM((4, capacity, 128), F32),
            pltpu.SemaphoreType.DMA((3,)),
        ],
        out_shape=[
            jax.ShapeDtypeStruct(hidden.shape, BF),
            jax.ShapeDtypeStruct(weight.shape, BF),
            jax.ShapeDtypeStruct((8, 128), F32),
        ],
        compiler_params=pltpu.CompilerParams(vmem_limit_bytes=32 << 20),
        cost_estimate=pl.CostEstimate(flops=100_000_000, bytes_accessed=0, transcendentals=0),
        name="backward_rows",
    )(hidden, weight, metas, other_metas, *grads, *after)


def last_sum_kernel(_, first_ref, *refs):
    total = first_ref[...]
    for ref in refs[:-1]:
        total = total + ref[...].astype(F32)
    refs[-1][...] = total.astype(BF)


def last_sum(parts, after):
    vmem = pl.BlockSpec(memory_space=pltpu.VMEM)
    return pl.pallas_call(
        last_sum_kernel,
        in_specs=[pl.BlockSpec(memory_space=pl.ANY)] + [vmem] * len(parts),
        out_specs=vmem,
        out_shape=jax.ShapeDtypeStruct(parts[0].shape, BF),
        compiler_params=pltpu.CompilerParams(vmem_limit_bytes=16 << 20),
        cost_estimate=pl.CostEstimate(flops=1000_000_000, bytes_accessed=0, transcendentals=0),
        name="last_sum",
    )(after, *parts)


def shared(hidden, down_weight, expert_ids, combine, out_grad):
    dp_count, cut_count = lax.axis_size("dp"), lax.axis_size("cuts")
    nz = cut_count // 2
    feat = out_grad.shape[1]

    def send(value, dp_flip, cut_flip):
        pairs = [
            (d * cut_count + c, (d ^ dp_flip) * cut_count + (c ^ cut_flip))
            for d in range(dp_count)
            for c in range(cut_count)
        ]
        return lax.ppermute(value, ("dp", "cuts"), pairs)

    def along(value, k):
        return lax.ppermute(value, "cuts", [(c, (c + 2 * k) % cut_count) for c in range(cut_count)])

    keep, away = forward(hidden, down_weight, out_grad.shape[1], dp_count)
    got = send(away, 1, 0)
    ids, coefs, _ = lax.optimization_barrier((expert_ids, combine, keep))
    own = jnp.pad(ids.T.astype(F32), ((0, 2), (0, 0))) + jnp.pad(coefs.T, ((2, 0), (0, 0)))
    to_x, by_x, to_y, by_y = spread(own, keep, got, out_grad)
    mine, meta, _ = lax.optimization_barrier((out_grad, own, by_x))
    far = [along(mine, k) for k in range(1, nz)]
    cross = send(mine, 2, 1)
    a, a_send, b, b_send, near_by, far = first_sum(
        out_grad, cross, own, by_x, send(to_x, 0, 1), by_y, send(to_y, 2, 0), far
    )
    terms = second_sum(own, a, b, send(a_send, 2, 0), send(b_send, 0, 1))
    sums = [terms[0]] + [along(terms[k], k) for k in range(1, nz)]

    far_y, far_x = send(far, 2, 0), send(far, 0, 1)
    near = send(meta, 2, 0)
    far_xy, metas = stack([along(cross, k) for k in range(1, nz)], own, near, a)
    parts = [near_by, far, far_x, far_y, far_xy]
    after = [None, None, None, None, sums[1]]
    grads = parts + [
        send(p if held is None else lax.optimization_barrier((p, held))[0], 1, 0) for p, held in zip(parts, after)
    ]
    hid_grad, down_grad, mark = backward(hidden, down_weight, metas, send(metas, 1, 0), grads, ())
    mixed = last_sum(sums, mark)
    return (mixed, hid_grad, down_grad)


def local(hidden, down_weight, expert_ids, combine, out_grad):
    dp_count, cut_count = lax.axis_size("dp"), lax.axis_size("cuts")
    few = dp_count == 4 and cut_count % 4 == 0 and dp_count * expert_ids.shape[0] <= 2 * hidden.shape[1]
    return (shared if few else routed)(hidden, down_weight, expert_ids, combine, out_grad)


def solution(mesh):
    return jax.shard_map(
        local,
        mesh=mesh,
        in_specs=(
            P("dp", None, "cuts"),
            P("dp", "cuts", None),
            P("dp", None),
            P("dp", None),
            P("dp", "cuts"),
        ),
        out_specs=(P("dp", "cuts"), P("dp", None, "cuts"), P("dp", "cuts", None)),
        check_vma=False,
    )
```

time: 61.1 us -> 57.9 us (0.948)
  starting transfers between devices: 29.4 us -> 21.4 us
  waiting for transfers between devices: 15.3 us -> 21.5 us
  local copies, waits for them, and re-layouts: 2.4 us -> 1.05 us
    ppermute x9, starting transfers between devices: 14.4 us -> 9.98 us  [along(): lax.ppermute(value, 'cuts', [(c, (c + 2 * k) % cut_count) for c in range(...]
    ppermute x9, waiting for transfers between devices: 10.3 us -> 14.2 us  [along(): lax.ppermute(value, 'cuts', [(c, (c + 2 * k) % cut_count) for c in range(...]
    ppermute x18 -> x15, starting transfers between devices: 15 us -> 11.5 us  [send(): return lax.ppermute(value, ('dp', 'cuts'), pairs)]
    ppermute x18 -> x15, waiting for transfers between devices: 5 us -> 7.3 us  [send(): return lax.ppermute(value, ('dp', 'cuts'), pairs)]
    unnamed x12, local copies, waits for them, and re-layouts: 2.4 us -> 1.05 us
    pallas_call x1, Pallas kernels: 1.64 us -> 0.75 us  [spread(): pl.pallas_call(functools.partial(spread_kernel, nz, capacity), out_shape=...]
  transfers between devices with their start and end apart: 27 -> 24, of which waited for: 9 -> 11; matrix products, arithmetic and copies ran while one was open for 0% -> 0% of each run, Pallas kernels for 11% -> 12%
where the time goes in v4:
time: 57.9 us; the launch traced here: 57.7 us
  waiting for transfers between devices  21.5 us (37%)
  starting transfers between devices  21.4 us (37%)
  Pallas kernels  12.9 us (22%)
  local copies, waits for them, and re-layouts  1.05 us (2%)
  between operations  0.74 us (1%)
    ppermute x9, waiting for transfers between devices, along(): lax.ppermute(value, 'cuts', [(c, (c + 2 * k) % cut_count) for c in range(...  14.2 us
    ppermute x15, starting transfers between devices, send(): return lax.ppermute(value, ('dp', 'cuts'), pairs)  11.5 us
    ppermute x9, starting transfers between devices, along(): lax.ppermute(value, 'cuts', [(c, (c + 2 * k) % cut_count) for c in range(...  9.98 us
    ppermute x15, waiting for transfers between devices, send(): return lax.ppermute(value, ('dp', 'cuts'), pairs)  7.3 us
    pallas_call x1, Pallas kernels, backward(): pl.pallas_call(functools.partial(backward_kernel, nz, capacity), in_specs...  6.26 us
    pallas_call x1, Pallas kernels, forward(): pl.pallas_call(functools.partial(forward_kernel, nz, capacity), in_specs=...  4.04 us
  transfers between devices with their start and end apart: 24, of which 11 were waited for; matrix products, arithmetic and copies ran while one was open for 0% of the time, Pallas kernels for 12%

profile of v4, /device:TPU:0, one launch (start us, length us, event | category | flops | bytes accessed | tf_op | source)
XLA Modules:
  0.0 57.7 jit_solution(7012020284355119590)
XLA Ops:
  0.6 1.0 %copy-done = bf16[1,256,1024]{2,1,0:T(8,128)(2,1)S(1)} copy-done((bf16[1,256,1024]{2,1,0:T(8,128)(2,1)S(1)}, bf16[1,256,1024]{2,1,0:T(8,128)(2,1)}, u32[]{:S(2)}) %copy-start) | copy-done | bytes 524312
  1.7 4.0 %forward_rows.1 = (bf16[4,2,2,64,384]{4,3,2,1,0:T(8,128)(2,1)S(1)}, bf16[4,2,2,64,384]{4,3,2,1,0:T(8,128)(2,1)S(1)}) custom-call(bf16[1,256,1024]{2,1,0:T(8,128)(2,1)S(1)} %copy-done, bf16[1,1024,3072]{2,1,0:T(8,128)(2,1)} %weight_ref.3), custom_call_target="tpu_custom_call" | custom-call | flops 1610612736 | bytes 8388608 | tf_op jit(solution)/shard_map/forward_rows/pallas_call | solution.py:112
  5.7 0.5 collective-permute-start
  6.3 1.9 %collective-permute-done.got_ref = bf16[4,2,2,64,384]{4,3,2,1,0:T(8,128)(2,1)S(1)} collective-permute-done((bf16[4,2,2,64,384]{4,3,2,1,0:T(8,128)(2,1)S(1)}, bf16[4,2,2,64,384]{4,3,2,1,0:T(8,128)(2,1)S(1)}, u32[]{:S(2)}, u32[]{:S(2)}) %collective-permute-start) | collective-permute-done | bytes 786464 | tf_op jit(solution)/shard_map/ppermute | solution.py:376
  8.2 0.8 %spread_rows.1 = (bf16[5,128,384]{2,1,0:T(8,128)(2,1)S(1)}, f32[4,128,384]{2,1,0:T(8,128)S(1)}, bf16[5,128,384]{2,1,0:T(8,128)(2,1)S(1)}, f32[4,128,384]{2,1,0:T(8,128)S(1)}) custom-call(f32[4,128]{1,0:T(4,128)S(1)} %pad_add_fusion.meta_ref, bf16[4,2,2,64,384]{4,3,2,1,0:T(8,128)(2,1)S(1)} %get-tuple-element.29.keep_ref, ...), custom_call_target="tpu_custom_call" | custom-call | flops 201326592 | bytes 4718592 | tf_op jit(solution)/shard_map/spread_rows/pallas_call | solution.py:172
  8.9 2.9 %collective-permute-start.2 = (bf16[5,128,384]{2,1,0:T(8,128)(2,1)S(1)}, bf16[5,128,384]{2,1,0:T(8,128)(2,1)S(1)}, u32[]{:S(2)}, u32[]{:S(2)}) collective-permute-start(bf16[5,128,384]{2,1,0:T(8,128)(2,1)S(1)} %get-tuple-element.35), channel_id=1, source_target_pairs={{0,1},{1,0},{2,3},{3,2},{4,5},{5,4},{6,7},{7,6},{8,9},{9,8},{10,11... | collective-permute-start | bytes 1474568 | tf_op jit(solution)/shard_map/ppermute | solution.py:376
  11.8 1.5 %collective-permute-start.3 = (bf16[5,128,384]{2,1,0:T(8,128)(2,1)S(1)}, bf16[5,128,384]{2,1,0:T(8,128)(2,1)S(1)}, u32[]{:S(2)}, u32[]{:S(2)}) collective-permute-start(bf16[5,128,384]{2,1,0:T(8,128)(2,1)S(1)} %get-tuple-element.37), channel_id=1, source_target_pairs={{0,16},{1,17},{2,18},{3,19},{4,20},{5,21},{6,22},{7,23},{8,24},{9,... | collective-permute-start | bytes 1474568 | tf_op jit(solution)/shard_map/ppermute | solution.py:376
  13.4 3.6 %collective-permute-start.6 = (bf16[128,384]{1,0:T(8,128)(2,1)S(1)}, bf16[128,384]{1,0:T(8,128)(2,1)S(1)}, u32[]{:S(2)}, u32[]{:S(2)}) collective-permute-start(bf16[128,384]{1,0:T(8,128)(2,1)S(1)} %copy-done.1), channel_id=1, source_target_pairs={{0,6},{1,7},{2,0},{3,1},{4,2},{5,3},{6,4},{7,5},{8,14},{9,15},{10,... | collective-permute-start | bytes 294920 | tf_op jit(solution)/shard_map/ppermute | solution.py:379
  17.0 1.0 %collective-permute-start.4 = (bf16[128,384]{1,0:T(8,128)(2,1)S(1)}, bf16[128,384]{1,0:T(8,128)(2,1)S(1)}, u32[]{:S(2)}, u32[]{:S(2)}) collective-permute-start(bf16[128,384]{1,0:T(8,128)(2,1)S(1)} %copy-done.1), channel_id=1, source_target_pairs={{0,2},{1,3},{2,4},{3,5},{4,6},{5,7},{6,0},{7,1},{8,10},{9,11},{10,... | collective-permute-start | bytes 294920 | tf_op jit(solution)/shard_map/ppermute | solution.py:379
  18.0 2.2 %collective-permute-done.6.refs_2_ = bf16[128,384]{1,0:T(8,128)(2,1)S(1)} collective-permute-done((bf16[128,384]{1,0:T(8,128)(2,1)S(1)}, bf16[128,384]{1,0:T(8,128)(2,1)S(1)}, u32[]{:S(2)}, u32[]{:S(2)}) %collective-permute-start.6) | collective-permute-done | bytes 98336 | tf_op jit(solution)/shard_map/ppermute | solution.py:379
  20.2 0.5 collective-permute-start.1
  20.7 4.6 %collective-permute-done.5.refs_1_ = bf16[128,384]{1,0:T(8,128)(2,1)S(1)} collective-permute-done((bf16[128,384]{1,0:T(8,128)(2,1)S(1)}, bf16[128,384]{1,0:T(8,128)(2,1)S(1)}, u32[]{:S(2)}, u32[]{:S(2)}) %collective-permute-start.5) | collective-permute-done | bytes 98336 | tf_op jit(solution)/shard_map/ppermute | solution.py:379
  25.3 1.5 %collective-permute-done.1.cross_ref = bf16[128,384]{1,0:T(8,128)(2,1)S(1)} collective-permute-done((bf16[128,384]{1,0:T(8,128)(2,1)S(1)}, bf16[128,384]{1,0:T(8,128)(2,1)S(1)}, u32[]{:S(2)}, u32[]{:S(2)}) %collective-permute-start.1) | collective-permute-done | bytes 98336 | tf_op jit(solution)/shard_map/ppermute | solution.py:376
  26.9 0.6 %first_sum.1 = (f32[2,128,384]{2,1,0:T(8,128)S(1)}, bf16[2,128,384]{2,1,0:T(8,128)(2,1)S(1)}, f32[2,128,384]{2,1,0:T(8,128)S(1)}, bf16[2,128,384]{2,1,0:T(8,128)...) custom-call(bf16[128,384]{1,0:T(8,128)(2,1)S(1)} %copy-done.1, ...), custom_call_target="tpu_custom_call" | custom-call | flops 1000000000 | tf_op jit(solution)/shard_map/first_sum/pallas_call | solution.py:205
  27.6 1.6 %collective-permute-start.18 = (bf16[2,128,384]{2,1,0:T(8,128)(2,1)S(1)}, bf16[2,128,384]{2,1,0:T(8,128)(2,1)S(1)}, u32[]{:S(2)}, u32[]{:S(2)}) collective-permute-start(bf16[2,128,384]{2,1,0:T(8,128)(2,1)S(1)} %get-tuple-element.45), channel_id=1, source_target_pairs={{0,16},{1,17},{2,18},{3,19},{4,20},{5,21},{6,22},{7,23},{8,24},{9,... | collective-permute-start | bytes 589832 | tf_op jit(solution)/shard_map/ppermute | solution.py:376
  29.2 0.5 collective-permute-start.19
  29.7 3.6 %collective-permute-start.10 = (bf16[128,384]{1,0:T(8,128)(2,1)S(1)}, bf16[128,384]{1,0:T(8,128)(2,1)S(1)}, u32[]{:S(2)}, u32[]{:S(2)}) collective-permute-start(bf16[128,384]{1,0:T(8,128)(2,1)S(1)} %collective-permute-done.1.cross_ref), channel_id=1, source_target_pairs={{0,6},{1,7},{2,0},{3,1},{4,2},{5,3},{6,4},{7,5},{8,14},{9,15},{10,... | collective-permute-start | bytes 294920 | tf_op jit(solution)/shard_map/ppermute | solution.py:379
  33.3 1.2 %collective-permute-start.7 = (f32[4,128]{1,0:T(4,128)S(1)}, f32[4,128]{1,0:T(4,128)S(1)}, u32[]{:S(2)}, u32[]{:S(2)}) collective-permute-start(f32[4,128]{1,0:T(4,128)S(1)} %pad_add_fusion.meta_ref), channel_id=1, source_target_pairs={{0,16},{1,17},{2,18},{3,19},{4,20},{5,21},{6,22},{7,23},{8,24},{9,... | collective-permute-start | bytes 6152 | tf_op jit(solution)/shard_map/ppermute | solution.py:376
  34.5 2.4 %collective-permute-done.7.near_ref = f32[4,128]{1,0:T(4,128)S(1)} collective-permute-done((f32[4,128]{1,0:T(4,128)S(1)}, f32[4,128]{1,0:T(4,128)S(1)}, u32[]{:S(2)}, u32[]{:S(2)}) %collective-permute-start.7) | collective-permute-done | bytes 2080 | tf_op jit(solution)/shard_map/ppermute | solution.py:376
  36.9 1.2 %collective-permute-start.13 = (bf16[3,128,384]{2,1,0:T(8,128)(2,1)S(1)}, bf16[3,128,384]{2,1,0:T(8,128)(2,1)S(1)}, u32[]{:S(2)}, u32[]{:S(2)}) collective-permute-start(bf16[3,128,384]{2,1,0:T(8,128)(2,1)S(1)} %get-tuple-element.42.refs_1_), channel_id=1, source_target_pairs={{0,16},{1,17},{2,18},{3,19},{4,20},{5,21},{6,22},{7,23},{8,24},{9,... | collective-permute-start | bytes 884744 | tf_op jit(solution)/shard_map/ppermute | solution.py:376
  38.1 0.8 %collective-permute-start.12 = (bf16[3,128,384]{2,1,0:T(8,128)(2,1)S(1)}, bf16[3,128,384]{2,1,0:T(8,128)(2,1)S(1)}, u32[]{:S(2)}, u32[]{:S(2)}) collective-permute-start(bf16[3,128,384]{2,1,0:T(8,128)(2,1)S(1)} %get-tuple-element.42.refs_1_), channel_id=1, source_target_pairs={{0,1},{1,0},{2,3},{3,2},{4,5},{5,4},{6,7},{7,6},{8,9},{9,8},{10,11... | collective-permute-start | bytes 884744 | tf_op jit(solution)/shard_map/ppermute | solution.py:376
  38.9 0.5 second_sum.1
  39.5 1.2 %collective-permute-done.9.refs_1_ = bf16[128,384]{1,0:T(8,128)(2,1)S(1)} collective-permute-done((bf16[128,384]{1,0:T(8,128)(2,1)S(1)}, bf16[128,384]{1,0:T(8,128)(2,1)S(1)}, u32[]{:S(2)}, u32[]{:S(2)}) %collective-permute-start.9) | collective-permute-done | bytes 98336 | tf_op jit(solution)/shard_map/ppermute | solution.py:379
  40.7 0.3 collective-permute-start.20
  40.9 2.4 %collective-permute-done.8.refs_0_ = bf16[128,384]{1,0:T(8,128)(2,1)S(1)} collective-permute-done((bf16[128,384]{1,0:T(8,128)(2,1)S(1)}, bf16[128,384]{1,0:T(8,128)(2,1)S(1)}, u32[]{:S(2)}, u32[]{:S(2)}) %collective-permute-start.8) | collective-permute-done | bytes 98336 | tf_op jit(solution)/shard_map/ppermute | solution.py:379
  43.4 3.7 %collective-permute-done.20.refs_0_ = bf16[128,384]{1,0:T(8,128)(2,1)S(1)} collective-permute-done((bf16[128,384]{1,0:T(8,128)(2,1)S(1)}, bf16[128,384]{1,0:T(8,128)(2,1)S(1)}, u32[]{:S(2)}, u32[]{:S(2)}) %collective-permute-start.20) | collective-permute-done | bytes 98336 | tf_op jit(solution)/shard_map/ppermute | solution.py:379
  47.1 1.2 %collective-permute-done.11.other_metas = f32[2,4,128]{2,1,0:T(4,128)S(1)} collective-permute-done((f32[2,4,128]{2,1,0:T(4,128)S(1)}, f32[2,4,128]{2,1,0:T(4,128)S(1)}, u32[]{:S(2)}, u32[]{:S(2)}) %collective-permute-start.11) | collective-permute-done | bytes 4128 | tf_op jit(solution)/shard_map/ppermute | solution.py:376
  48.4 0.3 collective-permute-start.17
  49.0 1.5 %collective-permute-start.23 = (bf16[128,384]{1,0:T(8,128)(2,1)S(1)}, bf16[128,384]{1,0:T(8,128)(2,1)S(1)}, u32[]{:S(2)}, u32[]{:S(2)}) collective-permute-start(bf16[128,384]{1,0:T(8,128)(2,1)S(1)} %get-tuple-element.52), channel_id=1, source_target_pairs={{0,6},{1,7},{2,0},{3,1},{4,2},{5,3},{6,4},{7,5},{8,14},{9,15},{10,... | collective-permute-start | bytes 294920 | tf_op jit(solution)/shard_map/ppermute | solution.py:379
  50.5 0.2 collective-permute-done.16.refs_7_
  50.7 6.3 %backward_rows.1 = (bf16[1,256,1024]{2,1,0:T(8,128)(2,1)}, bf16[1,1024,3072]{2,1,0:T(8,128)(2,1)}, f32[8,128]{1,0:T(8,128)S(1)}) custom-call(bf16[1,256,1024]{2,1,0:T(8,128)(2,1)S(1)} %copy-done, bf16[1,1024,3072]{2,1,0:T(8,128)(2,1)S(1)} %bitcast.4, f32[2,4,128]{2,1,0:T(4,128)S(1)} %get-tuple-element.40.metas, ...), custom_call_target="tpu_custom_call" | custom-call | flops 100000000 | tf_op jit(solution)/shard_map/backward_rows/pallas_call | solution.py:320
  57.0 0.7 %last_sum.1 = bf16[128,384]{1,0:T(8,128)(2,1)} custom-call(f32[8,128]{1,0:T(8,128)S(1)} %get-tuple-element.49._, f32[128,384]{1,0:T(8,128)S(1)} %get-tuple-element.50.first_ref, bf16[128,384]{1,0:T(8,128)(2,1)S(1)} %collective-permute-done.20.refs_0_, bf16[128,384]{1,0:T(8,128)(2,1)S(1)} %collective-permute-done.22.refs_1_, ...), custom_call_target="tpu_custom_call" | custom-call | flops 1000000000 | tf_op jit(solution)/shard_map/last_sum/pallas_call | solution.py:354
  (38 shorter events, 0.6 us)
Async XLA Ops:
  0.6 1.0 %copy-start = (bf16[1,256,1024]{2,1,0:T(8,128)(2,1)S(1)}, bf16[1,256,1024]{2,1,0:T(8,128)(2,1)}, u32[]{:S(2)}) copy-start(bf16[1,256,1024]{2,1,0:T(8,128)(2,1)} %hidden_ref.3) | copy-start | bytes 1572868
  1.7 4.6 %copy-start.2 = (s32[128,2]{0,1:T(2,128)S(1)}, s32[128,2]{0,1:T(2,128)}, u32[]{:S(2)}) copy-start(s32[128,2]{0,1:T(2,128)} %param.7) | copy-start | bytes 3076
  1.7 4.6 %copy-start.3 = (f32[128,2]{0,1:T(2,128)S(1)}, f32[128,2]{0,1:T(2,128)}, u32[]{:S(2)}) copy-start(f32[128,2]{0,1:T(2,128)} %param.8) | copy-start | bytes 3076
  1.7 6.5 %copy-start.1 = (bf16[128,384]{1,0:T(8,128)(2,1)S(1)}, bf16[128,384]{1,0:T(8,128)(2,1)}, u32[]{:S(2)}) copy-start(bf16[128,384]{1,0:T(8,128)(2,1)} %grad_ref.3) | copy-start | bytes 294916
  5.7 2.4 %collective-permute-start = (bf16[4,2,2,64,384]{4,3,2,1,0:T(8,128)(2,1)S(1)}, bf16[4,2,2,64,384]{4,3,2,1,0:T(8,128)(2,1)S(1)}, u32[]{:S(2)}, u32[]{:S(2)}) collective-permute-start(bf16[4,2,2,64,384]{4,3,2,1,0:T(8,128)(2,1)S(1)} %get-tuple-element.32), channel_id=1, source_target_pairs={{0,8},{1,9},{2,10},{3,11},{4,12},{5,13},{6,14},{7,15},{8,0},{9,1},... | collective-permute-start | bytes 2359304 | tf_op jit(solution)/shard_map/ppermute | solution.py:376
  8.9 17.9 %collective-permute-start.2 = (bf16[5,128,384]{2,1,0:T(8,128)(2,1)S(1)}, bf16[5,128,384]{2,1,0:T(8,128)(2,1)S(1)}, u32[]{:S(2)}, u32[]{:S(2)}) collective-permute-start(bf16[5,128,384]{2,1,0:T(8,128)(2,1)S(1)} %get-tuple-element.35), channel_id=1, source_target_pairs={{0,1},{1,0},{2,3},{3,2},{4,5},{5,4},{6,7},{7,6},{8,9},{9,8},{10,11... | collective-permute-start | bytes 1474568 | tf_op jit(solution)/shard_map/ppermute | solution.py:376
  11.8 15.1 %collective-permute-start.3 = (bf16[5,128,384]{2,1,0:T(8,128)(2,1)S(1)}, bf16[5,128,384]{2,1,0:T(8,128)(2,1)S(1)}, u32[]{:S(2)}, u32[]{:S(2)}) collective-permute-start(bf16[5,128,384]{2,1,0:T(8,128)(2,1)S(1)} %get-tuple-element.37), channel_id=1, source_target_pairs={{0,16},{1,17},{2,18},{3,19},{4,20},{5,21},{6,22},{7,23},{8,24},{9,... | collective-permute-start | bytes 1474568 | tf_op jit(solution)/shard_map/ppermute | solution.py:376
  13.4 6.8 %collective-permute-start.6 = (bf16[128,384]{1,0:T(8,128)(2,1)S(1)}, bf16[128,384]{1,0:T(8,128)(2,1)S(1)}, u32[]{:S(2)}, u32[]{:S(2)}) collective-permute-start(bf16[128,384]{1,0:T(8,128)(2,1)S(1)} %copy-done.1), channel_id=1, source_target_pairs={{0,6},{1,7},{2,0},{3,1},{4,2},{5,3},{6,4},{7,5},{8,14},{9,15},{10,... | collective-permute-start | bytes 294920 | tf_op jit(solution)/shard_map/ppermute | solution.py:379
  17.0 8.3 %collective-permute-start.5 = (bf16[128,384]{1,0:T(8,128)(2,1)S(1)}, bf16[128,384]{1,0:T(8,128)(2,1)S(1)}, u32[]{:S(2)}, u32[]{:S(2)}) collective-permute-start(bf16[128,384]{1,0:T(8,128)(2,1)S(1)} %copy-done.1), channel_id=1, source_target_pairs={{0,4},{1,5},{2,6},{3,7},{4,0},{5,1},{6,2},{7,3},{8,12},{9,13},{10,... | collective-permute-start | bytes 294920 | tf_op jit(solution)/shard_map/ppermute | solution.py:379
  17.0 8.3 %collective-permute-start.4 = (bf16[128,384]{1,0:T(8,128)(2,1)S(1)}, bf16[128,384]{1,0:T(8,128)(2,1)S(1)}, u32[]{:S(2)}, u32[]{:S(2)}) collective-permute-start(bf16[128,384]{1,0:T(8,128)(2,1)S(1)} %copy-done.1), channel_id=1, source_target_pairs={{0,2},{1,3},{2,4},{3,5},{4,6},{5,7},{6,0},{7,1},{8,10},{9,11},{10,... | collective-permute-start | bytes 294920 | tf_op jit(solution)/shard_map/ppermute | solution.py:379
  20.2 6.6 %collective-permute-start.1 = (bf16[128,384]{1,0:T(8,128)(2,1)S(1)}, bf16[128,384]{1,0:T(8,128)(2,1)S(1)}, u32[]{:S(2)}, u32[]{:S(2)}) collective-permute-start(bf16[128,384]{1,0:T(8,128)(2,1)S(1)} %copy-done.1), channel_id=1, source_target_pairs={{0,17},{1,16},{2,19},{3,18},{4,21},{5,20},{6,23},{7,22},{8,25},{9,... | collective-permute-start | bytes 294920 | tf_op jit(solution)/shard_map/ppermute | solution.py:376
  27.6 10.5 %collective-permute-start.18 = (bf16[2,128,384]{2,1,0:T(8,128)(2,1)S(1)}, bf16[2,128,384]{2,1,0:T(8,128)(2,1)S(1)}, u32[]{:S(2)}, u32[]{:S(2)}) collective-permute-start(bf16[2,128,384]{2,1,0:T(8,128)(2,1)S(1)} %get-tuple-element.45), channel_id=1, source_target_pairs={{0,16},{1,17},{2,18},{3,19},{4,20},{5,21},{6,22},{7,23},{8,24},{9,... | collective-permute-start | bytes 589832 | tf_op jit(solution)/shard_map/ppermute | solution.py:376
  29.2 9.8 %collective-permute-start.19 = (bf16[2,128,384]{2,1,0:T(8,128)(2,1)S(1)}, bf16[2,128,384]{2,1,0:T(8,128)(2,1)S(1)}, u32[]{:S(2)}, u32[]{:S(2)}) collective-permute-start(bf16[2,128,384]{2,1,0:T(8,128)(2,1)S(1)} %get-tuple-element.46), channel_id=1, source_target_pairs={{0,1},{1,0},{2,3},{3,2},{4,5},{5,4},{6,7},{7,6},{8,9},{9,8},{10,11... | collective-permute-start | bytes 589832 | tf_op jit(solution)/shard_map/ppermute | solution.py:376
  29.7 7.2 %collective-permute-start.10 = (bf16[128,384]{1,0:T(8,128)(2,1)S(1)}, bf16[128,384]{1,0:T(8,128)(2,1)S(1)}, u32[]{:S(2)}, u32[]{:S(2)}) collective-permute-start(bf16[128,384]{1,0:T(8,128)(2,1)S(1)} %collective-permute-done.1.cross_ref), channel_id=1, source_target_pairs={{0,6},{1,7},{2,0},{3,1},{4,2},{5,3},{6,4},{7,5},{8,14},{9,15},{10,... | collective-permute-start | bytes 294920 | tf_op jit(solution)/shard_map/ppermute | solution.py:379
  33.3 3.6 %collective-permute-start.7 = (f32[4,128]{1,0:T(4,128)S(1)}, f32[4,128]{1,0:T(4,128)S(1)}, u32[]{:S(2)}, u32[]{:S(2)}) collective-permute-start(f32[4,128]{1,0:T(4,128)S(1)} %pad_add_fusion.meta_ref), channel_id=1, source_target_pairs={{0,16},{1,17},{2,18},{3,19},{4,20},{5,21},{6,22},{7,23},{8,24},{9,... | collective-permute-start | bytes 6152 | tf_op jit(solution)/shard_map/ppermute | solution.py:376
  34.5 6.2 %collective-permute-start.9 = (bf16[128,384]{1,0:T(8,128)(2,1)S(1)}, bf16[128,384]{1,0:T(8,128)(2,1)S(1)}, u32[]{:S(2)}, u32[]{:S(2)}) collective-permute-start(bf16[128,384]{1,0:T(8,128)(2,1)S(1)} %collective-permute-done.1.cross_ref), channel_id=1, source_target_pairs={{0,4},{1,5},{2,6},{3,7},{4,0},{5,1},{6,2},{7,3},{8,12},{9,13},{10,... | collective-permute-start | bytes 294920 | tf_op jit(solution)/shard_map/ppermute | solution.py:379
  36.9 6.4 %collective-permute-start.8 = (bf16[128,384]{1,0:T(8,128)(2,1)S(1)}, bf16[128,384]{1,0:T(8,128)(2,1)S(1)}, u32[]{:S(2)}, u32[]{:S(2)}) collective-permute-start(bf16[128,384]{1,0:T(8,128)(2,1)S(1)} %collective-permute-done.1.cross_ref), channel_id=1, source_target_pairs={{0,2},{1,3},{2,4},{3,5},{4,6},{5,7},{6,0},{7,1},{8,10},{9,11},{10,... | collective-permute-start | bytes 294920 | tf_op jit(solution)/shard_map/ppermute | solution.py:379
  36.9 11.5 %collective-permute-start.13 = (bf16[3,128,384]{2,1,0:T(8,128)(2,1)S(1)}, bf16[3,128,384]{2,1,0:T(8,128)(2,1)S(1)}, u32[]{:S(2)}, u32[]{:S(2)}) collective-permute-start(bf16[3,128,384]{2,1,0:T(8,128)(2,1)S(1)} %get-tuple-element.42.refs_1_), channel_id=1, source_target_pairs={{0,16},{1,17},{2,18},{3,19},{4,20},{5,21},{6,22},{7,23},{8,24},{9,... | collective-permute-start | bytes 884744 | tf_op jit(solution)/shard_map/ppermute | solution.py:376
  38.1 10.7 %collective-permute-start.12 = (bf16[3,128,384]{2,1,0:T(8,128)(2,1)S(1)}, bf16[3,128,384]{2,1,0:T(8,128)(2,1)S(1)}, u32[]{:S(2)}, u32[]{:S(2)}) collective-permute-start(bf16[3,128,384]{2,1,0:T(8,128)(2,1)S(1)} %get-tuple-element.42.refs_1_), channel_id=1, source_target_pairs={{0,1},{1,0},{2,3},{3,2},{4,5},{5,4},{6,7},{7,6},{8,9},{9,8},{10,11... | collective-permute-start | bytes 884744 | tf_op jit(solution)/shard_map/ppermute | solution.py:376
  38.9 10.0 %collective-permute-start.14 = (bf16[4,128,384]{2,1,0:T(8,128)(2,1)S(1)}, bf16[4,128,384]{2,1,0:T(8,128)(2,1)S(1)}, u32[]{:S(2)}, u32[]{:S(2)}) collective-permute-start(bf16[4,128,384]{2,1,0:T(8,128)(2,1)S(1)} %get-tuple-element.41.refs_0_), channel_id=1, source_target_pairs={{0,8},{1,9},{2,10},{3,11},{4,12},{5,13},{6,14},{7,15},{8,0},{9,1},... | collective-permute-start | bytes 1179656 | tf_op jit(solution)/shard_map/ppermute | solution.py:376
  38.9 11.8 %slice-start = ((s8[6291456]{0:T(1024)(128)(4,1)}), s8[4194304]{0:T(1024)(128)(4,1)S(1)}, s32[]{:S(2)}) async-start(s8[6291456]{0:T(1024)(128)(4,1)} %bitcast.3), calls=%async_computation | async-start | bytes 8388608
  38.9 11.8 %slice-start.1 = ((s8[6291456]{0:T(1024)(128)(4,1)}), s8[2097152]{0:T(1024)(128)(4,1)S(1)}, s32[]{:S(2)}) async-start(s8[6291456]{0:T(1024)(128)(4,1)} %bitcast.3), calls=%async_computation.1 | async-start | bytes 4194304
  40.7 6.4 %collective-permute-start.20 = (bf16[128,384]{1,0:T(8,128)(2,1)S(1)}, bf16[128,384]{1,0:T(8,128)(2,1)S(1)}, u32[]{:S(2)}, u32[]{:S(2)}) collective-permute-start(bf16[128,384]{1,0:T(8,128)(2,1)S(1)} %get-tuple-element.47), channel_id=1, source_target_pairs={{0,2},{1,3},{2,4},{3,5},{4,6},{5,7},{6,0},{7,1},{8,10},{9,11},{10,... | collective-permute-start | bytes 294920 | tf_op jit(solution)/shard_map/ppermute | solution.py:379
  43.3 5.6 %collective-permute-start.15 = (bf16[3,128,384]{2,1,0:T(8,128)(2,1)S(1)}, bf16[3,128,384]{2,1,0:T(8,128)(2,1)S(1)}, u32[]{:S(2)}, u32[]{:S(2)}) collective-permute-start(bf16[3,128,384]{2,1,0:T(8,128)(2,1)S(1)} %get-tuple-element.42.refs_1_), channel_id=1, source_target_pairs={{0,8},{1,9},{2,10},{3,11},{4,12},{5,13},{6,14},{7,15},{8,0},{9,1},... | collective-permute-start | bytes 884744 | tf_op jit(solution)/shard_map/ppermute | solution.py:376
  47.1 1.2 %collective-permute-start.11 = (f32[2,4,128]{2,1,0:T(4,128)S(1)}, f32[2,4,128]{2,1,0:T(4,128)S(1)}, u32[]{:S(2)}, u32[]{:S(2)}) collective-permute-start(f32[2,4,128]{2,1,0:T(4,128)S(1)} %get-tuple-element.40.metas), channel_id=1, source_target_pairs={{0,8},{1,9},{2,10},{3,11},{4,12},{5,13},{6,14},{7,15},{8,0},{9,1},... | collective-permute-start | bytes 12296 | tf_op jit(solution)/shard_map/ppermute | solution.py:376
  48.3 2.2 %collective-permute-start.21 = (bf16[3,128,384]{2,1,0:T(8,128)(2,1)S(1)}, bf16[3,128,384]{2,1,0:T(8,128)(2,1)S(1)}, u32[]{:S(2)}, u32[]{:S(2)}) collective-permute-start(bf16[3,128,384]{2,1,0:T(8,128)(2,1)S(1)} %get-tuple-element.48.refs_4_), channel_id=1, source_target_pairs={{0,8},{1,9},{2,10},{3,11},{4,12},{5,13},{6,14},{7,15},{8,0},{9,1},... | collective-permute-start | bytes 884744 | tf_op jit(solution)/shard_map/ppermute | solution.py:376
  48.4 2.0 %collective-permute-start.17 = (bf16[3,128,384]{2,1,0:T(8,128)(2,1)S(1)}, bf16[3,128,384]{2,1,0:T(8,128)(2,1)S(1)}, u32[]{:S(2)}, u32[]{:S(2)}) collective-permute-start(bf16[3,128,384]{2,1,0:T(8,128)(2,1)S(1)} %collective-permute-done.13.refs_3_), channel_id=1, source_target_pairs={{0,8},{1,9},{2,10},{3,11},{4,12},{5,13},{6,14},{7,15},{8,0},{9,1},... | collective-permute-start | bytes 884744 | tf_op jit(solution)/shard_map/ppermute | solution.py:376
  48.8 1.9 %collective-permute-start.16 = (bf16[3,128,384]{2,1,0:T(8,128)(2,1)S(1)}, bf16[3,128,384]{2,1,0:T(8,128)(2,1)S(1)}, u32[]{:S(2)}, u32[]{:S(2)}) collective-permute-start(bf16[3,128,384]{2,1,0:T(8,128)(2,1)S(1)} %collective-permute-done.12.refs_2_), channel_id=1, source_target_pairs={{0,8},{1,9},{2,10},{3,11},{4,12},{5,13},{6,14},{7,15},{8,0},{9,1},... | collective-permute-start | bytes 884744 | tf_op jit(solution)/shard_map/ppermute | solution.py:376
  49.0 8.0 %collective-permute-start.22 = (bf16[128,384]{1,0:T(8,128)(2,1)S(1)}, bf16[128,384]{1,0:T(8,128)(2,1)S(1)}, u32[]{:S(2)}, u32[]{:S(2)}) collective-permute-start(bf16[128,384]{1,0:T(8,128)(2,1)S(1)} %get-tuple-element.51), channel_id=1, source_target_pairs={{0,4},{1,5},{2,6},{3,7},{4,0},{5,1},{6,2},{7,3},{8,12},{9,13},{10,... | collective-permute-start | bytes 294920 | tf_op jit(solution)/shard_map/ppermute | solution.py:379
  49.0 8.0 %collective-permute-start.23 = (bf16[128,384]{1,0:T(8,128)(2,1)S(1)}, bf16[128,384]{1,0:T(8,128)(2,1)S(1)}, u32[]{:S(2)}, u32[]{:S(2)}) collective-permute-start(bf16[128,384]{1,0:T(8,128)(2,1)S(1)} %get-tuple-element.52), channel_id=1, source_target_pairs={{0,6},{1,7},{2,0},{3,1},{4,2},{5,3},{6,4},{7,5},{8,14},{9,15},{10,... | collective-permute-start | bytes 294920 | tf_op jit(solution)/shard_map/ppermute | solution.py:379

commit v5 on v4

--- a/solution.py
+++ b/solution.py
@@ -146,11 +146,20 @@
     return add_up
 
 
-def spread_kernel(nz, capacity, meta_ref, keep_ref, got_ref, grad_ref, to_x, by_x, to_y, by_y):
+def spread_kernel(nz, capacity, meta_ref, keep_ref, got_ref, grad_ref, to_x, by_x, to_y, by_y, split):
     me, x = lax.axis_index("dp"), lax.axis_index("cuts") % 2
     half = nz // 2
+    tok = grad_ref.shape[0]
     to_x[nz] = grad_ref[...]
-    to_y[nz] = grad_ref[...]
+    to_y[nz * tok : (nz + 1) * tok] = grad_ref[...]
+    rest = meta_ref[...]
+    count = rest.shape[0]
+    split[...] = jnp.zeros_like(split)
+    for i in range(3):
+        piece = rest.astype(BF).astype(F32)
+        split[count * i : count * (i + 1)] = piece
+        rest = rest - piece
+    to_y[(nz + 1) * tok :, :tok] = split[...].astype(BF)
     add_up = by_token(meta_ref[...], (me, me ^ 1), capacity)
     for z in range(half):
         to_x[z] = add_up(keep_ref[z, x ^ 1, 0], got_ref[z, x ^ 1, 0]).astype(BF)
@@ -161,17 +170,24 @@
         by_x[half + z, capacity:] = got_ref[z, x, 1].astype(F32)
         for dx in range(2):
             by_y[half * dx + z] = add_up(keep_ref[half + z, x ^ dx, 0], got_ref[half + z, x ^ dx, 0])
-            to_y[half * dx + z, :capacity] = keep_ref[half + z, x ^ dx, 1]
-            to_y[half * dx + z, capacity:] = got_ref[half + z, x ^ dx, 1]
+            at = (half * dx + z) * tok
+            to_y[at : at + capacity] = keep_ref[half + z, x ^ dx, 1]
+            to_y[at + capacity : at + tok] = got_ref[half + z, x ^ dx, 1]
 
 
 def spread(meta, keep, got, grad):
     nz, _, _, capacity, _ = keep.shape
     tok, feat = grad.shape
-    shapes = [jax.ShapeDtypeStruct((nz + 1, tok, feat), BF), jax.ShapeDtypeStruct((nz, tok, feat), F32)] * 2
+    kept = jax.ShapeDtypeStruct((nz, tok, feat), F32)
     return pl.pallas_call(
         functools.partial(spread_kernel, nz, capacity),
-        out_shape=shapes,
+        out_shape=[
+            jax.ShapeDtypeStruct((nz + 1, tok, feat), BF),
+            kept,
+            jax.ShapeDtypeStruct(((nz + 1) * tok + 16, feat), BF),
+            kept,
+        ],
+        scratch_shapes=[pltpu.VMEM((16, tok), F32)],
         compiler_params=pltpu.CompilerParams(vmem_limit_bytes=24 << 20),
         cost_estimate=pl.CostEstimate(
             flops=16 * tok * capacity * nz * feat, bytes_accessed=24 * tok * nz * feat, transcendentals=0
@@ -180,50 +196,84 @@
     )(meta, keep, got, grad)
 
 
-def first_sum_kernel(half, grad_ref, cross_ref, meta_ref, x_kept, x_got, y_kept, y_got, *refs):
-    far, (x_keep, x_send, y_keep, y_send, near_by, stacked) = refs[:-6], refs[-6:]
-    me, capacity = lax.axis_index("dp"), x_kept.shape[1] // 2
-    for k, ref in enumerate(far):
-        stacked[k] = ref[...]
-    for i, rows in enumerate((grad_ref[...], x_got[2 * half], y_got[2 * half], cross_ref[...])):
-        near_by[i] = rows
+def first_sum_kernel(half, grad_ref, meta_ref, x_kept, x_got, y_kept, y_got, *refs):
+    x_keep, x_send, y_keep, y_send, near_by, metas = refs
+    me, tok, count = lax.axis_index("dp"), x_kept.shape[1], meta_ref.shape[0]
+    capacity, mid = tok // 2, tok // 2
+    own = 2 * half * tok
+    near_by[0] = grad_ref[...]
+    near_by[1] = x_got[2 * half]
+    near_by[2] = y_got[own : own + tok]
+    x_send[half * tok :] = x_got[2 * half, :mid]
+    y_send[half * tok :] = y_got[own + mid : own + tok]
+    split = y_got[own + tok :, :tok].astype(F32)
+    metas[0] = meta_ref[...]
+    metas[1] = split[:count] + split[count : 2 * count] + split[2 * count : 3 * count]
     add_up = by_token(meta_ref[...], (me ^ 2, me ^ 3), capacity)
+
+    def come(place):
+        at = place * tok
+        return add_up(y_got[at : at + capacity], y_got[at + capacity : at + tok])
+
     for z in range(half):
+        here = slice(z * tok, (z + 1) * tok)
         x_keep[z] = x_kept[z] + x_got[z].astype(F32)
-        x_send[z] = (x_kept[half + z] + x_got[half + z].astype(F32)).astype(BF)
-        y_keep[z] = y_kept[z] + add_up(y_got[z, :capacity], y_got[z, capacity:])
-        y_send[z] = (y_kept[half + z] + add_up(y_got[half + z, :capacity], y_got[half + z, capacity:])).astype(BF)
-
-
-def first_sum(grad, cross, meta, x_kept, x_got, y_kept, y_got, far):
+        x_send[here] = (x_kept[half + z] + x_got[half + z].astype(F32)).astype(BF)
+        y_keep[z] = y_kept[z] + come(z)
+        y_send[here] = (y_kept[half + z] + come(half + z)).astype(BF)
+
+
+def first_sum(grad, meta, x_kept, x_got, y_kept, y_got):
     nz, tok, feat = x_kept.shape
     half = nz // 2
     shapes = [
         jax.ShapeDtypeStruct((half, tok, feat), F32),
-        jax.ShapeDtypeStruct((half, tok, feat), BF),
+        jax.ShapeDtypeStruct((half * tok + tok // 2, feat), BF),
     ]
     return pl.pallas_call(
         functools.partial(first_sum_kernel, half),
         out_shape=shapes
         + shapes
         + [
-            jax.ShapeDtypeStruct((4, tok, feat), BF),
-            jax.ShapeDtypeStruct((len(far), tok, feat), BF),
+            jax.ShapeDtypeStruct((3, tok, feat), BF),
+            jax.ShapeDtypeStruct((2, *meta.shape), F32),
         ],
         compiler_params=pltpu.CompilerParams(vmem_limit_bytes=16 << 20),
         cost_estimate=pl.CostEstimate(flops=1000_000_000, bytes_accessed=0, transcendentals=0),
         name="first_sum",
-    )(grad, cross, meta, x_kept, x_got, y_kept, y_got, *far)
+    )(grad, meta, x_kept, x_got, y_kept, y_got)
+
+
+def stack_kernel(_, *refs):
+    for k, ref in enumerate(refs[:-1]):
+        refs[-1][k] = ref[...]
+
+
+def stack(parts, after):
+    vmem = pl.BlockSpec(memory_space=pltpu.VMEM)
+    return pl.pallas_call(
+        stack_kernel,
+        in_specs=[pl.BlockSpec(memory_space=pl.ANY)] + [vmem] * len(parts),
+        out_specs=vmem,
+        out_shape=jax.ShapeDtypeStruct((len(parts), *parts[0].shape), BF),
+        compiler_params=pltpu.CompilerParams(vmem_limit_bytes=16 << 20),
+        cost_estimate=pl.CostEstimate(flops=1000_000_000, bytes_accessed=0, transcendentals=0),
+        name="stack_blocks",
+    )(after, *parts)
 
 
 def second_sum_kernel(nz, meta_ref, x_kept, y_kept, by_y, by_x, *refs):
-    outs, total = refs[:nz], refs[nz]
+    outs, cross, total = refs[:nz], refs[nz], refs[nz + 1]
     me, z, half = lax.axis_index("dp"), lax.axis_index("cuts") // 2, nz // 2
-    capacity = by_y.shape[1] // 2
+    tok = x_kept.shape[1]
+    capacity, mid = tok // 2, tok // 2
+    cross[:mid] = by_y[half * tok :]
+    cross[mid:] = by_x[half * tok :]
     add_up = by_token(meta_ref[...], (me ^ 2, me ^ 3), capacity)
     for i in range(half):
-        total[i] = x_kept[i] + add_up(by_y[i, :capacity], by_y[i, capacity:])
-        total[half + i] = y_kept[i] + by_x[i].astype(F32)
+        at = i * tok
+        total[i] = x_kept[i] + add_up(by_y[at : at + capacity], by_y[at + capacity : at + tok])
+        total[half + i] = y_kept[i] + by_x[at : at + tok].astype(F32)
     for k in range(nz):
         outs[k][...] = total[lax.rem(z + k, nz)].astype(outs[k].dtype)
 
@@ -233,76 +283,100 @@
     nz = 2 * half
     return pl.pallas_call(
         functools.partial(second_sum_kernel, nz),
-        out_shape=[jax.ShapeDtypeStruct((tok, feat), F32 if k == 0 else BF) for k in range(nz)],
+        out_shape=[jax.ShapeDtypeStruct((tok, feat), F32 if k == 0 else BF) for k in range(nz)]
+        + [jax.ShapeDtypeStruct((tok, feat), BF)],
         scratch_shapes=[pltpu.VMEM((nz, tok, feat), F32)],
         compiler_params=pltpu.CompilerParams(vmem_limit_bytes=16 << 20),
-        cost_estimate=pl.CostEstimate(flops=5000_000_000, bytes_accessed=0, transcendentals=0),
+        cost_estimate=pl.CostEstimate(flops=1000_000_000, bytes_accessed=0, transcendentals=0),
         name="second_sum",
     )(meta, x_kept, y_kept, by_y, by_x)
 
 
-def stack_kernel(_, meta_ref, near_ref, *refs):
-    refs, (stacked, metas) = refs[:-2], refs[-2:]
-    for k, ref in enumerate(refs):
-        stacked[k] = ref[...]
-    metas[0] = meta_ref[...]
-    metas[1] = near_ref[...]
-
-
-def stack(parts, meta, near, after):
-    vmem = pl.BlockSpec(memory_space=pltpu.VMEM)
-    return pl.pallas_call(
-        stack_kernel,
-        in_specs=[pl.BlockSpec(memory_space=pl.ANY)] + [vmem] * (2 + len(parts)),
-        out_specs=[vmem] * 2,
-        out_shape=[
-            jax.ShapeDtypeStruct((len(parts), *parts[0].shape), BF),
-            jax.ShapeDtypeStruct((2, *meta.shape), F32),
-        ],
-        compiler_params=pltpu.CompilerParams(vmem_limit_bytes=16 << 20),
-        cost_estimate=pl.CostEstimate(flops=1000_000_000, bytes_accessed=0, transcendentals=0),
-        name="stack_blocks",
-    )(after, meta, near, *parts)
-
-
-def backward_kernel(nz, capacity, hidden_ref, weight_ref, metas, other_metas, *refs):
-    grads, refs = (refs[:5], refs[5:10]), refs[10:]
-    hid_out, down_out, mark, made, rows_ref, turned, total, done, hots, cols, sems = refs[-11:]
-    mark[...] = jnp.zeros_like(mark)
-    me, x, z = lax.axis_index("dp"), lax.axis_index("cuts") % 2, lax.axis_index("cuts") // 2
-    feat = rows_ref.shape[1] // 2
-
+def put(rows_ref, hots, cols, dx, q, grads):
+    capacity, feat = hots.shape[1], grads.shape[1]
+    lane = pl.multiple_of((lax.axis_index("cuts") % 2 ^ dx) * feat, feat)
+    at = pl.multiple_of((lax.axis_index("dp") ^ q) * capacity, capacity)
+    picked = jnp.dot(hots[q], grads, preferred_element_type=F32)
+    rows_ref[pl.ds(at, capacity), pl.ds(lane, feat)] = (picked * cols[q][:, 0:1]).astype(BF)
+
+
+def columns(nz, k, feat):
+    z = lax.rem(lax.axis_index("cuts") // 2 - k + nz, nz)
+    return pl.ds(pl.multiple_of(z * 2 * feat, 2 * feat), 2 * feat)
+
+
+def times_transposed(rows, weight):
+    return lax.dot_general(rows, weight, (((1,), (1,)), ((), ())), preferred_element_type=F32)
+
+
+def backward_here_kernel(nz, hidden_ref, weight_ref, metas, other_metas, *refs):
+    grads, (part, down_out, turned, hots, cols), (made, rows_ref, sem) = refs[:4], refs[-8:-3], refs[-3:]
+    me, capacity, feat = lax.axis_index("dp"), hots.shape[1], rows_ref.shape[1] // 2
     for dy in range(2):
         for dc, ref in enumerate((metas, other_metas)):
             hot, weight = routing(ref[dy], me, capacity)
             hots[2 * dy + dc] = hot.astype(BF)
             cols[2 * dy + dc] = jnp.broadcast_to(jnp.sum(hot * weight, axis=1, keepdims=True), cols.shape[1:])
     turned[...] = hidden_ref[0].T
-
-    def put(dx, q, rows):
-        lane = pl.multiple_of((x ^ dx) * feat, feat)
-        at = pl.multiple_of((me ^ q) * capacity, capacity)
-        picked = jnp.dot(hots[q], rows, preferred_element_type=F32)
-        rows_ref[pl.ds(at, capacity), pl.ds(lane, feat)] = (picked * cols[q][:, 0:1]).astype(BF)
-
+    for dc in range(2):
+        for j in range(4):
+            put(rows_ref, hots, cols, j % 2, 2 * (j // 2) + dc, grads[dc][j] if j < 3 else grads[2 + dc][...])
+    rows, column = rows_ref[...], columns(nz, 0, feat)
+    made[...] = jnp.dot(turned[...], rows, preferred_element_type=F32).astype(BF)
+    copy = pltpu.make_async_copy(made, down_out.at[0, :, column], sem)
+    copy.start()
+    part[...] = times_transposed(rows, weight_ref[0, :, column])
+    copy.wait()
+
+
+def backward_here(hidden, weight, metas, other_metas, near_by, cross, after=()):
+    _, slots, ff = hidden.shape
+    tok, feat = near_by[0].shape[1:]
+    capacity = slots // 4
+    anywhere, vmem = pl.BlockSpec(memory_space=pl.ANY), pl.BlockSpec(memory_space=pltpu.VMEM)
+    return pl.pallas_call(
+        functools.partial(backward_here_kernel, weight.shape[2] // (2 * feat)),
+        in_specs=[vmem] * 8 + [anywhere] * len(after),
+        out_specs=[vmem, anywhere, vmem, vmem, vmem],
+        scratch_shapes=[
+            pltpu.VMEM((ff, 2 * feat), BF),
+            pltpu.VMEM((slots, 2 * feat), BF),
+            pltpu.SemaphoreType.DMA,
+        ],
+        out_shape=[
+            jax.ShapeDtypeStruct((slots, ff), F32),
+            jax.ShapeDtypeStruct(weight.shape, BF),
+            jax.ShapeDtypeStruct((ff, slots), BF),
+            jax.ShapeDtypeStruct((4, capacity, tok), BF),
+            jax.ShapeDtypeStruct((4, capacity, 128), F32),
+        ],
+        compiler_params=pltpu.CompilerParams(vmem_limit_bytes=16 << 20),
+        cost_estimate=pl.CostEstimate(flops=2000_000_000, bytes_accessed=0, transcendentals=0),
+        name="backward_here",
+    )(hidden, weight, metas, other_metas, *near_by, *cross, *after)
+
+
+def backward_kernel(nz, weight_ref, part_ref, turned, hots, cols, *refs):
+    grads, (hid_out, down_out, mark), (made, rows_ref, total, done, sems) = (refs[:5], refs[5:10]), refs[-8:-5], refs[-5:]
+    feat = rows_ref.shape[1] // 2
+    mark[...] = jnp.zeros_like(mark)
     leaving = []
-    for k in range(nz):
+    for k in range(1, nz):
         for dc in range(2):
-            near_by, far, far_x, far_y, far_xy = grads[dc]
-            for j, ref in enumerate((far, far_x, far_y, far_xy)):
-                put(j % 2, 2 * (j // 2) + dc, near_by[j] if k == 0 else ref[k - 1])
-        rows = rows_ref[...]
-        column = pl.ds(pl.multiple_of(lax.rem(z - k + nz, nz) * 2 * feat, 2 * feat), 2 * feat)
-        part = lax.dot_general(rows, weight_ref[0, :, column], (((1,), (1,)), ((), ())), preferred_element_type=F32)
-        if k:
-            part = total[...] + part
+            far, far_x, far_y, low, high = grads[dc]
+            count = low.shape[0]
+            cross = low[k - 1] if k <= count else high[k - 1 - count]
+            for j, rows in enumerate((far[k - 1], far_x[k - 1], far_y[k - 1], cross)):
+                put(rows_ref, hots, cols, j % 2, 2 * (j // 2) + dc, rows)
+        rows, column = rows_ref[...], columns(nz, k, feat)
+        part = (part_ref if k == 1 else total)[...] + times_transposed(rows, weight_ref[0, :, column])
         if k < nz - 1:
             total[...] = part
         else:
             done[...] = part.astype(BF)
             leaving.append(pltpu.make_async_copy(done, hid_out.at[0], sems.at[2]))
             leaving[-1].start()
-        if k >= 2:
+        if k > 2:
             leaving.pop(0).wait()
         made[k % 2] = jnp.dot(turned[...], rows, preferred_element_type=F32).astype(BF)
         leaving.append(pltpu.make_async_copy(made.at[k % 2], down_out.at[0, :, column], sems.at[k % 2]))
@@ -311,24 +385,20 @@
         copy.wait()
 
 
-def backward(hidden, weight, metas, other_metas, grads, after=()):
-    tok, feat = grads[1].shape[1:]
+def backward(hidden, weight, here, grads, after=()):
+    part, down, turned, hots, cols = here
+    feat = grads[0].shape[2]
     _, slots, ff = hidden.shape
-    width = weight.shape[2]
-    nz, capacity = width // (2 * feat), slots // 4
     anywhere, vmem = pl.BlockSpec(memory_space=pl.ANY), pl.BlockSpec(memory_space=pltpu.VMEM)
     return pl.pallas_call(
-        functools.partial(backward_kernel, nz, capacity),
-        in_specs=[vmem] * 14 + [anywhere] * len(after),
+        functools.partial(backward_kernel, weight.shape[2] // (2 * feat)),
+        in_specs=[vmem] * 15 + [anywhere] * (1 + len(after)),
         out_specs=[anywhere, anywhere, vmem],
         scratch_shapes=[
             pltpu.VMEM((2, ff, 2 * feat), BF),
             pltpu.VMEM((slots, 2 * feat), BF),
-            pltpu.VMEM((ff, slots), BF),
             pltpu.VMEM((slots, ff), F32),
             pltpu.VMEM((slots, ff), BF),
-            pltpu.VMEM((4, capacity, tok), BF),
-            pltpu.VMEM((4, capacity, 128), F32),
             pltpu.SemaphoreType.DMA((3,)),
         ],
         out_shape=[
@@ -336,10 +406,11 @@
             jax.ShapeDtypeStruct(weight.shape, BF),
             jax.ShapeDtypeStruct((8, 128), F32),
         ],
+        input_output_aliases={15: 1},
         compiler_params=pltpu.CompilerParams(vmem_limit_bytes=32 << 20),
         cost_estimate=pl.CostEstimate(flops=100_000_000, bytes_accessed=0, transcendentals=0),
         name="backward_rows",
-    )(hidden, weight, metas, other_metas, *grads, *after)
+    )(weight, part, turned, hots, cols, *grads, down, *after)
 
 
 def last_sum_kernel(_, first_ref, *refs):
@@ -383,31 +454,34 @@
     ids, coefs, _ = lax.optimization_barrier((expert_ids, combine, keep))
     own = jnp.pad(ids.T.astype(F32), ((0, 2), (0, 0))) + jnp.pad(coefs.T, ((2, 0), (0, 0)))
     to_x, by_x, to_y, by_y = spread(own, keep, got, out_grad)
-    mine, meta, _ = lax.optimization_barrier((out_grad, own, by_x))
+    mine, _ = lax.optimization_barrier((out_grad, by_x))
     far = [along(mine, k) for k in range(1, nz)]
-    cross = send(mine, 2, 1)
-    a, a_send, b, b_send, near_by, far = first_sum(
-        out_grad, cross, own, by_x, send(to_x, 0, 1), by_y, send(to_y, 2, 0), far
-    )
-    terms = second_sum(own, a, b, send(a_send, 2, 0), send(b_send, 0, 1))
+    a, a_send, b, b_send, near_by, metas = first_sum(
+        out_grad, own, by_x, send(to_x, 0, 1), by_y, send(to_y, 2, 0)
+    )
+    other = send(near_by, 1, 0)
+    far = stack(far, a)
+    *terms, cross = second_sum(own, a, b, send(a_send, 2, 0), send(b_send, 0, 1))
     sums = [terms[0]] + [along(terms[k], k) for k in range(1, nz)]
 
     far_y, far_x = send(far, 2, 0), send(far, 0, 1)
-    near = send(meta, 2, 0)
-    far_xy, metas = stack([along(cross, k) for k in range(1, nz)], own, near, a)
-    parts = [near_by, far, far_x, far_y, far_xy]
-    after = [None, None, None, None, sums[1]]
+    low, high = send(far_x[: nz // 2], 2, 0), send(far_y[nz // 2 :], 0, 1)
+    here = backward_here(
+        hidden, down_weight, metas, send(metas, 1, 0), (near_by, other), (cross, send(cross, 1, 0)), (sums[1], sums[-1])
+    )
+    parts = [far, far_x, far_y, low, high]
+    after = [None, None, None, here[0], sums[-1]]
     grads = parts + [
         send(p if held is None else lax.optimization_barrier((p, held))[0], 1, 0) for p, held in zip(parts, after)
     ]
-    hid_grad, down_grad, mark = backward(hidden, down_weight, metas, send(metas, 1, 0), grads, ())
+    hid_grad, down_grad, mark = backward(hidden, down_weight, here, grads, ())
     mixed = last_sum(sums, mark)
     return (mixed, hid_grad, down_grad)
 
 
 def local(hidden, down_weight, expert_ids, combine, out_grad):
     dp_count, cut_count = lax.axis_size("dp"), lax.axis_size("cuts")
-    few = dp_count == 4 and cut_count % 4 == 0 and dp_count * expert_ids.shape[0] <= 2 * hidden.shape[1]
+    few = dp_count == 4 and cut_count % 4 == 0 and expert_ids.shape[0] <= out_grad.shape[1] and dp_count * expert_ids.shape[0] <= 2 * hidden.shape[1]
     return (shared if few else routed)(hidden, down_weight, expert_ids, combine, out_grad)
 
 

time: 57.9 us -> 56.5 us (0.976)
  waiting for transfers between devices: 21.5 us -> 16.5 us
  starting transfers between devices: 21.4 us -> 24 us
  Pallas kernels: 12.9 us -> 14 us
    ppermute x9 -> x6, waiting for transfers between devices: 14.2 us -> 2.34 us  [along(): lax.ppermute(value, 'cuts', [(c, (c + 2 * k) % cut_count) for c in range(...]
    ppermute x15 -> x17, waiting for transfers between devices: 7.3 us -> 14.1 us  [send(): return lax.ppermute(value, ('dp', 'cuts'), pairs)]
    ppermute x15 -> x17, starting transfers between devices: 11.5 us -> 13.5 us  [send(): return lax.ppermute(value, ('dp', 'cuts'), pairs)]
    pallas_call x1 -> x2, Pallas kernels: 6.26 us -> 7.36 us  [the longest x1 5 us: backward(): pl.pallas_call(functools.partial(backward_kernel, weight.shape[2] // (2 *...]
    ppermute x9 -> x6, starting transfers between devices: 9.98 us -> 10.5 us  [along(): lax.ppermute(value, 'cuts', [(c, (c + 2 * k) % cut_count) for c in range(...]
  transfers between devices with their start and end apart: 24 -> 23, of which waited for: 11 -> 7; matrix products, arithmetic and copies ran while one was open for 0% -> 0% of each run, Pallas kernels for 12% -> 15%
where the time goes in v5:
time: 56.5 us; the launch traced here: 56.3 us
  starting transfers between devices  24 us (42%)
  waiting for transfers between devices  16.5 us (29%)
  Pallas kernels  14 us (25%)
  local copies, waits for them, and re-layouts  1.09 us (2%)
  between operations  0.79 us (1%)
    ppermute x17, waiting for transfers between devices, send(): return lax.ppermute(value, ('dp', 'cuts'), pairs)  14.1 us
    ppermute x17, starting transfers between devices, send(): return lax.ppermute(value, ('dp', 'cuts'), pairs)  13.5 us
    ppermute x6, starting transfers between devices, along(): lax.ppermute(value, 'cuts', [(c, (c + 2 * k) % cut_count) for c in range(...  10.5 us
    pallas_call x1, Pallas kernels, backward(): pl.pallas_call(functools.partial(backward_kernel, weight.shape[2] // (2 *...  5 us
    pallas_call x1, Pallas kernels, forward(): pl.pallas_call(functools.partial(forward_kernel, nz, capacity), in_specs=...  4.04 us
    pallas_call x1, Pallas kernels, backward_here(): pl.pallas_call(functools.partial(backward_here_kernel, weight.shape[2] //...  2.36 us
    ppermute x6, waiting for transfers between devices, along(): lax.ppermute(value, 'cuts', [(c, (c + 2 * k) % cut_count) for c in range(...  2.34 us
  transfers between devices with their start and end apart: 23, of which 7 were waited for; matrix products, arithmetic and copies ran while one was open for 0% of the time, Pallas kernels for 15%

profile of v5, /device:TPU:0, one launch (start us, length us, event | category | flops | bytes accessed | tf_op | source)
XLA Modules:
  0.0 56.3 jit_solution(14200529677031177063)
XLA Ops:
  0.6 1.0 %copy-done = bf16[1,256,1024]{2,1,0:T(8,128)(2,1)S(1)} copy-done((bf16[1,256,1024]{2,1,0:T(8,128)(2,1)S(1)}, bf16[1,256,1024]{2,1,0:T(8,128)(2,1)}, u32[]{:S(2)}) %copy-start) | copy-done | bytes 524312
  1.7 4.0 %forward_rows.1 = (bf16[4,2,2,64,384]{4,3,2,1,0:T(8,128)(2,1)S(1)}, bf16[4,2,2,64,384]{4,3,2,1,0:T(8,128)(2,1)S(1)}) custom-call(bf16[1,256,1024]{2,1,0:T(8,128)(2,1)S(1)} %copy-done, bf16[1,1024,3072]{2,1,0:T(8,128)(2,1)} %weight_ref.5), custom_call_target="tpu_custom_call" | custom-call | flops 1610612736 | bytes 8388608 | tf_op jit(solution)/shard_map/forward_rows/pallas_call | solution.py:112
  5.7 0.5 collective-permute-start
  6.3 1.9 %collective-permute-done.got_ref = bf16[4,2,2,64,384]{4,3,2,1,0:T(8,128)(2,1)S(1)} collective-permute-done((bf16[4,2,2,64,384]{4,3,2,1,0:T(8,128)(2,1)S(1)}, bf16[4,2,2,64,384]{4,3,2,1,0:T(8,128)(2,1)S(1)}, u32[]{:S(2)}, u32[]{:S(2)}) %collective-permute-start) | collective-permute-done | bytes 786464 | tf_op jit(solution)/shard_map/ppermute | solution.py:447
  8.2 0.7 %spread_rows.1 = (bf16[5,128,384]{2,1,0:T(8,128)(2,1)S(1)}, f32[4,128,384]{2,1,0:T(8,128)S(1)}, bf16[656,384]{1,0:T(8,128)(2,1)S(1)}, f32[4,128,384]{2,1,0:T(8,128)S(1)}) custom-call(f32[4,128]{1,0:T(4,128)S(1)} %pad_add_fusion.meta_ref, bf16[4,2,2,64,384]{4,3,2,1,0:T(8,128)(2,1)S(1)} %get-tuple-element.33.keep_ref, ...), custom_call_target="tpu_custom_call" | custom-call | flops 201326592 | bytes 4718592 | tf_op jit(solution)/shard_map/spread_rows/pallas_call | solution.py:182
  8.9 3.0 %collective-permute-start.2 = (bf16[656,384]{1,0:T(8,128)(2,1)S(1)}, bf16[656,384]{1,0:T(8,128)(2,1)S(1)}, u32[]{:S(2)}, u32[]{:S(2)}) collective-permute-start(bf16[656,384]{1,0:T(8,128)(2,1)S(1)} %get-tuple-element.40), channel_id=1, source_target_pairs={{0,16},{1,17},{2,18},{3,19},{4,20},{5,21},{6,22},{7,23},{8,24},{9,... | collective-permute-start | bytes 1511432 | tf_op jit(solution)/shard_map/ppermute | solution.py:447
  11.9 1.5 %collective-permute-start.1 = (bf16[5,128,384]{2,1,0:T(8,128)(2,1)S(1)}, bf16[5,128,384]{2,1,0:T(8,128)(2,1)S(1)}, u32[]{:S(2)}, u32[]{:S(2)}) collective-permute-start(bf16[5,128,384]{2,1,0:T(8,128)(2,1)S(1)} %get-tuple-element.38), channel_id=1, source_target_pairs={{0,1},{1,0},{2,3},{3,2},{4,5},{5,4},{6,7},{7,6},{8,9},{9,8},{10,11... | collective-permute-start | bytes 1474568 | tf_op jit(solution)/shard_map/ppermute | solution.py:447
  13.4 3.6 %collective-permute-start.12 = (bf16[128,384]{1,0:T(8,128)(2,1)S(1)}, bf16[128,384]{1,0:T(8,128)(2,1)S(1)}, u32[]{:S(2)}, u32[]{:S(2)}) collective-permute-start(bf16[128,384]{1,0:T(8,128)(2,1)S(1)} %copy-done.1), channel_id=1, source_target_pairs={{0,6},{1,7},{2,0},{3,1},{4,2},{5,3},{6,4},{7,5},{8,14},{9,15},{10,... | collective-permute-start | bytes 294920 | tf_op jit(solution)/shard_map/ppermute | solution.py:450
  17.0 1.0 %collective-permute-start.10 = (bf16[128,384]{1,0:T(8,128)(2,1)S(1)}, bf16[128,384]{1,0:T(8,128)(2,1)S(1)}, u32[]{:S(2)}, u32[]{:S(2)}) collective-permute-start(bf16[128,384]{1,0:T(8,128)(2,1)S(1)} %copy-done.1), channel_id=1, source_target_pairs={{0,2},{1,3},{2,4},{3,5},{4,6},{5,7},{6,0},{7,1},{8,10},{9,11},{10,... | collective-permute-start | bytes 294920 | tf_op jit(solution)/shard_map/ppermute | solution.py:450
  18.0 6.9 %collective-permute-done.1.x_got = bf16[5,128,384]{2,1,0:T(8,128)(2,1)S(1)} collective-permute-done((bf16[5,128,384]{2,1,0:T(8,128)(2,1)S(1)}, bf16[5,128,384]{2,1,0:T(8,128)(2,1)S(1)}, u32[]{:S(2)}, u32[]{:S(2)}) %collective-permute-start.1) | collective-permute-done | bytes 491552 | tf_op jit(solution)/shard_map/ppermute | solution.py:447
  24.9 0.6 %first_sum.1 = (f32[2,128,384]{2,1,0:T(8,128)S(1)}, bf16[320,384]{1,0:T(8,128)(2,1)S(1)}, f32[2,128,384]{2,1,0:T(8,128)S(1)}, bf16[320,384]{1,0:T(8,128)(2,1)S(1...) custom-call(bf16[128,384]{1,0:T(8,128)(2,1)S(1)} %copy-done.1, f32[4,128]{1,0:T(4,128)S(1)} %pad_add_fusion.meta_ref, ...), custom_call_target="tpu_custom_call" | custom-call | flops 1000000000 | tf_op jit(solution)/shard_map/first_sum/pallas_call | solution.py:233
  25.5 0.6 %collective-permute-start.5 = (bf16[320,384]{1,0:T(8,128)(2,1)S(1)}, bf16[320,384]{1,0:T(8,128)(2,1)S(1)}, u32[]{:S(2)}, u32[]{:S(2)}) collective-permute-start(bf16[320,384]{1,0:T(8,128)(2,1)S(1)} %get-tuple-element.45), channel_id=1, source_target_pairs={{0,16},{1,17},{2,18},{3,19},{4,20},{5,21},{6,22},{7,23},{8,24},{9,... | collective-permute-start | bytes 737288 | tf_op jit(solution)/shard_map/ppermute | solution.py:447
  26.1 1.5 %collective-permute-start.6 = (bf16[320,384]{1,0:T(8,128)(2,1)S(1)}, bf16[320,384]{1,0:T(8,128)(2,1)S(1)}, u32[]{:S(2)}, u32[]{:S(2)}) collective-permute-start(bf16[320,384]{1,0:T(8,128)(2,1)S(1)} %get-tuple-element.46), channel_id=1, source_target_pairs={{0,1},{1,0},{2,3},{3,2},{4,5},{5,4},{6,7},{7,6},{8,9},{9,8},{10,11... | collective-permute-start | bytes 737288 | tf_op jit(solution)/shard_map/ppermute | solution.py:447
  27.6 0.6 %collective-permute-start.13 = (bf16[3,128,384]{2,1,0:T(8,128)(2,1)S(1)}, bf16[3,128,384]{2,1,0:T(8,128)(2,1)S(1)}, u32[]{:S(2)}, u32[]{:S(2)}) collective-permute-start(bf16[3,128,384]{2,1,0:T(8,128)(2,1)S(1)} %stack_blocks.1.refs_0_), channel_id=1, source_target_pairs={{0,1},{1,0},{2,3},{3,2},{4,5},{5,4},{6,7},{7,6},{8,9},{9,8},{10,11... | collective-permute-start | bytes 884744 | tf_op jit(solution)/shard_map/ppermute | solution.py:447
  28.2 1.5 %collective-permute-start.14 = (bf16[3,128,384]{2,1,0:T(8,128)(2,1)S(1)}, bf16[3,128,384]{2,1,0:T(8,128)(2,1)S(1)}, u32[]{:S(2)}, u32[]{:S(2)}) collective-permute-start(bf16[3,128,384]{2,1,0:T(8,128)(2,1)S(1)} %stack_blocks.1.refs_0_), channel_id=1, source_target_pairs={{0,16},{1,17},{2,18},{3,19},{4,20},{5,21},{6,22},{7,23},{8,24},{9,... | collective-permute-start | bytes 884744 | tf_op jit(solution)/shard_map/ppermute | solution.py:447
  29.7 4.7 %collective-permute-done.5.by_y = bf16[320,384]{1,0:T(8,128)(2,1)S(1)} collective-permute-done((bf16[320,384]{1,0:T(8,128)(2,1)S(1)}, bf16[320,384]{1,0:T(8,128)(2,1)S(1)}, u32[]{:S(2)}, u32[]{:S(2)}) %collective-permute-start.5) | collective-permute-done | bytes 245792 | tf_op jit(solution)/shard_map/ppermute | solution.py:447
  34.4 0.5 collective-permute-done.6.by_x
  35.0 0.5 second_sum.1
  35.5 1.6 %collective-permute-start.8 = (bf16[128,384]{1,0:T(8,128)(2,1)S(1)}, bf16[128,384]{1,0:T(8,128)(2,1)S(1)}, u32[]{:S(2)}, u32[]{:S(2)}) collective-permute-start(bf16[128,384]{1,0:T(8,128)(2,1)S(1)} %get-tuple-element.48), channel_id=1, source_target_pairs={{0,2},{1,3},{2,4},{3,5},{4,6},{5,7},{6,0},{7,1},{8,10},{9,11},{10,... | collective-permute-start | bytes 294920 | tf_op jit(solution)/shard_map/ppermute | solution.py:450
  37.1 2.2 %collective-permute-start.9 = (bf16[128,384]{1,0:T(8,128)(2,1)S(1)}, bf16[128,384]{1,0:T(8,128)(2,1)S(1)}, u32[]{:S(2)}, u32[]{:S(2)}) collective-permute-start(bf16[128,384]{1,0:T(8,128)(2,1)S(1)} %get-tuple-element.49), channel_id=1, source_target_pairs={{0,6},{1,7},{2,0},{3,1},{4,2},{5,3},{6,4},{7,5},{8,14},{9,15},{10,... | collective-permute-start | bytes 294920 | tf_op jit(solution)/shard_map/ppermute | solution.py:450
  39.4 1.5 %collective-permute-start.15 = (bf16[2,128,384]{2,1,0:T(8,128)(2,1)S(1)}, bf16[2,128,384]{2,1,0:T(8,128)(2,1)S(1)}, u32[]{:S(2)}, u32[]{:S(2)}) collective-permute-start(bf16[2,128,384]{2,1,0:T(8,128)(2,1)S(1)} %slice.8), channel_id=1, source_target_pairs={{0,16},{1,17},{2,18},{3,19},{4,20},{5,21},{6,22},{7,23},{8,24},{9,... | collective-permute-start | bytes 589832 | tf_op jit(solution)/shard_map/ppermute | solution.py:447
  41.0 0.3 collective-permute-start.17
  41.3 1.5 %collective-permute-done.8.refs_4_.refs_0_ = bf16[128,384]{1,0:T(8,128)(2,1)S(1)} collective-permute-done((bf16[128,384]{1,0:T(8,128)(2,1)S(1)}, bf16[128,384]{1,0:T(8,128)(2,1)S(1)}, u32[]{:S(2)}, u32[]{:S(2)}) %collective-permute-start.8) | collective-permute-done | bytes 98336 | tf_op jit(solution)/shard_map/ppermute | solution.py:450
  42.8 1.5 %collective-permute-start.16 = (bf16[1,128,384]{2,1,0:T(8,128)(2,1)S(1)}, bf16[1,128,384]{2,1,0:T(8,128)(2,1)S(1)}, u32[]{:S(2)}, u32[]{:S(2)}) collective-permute-start(bf16[1,128,384]{2,1,0:T(8,128)(2,1)S(1)} %slice.9), channel_id=1, source_target_pairs={{0,1},{1,0},{2,3},{3,2},{4,5},{5,4},{6,7},{7,6},{8,9},{9,8},{10,11... | collective-permute-start | bytes 294920 | tf_op jit(solution)/shard_map/ppermute | solution.py:447
  44.3 0.5 collective-permute-start.18
  44.8 2.4 %backward_here.1 = (f32[256,1024]{1,0:T(8,128)S(1)}, bf16[1,1024,3072]{2,1,0:T(8,128)(2,1)}, bf16[1024,256]{1,0:T(8,128)(2,1)S(1)}, bf16[4,64,128]{2,1,0:T(8,128)(2,1)S(1)}, f32[4,64,128]{2,1,0:T(8,128)S(1)}) custom-call(bf16[1,256,1024]{2,1,0:T(8,128)(2,1)S(1)} %copy-done, bf16[1,1024,3072]{2,1,0:T(8,128)(2,1)S(1)} %bitcast.4, ...), custom_call_target="tpu_custom_call" | custom-call | flops 2000000000 | tf_op jit(solution)/shard_map/backward_here/pallas_call | solution.py:337
  47.2 0.1 collective-permute-start.20
  47.4 0.4 collective-permute-start.21
  47.8 2.0 %collective-permute-start.22 = (bf16[128,384]{1,0:T(8,128)(2,1)S(1)}, bf16[128,384]{1,0:T(8,128)(2,1)S(1)}, u32[]{:S(2)}, u32[]{:S(2)}) collective-permute-start(bf16[128,384]{1,0:T(8,128)(2,1)S(1)} %get-tuple-element.60), channel_id=1, source_target_pairs={{0,4},{1,5},{2,6},{3,7},{4,0},{5,1},{6,2},{7,3},{8,12},{9,13},{10,... | collective-permute-start | bytes 294920 | tf_op jit(solution)/shard_map/ppermute | solution.py:450
  49.8 5.0 %backward_rows.1 = (bf16[1,256,1024]{2,1,0:T(8,128)(2,1)}, bf16[1,1024,3072]{2,1,0:T(8,128)(2,1)}, f32[8,128]{1,0:T(8,128)S(1)}) custom-call(bf16[1,1024,3072]{2,1,0:T(8,128)(2,1)S(1)} %bitcast.4, f32[256,1024]{1,0:T(8,128)S(1)} %get-tuple-element.50.part_ref, bf16[1024,256]{1,0:T(8,128)(2,1)S(1)} %get-tuple-element.51.turned, ...), custom_call_target="tpu_custom_call", output_to_operand_aliasing={{1}: (15, {})} | custom-call | flops 100000000 | tf_op jit(solution)/shard_map/backward_rows/pallas_call | solution.py:393
  54.8 0.8 %collective-permute-done.22.refs_1_ = bf16[128,384]{1,0:T(8,128)(2,1)S(1)} collective-permute-done((bf16[128,384]{1,0:T(8,128)(2,1)S(1)}, bf16[128,384]{1,0:T(8,128)(2,1)S(1)}, u32[]{:S(2)}, u32[]{:S(2)}) %collective-permute-start.22) | collective-permute-done | bytes 98336 | tf_op jit(solution)/shard_map/ppermute | solution.py:450
  55.6 0.7 %last_sum.1 = bf16[128,384]{1,0:T(8,128)(2,1)} custom-call(f32[8,128]{1,0:T(8,128)S(1)} %get-tuple-element.58._, f32[128,384]{1,0:T(8,128)S(1)} %get-tuple-element.59.first_ref, bf16[128,384]{1,0:T(8,128)(2,1)S(1)} %collective-permute-done.8.refs_4_.refs_0_, bf16[128,384]{1,0:T(8,128)(2,1)S(1)} %collective-permute-done.22.refs_1_, ...), custom_call_target="tpu_custom_call" | custom-call | flops 1000000000 | tf_op jit(solution)/shard_map/last_sum/pallas_call | solution.py:425
  (39 shorter events, 0.2 us)
Async XLA Ops:
  0.6 1.0 %copy-start = (bf16[1,256,1024]{2,1,0:T(8,128)(2,1)S(1)}, bf16[1,256,1024]{2,1,0:T(8,128)(2,1)}, u32[]{:S(2)}) copy-start(bf16[1,256,1024]{2,1,0:T(8,128)(2,1)} %hidden_ref.3) | copy-start | bytes 1572868
  1.7 4.6 %copy-start.2 = (s32[128,2]{0,1:T(2,128)S(1)}, s32[128,2]{0,1:T(2,128)}, u32[]{:S(2)}) copy-start(s32[128,2]{0,1:T(2,128)} %param.7) | copy-start | bytes 3076
  1.7 4.6 %copy-start.3 = (f32[128,2]{0,1:T(2,128)S(1)}, f32[128,2]{0,1:T(2,128)}, u32[]{:S(2)}) copy-start(f32[128,2]{0,1:T(2,128)} %param.8) | copy-start | bytes 3076
  1.7 6.5 %copy-start.1 = (bf16[128,384]{1,0:T(8,128)(2,1)S(1)}, bf16[128,384]{1,0:T(8,128)(2,1)}, u32[]{:S(2)}) copy-start(bf16[128,384]{1,0:T(8,128)(2,1)} %grad_ref.3) | copy-start | bytes 294916
  5.7 2.4 %collective-permute-start = (bf16[4,2,2,64,384]{4,3,2,1,0:T(8,128)(2,1)S(1)}, bf16[4,2,2,64,384]{4,3,2,1,0:T(8,128)(2,1)S(1)}, u32[]{:S(2)}, u32[]{:S(2)}) collective-permute-start(bf16[4,2,2,64,384]{4,3,2,1,0:T(8,128)(2,1)S(1)} %get-tuple-element.36), channel_id=1, source_target_pairs={{0,8},{1,9},{2,10},{3,11},{4,12},{5,13},{6,14},{7,15},{8,0},{9,1},... | collective-permute-start | bytes 2359304 | tf_op jit(solution)/shard_map/ppermute | solution.py:447
  6.3 38.5 %slice-start = ((s8[6291456]{0:T(1024)(128)(4,1)}), s8[4194304]{0:T(1024)(128)(4,1)S(1)}, s32[]{:S(2)}) async-start(s8[6291456]{0:T(1024)(128)(4,1)} %bitcast.3), calls=%async_computation | async-start | bytes 8388608
  8.9 15.9 %collective-permute-start.2 = (bf16[656,384]{1,0:T(8,128)(2,1)S(1)}, bf16[656,384]{1,0:T(8,128)(2,1)S(1)}, u32[]{:S(2)}, u32[]{:S(2)}) collective-permute-start(bf16[656,384]{1,0:T(8,128)(2,1)S(1)} %get-tuple-element.40), channel_id=1, source_target_pairs={{0,16},{1,17},{2,18},{3,19},{4,20},{5,21},{6,22},{7,23},{8,24},{9,... | collective-permute-start | bytes 1511432 | tf_op jit(solution)/shard_map/ppermute | solution.py:447
  11.9 13.0 %collective-permute-start.1 = (bf16[5,128,384]{2,1,0:T(8,128)(2,1)S(1)}, bf16[5,128,384]{2,1,0:T(8,128)(2,1)S(1)}, u32[]{:S(2)}, u32[]{:S(2)}) collective-permute-start(bf16[5,128,384]{2,1,0:T(8,128)(2,1)S(1)} %get-tuple-element.38), channel_id=1, source_target_pairs={{0,1},{1,0},{2,3},{3,2},{4,5},{5,4},{6,7},{7,6},{8,9},{9,8},{10,11... | collective-permute-start | bytes 1474568 | tf_op jit(solution)/shard_map/ppermute | solution.py:447
  13.4 14.2 %collective-permute-start.12 = (bf16[128,384]{1,0:T(8,128)(2,1)S(1)}, bf16[128,384]{1,0:T(8,128)(2,1)S(1)}, u32[]{:S(2)}, u32[]{:S(2)}) collective-permute-start(bf16[128,384]{1,0:T(8,128)(2,1)S(1)} %copy-done.1), channel_id=1, source_target_pairs={{0,6},{1,7},{2,0},{3,1},{4,2},{5,3},{6,4},{7,5},{8,14},{9,15},{10,... | collective-permute-start | bytes 294920 | tf_op jit(solution)/shard_map/ppermute | solution.py:450
  17.0 10.6 %collective-permute-start.11 = (bf16[128,384]{1,0:T(8,128)(2,1)S(1)}, bf16[128,384]{1,0:T(8,128)(2,1)S(1)}, u32[]{:S(2)}, u32[]{:S(2)}) collective-permute-start(bf16[128,384]{1,0:T(8,128)(2,1)S(1)} %copy-done.1), channel_id=1, source_target_pairs={{0,4},{1,5},{2,6},{3,7},{4,0},{5,1},{6,2},{7,3},{8,12},{9,13},{10,... | collective-permute-start | bytes 294920 | tf_op jit(solution)/shard_map/ppermute | solution.py:450
  17.0 10.6 %collective-permute-start.10 = (bf16[128,384]{1,0:T(8,128)(2,1)S(1)}, bf16[128,384]{1,0:T(8,128)(2,1)S(1)}, u32[]{:S(2)}, u32[]{:S(2)}) collective-permute-start(bf16[128,384]{1,0:T(8,128)(2,1)S(1)} %copy-done.1), channel_id=1, source_target_pairs={{0,2},{1,3},{2,4},{3,5},{4,6},{5,7},{6,0},{7,1},{8,10},{9,11},{10,... | collective-permute-start | bytes 294920 | tf_op jit(solution)/shard_map/ppermute | solution.py:450
  25.5 9.0 %collective-permute-start.5 = (bf16[320,384]{1,0:T(8,128)(2,1)S(1)}, bf16[320,384]{1,0:T(8,128)(2,1)S(1)}, u32[]{:S(2)}, u32[]{:S(2)}) collective-permute-start(bf16[320,384]{1,0:T(8,128)(2,1)S(1)} %get-tuple-element.45), channel_id=1, source_target_pairs={{0,16},{1,17},{2,18},{3,19},{4,20},{5,21},{6,22},{7,23},{8,24},{9,... | collective-permute-start | bytes 737288 | tf_op jit(solution)/shard_map/ppermute | solution.py:447
  26.1 8.9 %collective-permute-start.6 = (bf16[320,384]{1,0:T(8,128)(2,1)S(1)}, bf16[320,384]{1,0:T(8,128)(2,1)S(1)}, u32[]{:S(2)}, u32[]{:S(2)}) collective-permute-start(bf16[320,384]{1,0:T(8,128)(2,1)S(1)} %get-tuple-element.46), channel_id=1, source_target_pairs={{0,1},{1,0},{2,3},{3,2},{4,5},{5,4},{6,7},{7,6},{8,9},{9,8},{10,11... | collective-permute-start | bytes 737288 | tf_op jit(solution)/shard_map/ppermute | solution.py:447
  27.6 17.2 %slice-start.1 = ((s8[6291456]{0:T(1024)(128)(4,1)}), s8[2097152]{0:T(1024)(128)(4,1)S(1)}, s32[]{:S(2)}) async-start(s8[6291456]{0:T(1024)(128)(4,1)} %bitcast.3), calls=%async_computation.1 | async-start | bytes 4194304
  27.6 11.8 %collective-permute-start.13 = (bf16[3,128,384]{2,1,0:T(8,128)(2,1)S(1)}, bf16[3,128,384]{2,1,0:T(8,128)(2,1)S(1)}, u32[]{:S(2)}, u32[]{:S(2)}) collective-permute-start(bf16[3,128,384]{2,1,0:T(8,128)(2,1)S(1)} %stack_blocks.1.refs_0_), channel_id=1, source_target_pairs={{0,1},{1,0},{2,3},{3,2},{4,5},{5,4},{6,7},{7,6},{8,9},{9,8},{10,11... | collective-permute-start | bytes 884744 | tf_op jit(solution)/shard_map/ppermute | solution.py:447
  28.2 11.2 %collective-permute-start.14 = (bf16[3,128,384]{2,1,0:T(8,128)(2,1)S(1)}, bf16[3,128,384]{2,1,0:T(8,128)(2,1)S(1)}, u32[]{:S(2)}, u32[]{:S(2)}) collective-permute-start(bf16[3,128,384]{2,1,0:T(8,128)(2,1)S(1)} %stack_blocks.1.refs_0_), channel_id=1, source_target_pairs={{0,16},{1,17},{2,18},{3,19},{4,20},{5,21},{6,22},{7,23},{8,24},{9,... | collective-permute-start | bytes 884744 | tf_op jit(solution)/shard_map/ppermute | solution.py:447
  29.7 11.3 %collective-permute-start.4 = (bf16[3,128,384]{2,1,0:T(8,128)(2,1)S(1)}, bf16[3,128,384]{2,1,0:T(8,128)(2,1)S(1)}, u32[]{:S(2)}, u32[]{:S(2)}) collective-permute-start(bf16[3,128,384]{2,1,0:T(8,128)(2,1)S(1)} %get-tuple-element.42.refs_0_), channel_id=1, source_target_pairs={{0,8},{1,9},{2,10},{3,11},{4,12},{5,13},{6,14},{7,15},{8,0},{9,1},... | collective-permute-start | bytes 884744 | tf_op jit(solution)/shard_map/ppermute | solution.py:447
  34.4 2.7 %collective-permute-start.3 = (f32[2,4,128]{2,1,0:T(4,128)S(1)}, f32[2,4,128]{2,1,0:T(4,128)S(1)}, u32[]{:S(2)}, u32[]{:S(2)}) collective-permute-start(f32[2,4,128]{2,1,0:T(4,128)S(1)} %get-tuple-element.41.metas), channel_id=1, source_target_pairs={{0,8},{1,9},{2,10},{3,11},{4,12},{5,13},{6,14},{7,15},{8,0},{9,1},... | collective-permute-start | bytes 12296 | tf_op jit(solution)/shard_map/ppermute | solution.py:447
  35.5 7.3 %collective-permute-start.8 = (bf16[128,384]{1,0:T(8,128)(2,1)S(1)}, bf16[128,384]{1,0:T(8,128)(2,1)S(1)}, u32[]{:S(2)}, u32[]{:S(2)}) collective-permute-start(bf16[128,384]{1,0:T(8,128)(2,1)S(1)} %get-tuple-element.48), channel_id=1, source_target_pairs={{0,2},{1,3},{2,4},{3,5},{4,6},{5,7},{6,0},{7,1},{8,10},{9,11},{10,... | collective-permute-start | bytes 294920 | tf_op jit(solution)/shard_map/ppermute | solution.py:450
  37.1 7.2 %collective-permute-start.9 = (bf16[128,384]{1,0:T(8,128)(2,1)S(1)}, bf16[128,384]{1,0:T(8,128)(2,1)S(1)}, u32[]{:S(2)}, u32[]{:S(2)}) collective-permute-start(bf16[128,384]{1,0:T(8,128)(2,1)S(1)} %get-tuple-element.49), channel_id=1, source_target_pairs={{0,6},{1,7},{2,0},{3,1},{4,2},{5,3},{6,4},{7,5},{8,14},{9,15},{10,... | collective-permute-start | bytes 294920 | tf_op jit(solution)/shard_map/ppermute | solution.py:450
  39.4 4.9 %collective-permute-start.7 = (bf16[128,384]{1,0:T(8,128)(2,1)S(1)}, bf16[128,384]{1,0:T(8,128)(2,1)S(1)}, u32[]{:S(2)}, u32[]{:S(2)}) collective-permute-start(bf16[128,384]{1,0:T(8,128)(2,1)S(1)} %get-tuple-element.47.refs_2_), channel_id=1, source_target_pairs={{0,8},{1,9},{2,10},{3,11},{4,12},{5,13},{6,14},{7,15},{8,0},{9,1},... | collective-permute-start | bytes 294920 | tf_op jit(solution)/shard_map/ppermute | solution.py:447
  39.4 7.8 %collective-permute-start.15 = (bf16[2,128,384]{2,1,0:T(8,128)(2,1)S(1)}, bf16[2,128,384]{2,1,0:T(8,128)(2,1)S(1)}, u32[]{:S(2)}, u32[]{:S(2)}) collective-permute-start(bf16[2,128,384]{2,1,0:T(8,128)(2,1)S(1)} %slice.8), channel_id=1, source_target_pairs={{0,16},{1,17},{2,18},{3,19},{4,20},{5,21},{6,22},{7,23},{8,24},{9,... | collective-permute-start | bytes 589832 | tf_op jit(solution)/shard_map/ppermute | solution.py:447
  41.0 6.8 %collective-permute-start.17 = (bf16[3,128,384]{2,1,0:T(8,128)(2,1)S(1)}, bf16[3,128,384]{2,1,0:T(8,128)(2,1)S(1)}, u32[]{:S(2)}, u32[]{:S(2)}) collective-permute-start(bf16[3,128,384]{2,1,0:T(8,128)(2,1)S(1)} %stack_blocks.1.refs_0_), channel_id=1, source_target_pairs={{0,8},{1,9},{2,10},{3,11},{4,12},{5,13},{6,14},{7,15},{8,0},{9,1},... | collective-permute-start | bytes 884744 | tf_op jit(solution)/shard_map/ppermute | solution.py:447
  42.8 4.6 %collective-permute-start.16 = (bf16[1,128,384]{2,1,0:T(8,128)(2,1)S(1)}, bf16[1,128,384]{2,1,0:T(8,128)(2,1)S(1)}, u32[]{:S(2)}, u32[]{:S(2)}) collective-permute-start(bf16[1,128,384]{2,1,0:T(8,128)(2,1)S(1)} %slice.9), channel_id=1, source_target_pairs={{0,1},{1,0},{2,3},{3,2},{4,5},{5,4},{6,7},{7,6},{8,9},{9,8},{10,11... | collective-permute-start | bytes 294920 | tf_op jit(solution)/shard_map/ppermute | solution.py:447
  44.3 5.5 %collective-permute-start.19 = (bf16[3,128,384]{2,1,0:T(8,128)(2,1)S(1)}, bf16[3,128,384]{2,1,0:T(8,128)(2,1)S(1)}, u32[]{:S(2)}, u32[]{:S(2)}) collective-permute-start(bf16[3,128,384]{2,1,0:T(8,128)(2,1)S(1)} %collective-permute-done.14.refs_2_), channel_id=1, source_target_pairs={{0,8},{1,9},{2,10},{3,11},{4,12},{5,13},{6,14},{7,15},{8,0},{9,1},... | collective-permute-start | bytes 884744 | tf_op jit(solution)/shard_map/ppermute | solution.py:447
  44.3 5.5 %collective-permute-start.18 = (bf16[3,128,384]{2,1,0:T(8,128)(2,1)S(1)}, bf16[3,128,384]{2,1,0:T(8,128)(2,1)S(1)}, u32[]{:S(2)}, u32[]{:S(2)}) collective-permute-start(bf16[3,128,384]{2,1,0:T(8,128)(2,1)S(1)} %collective-permute-done.13.refs_1_), channel_id=1, source_target_pairs={{0,8},{1,9},{2,10},{3,11},{4,12},{5,13},{6,14},{7,15},{8,0},{9,1},... | collective-permute-start | bytes 884744 | tf_op jit(solution)/shard_map/ppermute | solution.py:447
  47.2 2.6 %collective-permute-start.20 = (bf16[2,128,384]{2,1,0:T(8,128)(2,1)S(1)}, bf16[2,128,384]{2,1,0:T(8,128)(2,1)S(1)}, u32[]{:S(2)}, u32[]{:S(2)}) collective-permute-start(bf16[2,128,384]{2,1,0:T(8,128)(2,1)S(1)} %collective-permute-done.15.refs_3_), channel_id=1, source_target_pairs={{0,8},{1,9},{2,10},{3,11},{4,12},{5,13},{6,14},{7,15},{8,0},{9,1},... | collective-permute-start | bytes 589832 | tf_op jit(solution)/shard_map/ppermute | solution.py:447
  47.4 2.4 %collective-permute-start.21 = (bf16[1,128,384]{2,1,0:T(8,128)(2,1)S(1)}, bf16[1,128,384]{2,1,0:T(8,128)(2,1)S(1)}, u32[]{:S(2)}, u32[]{:S(2)}) collective-permute-start(bf16[1,128,384]{2,1,0:T(8,128)(2,1)S(1)} %collective-permute-done.16.refs_4_), channel_id=1, source_target_pairs={{0,8},{1,9},{2,10},{3,11},{4,12},{5,13},{6,14},{7,15},{8,0},{9,1},... | collective-permute-start | bytes 294920 | tf_op jit(solution)/shard_map/ppermute | solution.py:447
  47.8 7.9 %collective-permute-start.22 = (bf16[128,384]{1,0:T(8,128)(2,1)S(1)}, bf16[128,384]{1,0:T(8,128)(2,1)S(1)}, u32[]{:S(2)}, u32[]{:S(2)}) collective-permute-start(bf16[128,384]{1,0:T(8,128)(2,1)S(1)} %get-tuple-element.60), channel_id=1, source_target_pairs={{0,4},{1,5},{2,6},{3,7},{4,0},{5,1},{6,2},{7,3},{8,12},{9,13},{10,... | collective-permute-start | bytes 294920 | tf_op jit(solution)/shard_map/ppermute | solution.py:450

commit v6 on v5

--- a/solution.py
+++ b/solution.py
@@ -369,6 +369,11 @@
             for j, rows in enumerate((far[k - 1], far_x[k - 1], far_y[k - 1], cross)):
                 put(rows_ref, hots, cols, j % 2, 2 * (j // 2) + dc, rows)
         rows, column = rows_ref[...], columns(nz, k, feat)
+        if k > 2:
+            leaving.pop(0).wait()
+        made[k % 2] = jnp.dot(turned[...], rows, preferred_element_type=F32).astype(BF)
+        leaving.append(pltpu.make_async_copy(made.at[k % 2], down_out.at[0, :, column], sems.at[k % 2]))
+        leaving[-1].start()
         part = (part_ref if k == 1 else total)[...] + times_transposed(rows, weight_ref[0, :, column])
         if k < nz - 1:
             total[...] = part
@@ -376,11 +381,6 @@
             done[...] = part.astype(BF)
             leaving.append(pltpu.make_async_copy(done, hid_out.at[0], sems.at[2]))
             leaving[-1].start()
-        if k > 2:
-            leaving.pop(0).wait()
-        made[k % 2] = jnp.dot(turned[...], rows, preferred_element_type=F32).astype(BF)
-        leaving.append(pltpu.make_async_copy(made.at[k % 2], down_out.at[0, :, column], sems.at[k % 2]))
-        leaving[-1].start()
     for copy in leaving:
         copy.wait()
 
@@ -470,7 +470,7 @@
         hidden, down_weight, metas, send(metas, 1, 0), (near_by, other), (cross, send(cross, 1, 0)), (sums[1], sums[-1])
     )
     parts = [far, far_x, far_y, low, high]
-    after = [None, None, None, here[0], sums[-1]]
+    after = [None, None, None, here[0], None]
     grads = parts + [
         send(p if held is None else lax.optimization_barrier((p, held))[0], 1, 0) for p, held in zip(parts, after)
     ]

time: 56.5 us -> 56.5 us (level)
  no operation moved by 1% of the time
where the time goes in v6:
time: 56.5 us; the launch traced here: 56.3 us
  starting transfers between devices  24 us (42%)
  waiting for transfers between devices  16.7 us (30%)
  Pallas kernels  13.8 us (24%)
  local copies, waits for them, and re-layouts  1.09 us (2%)
  between operations  0.79 us (1%)
    ppermute x17, waiting for transfers between devices, send(): return lax.ppermute(value, ('dp', 'cuts'), pairs)  14.1 us
    ppermute x17, starting transfers between devices, send(): return lax.ppermute(value, ('dp', 'cuts'), pairs)  13.5 us
    ppermute x6, starting transfers between devices, along(): lax.ppermute(value, 'cuts', [(c, (c + 2 * k) % cut_count) for c in range(...  10.5 us
    pallas_call x1, Pallas kernels, backward(): pl.pallas_call(functools.partial(backward_kernel, weight.shape[2] // (2 *...  4.8 us
    pallas_call x1, Pallas kernels, forward(): pl.pallas_call(functools.partial(forward_kernel, nz, capacity), in_specs=...  4.04 us
    ppermute x6, waiting for transfers between devices, along(): lax.ppermute(value, 'cuts', [(c, (c + 2 * k) % cut_count) for c in range(...  2.54 us
    pallas_call x1, Pallas kernels, backward_here(): pl.pallas_call(functools.partial(backward_here_kernel, weight.shape[2] //...  2.36 us
  transfers between devices with their start and end apart: 23, of which 7 were waited for; matrix products, arithmetic and copies ran while one was open for 0% of the time, Pallas kernels for 15%

profile of v6, /device:TPU:0, one launch (start us, length us, event | category | flops | bytes accessed | tf_op | source)
XLA Modules:
  0.0 56.3 jit_solution(2892509789259251253)
XLA Ops:
  0.6 1.0 %copy-done = bf16[1,256,1024]{2,1,0:T(8,128)(2,1)S(1)} copy-done((bf16[1,256,1024]{2,1,0:T(8,128)(2,1)S(1)}, bf16[1,256,1024]{2,1,0:T(8,128)(2,1)}, u32[]{:S(2)}) %copy-start) | copy-done | bytes 524312
  1.7 4.0 %forward_rows.1 = (bf16[4,2,2,64,384]{4,3,2,1,0:T(8,128)(2,1)S(1)}, bf16[4,2,2,64,384]{4,3,2,1,0:T(8,128)(2,1)S(1)}) custom-call(bf16[1,256,1024]{2,1,0:T(8,128)(2,1)S(1)} %copy-done, bf16[1,1024,3072]{2,1,0:T(8,128)(2,1)} %weight_ref.5), custom_call_target="tpu_custom_call" | custom-call | flops 1610612736 | bytes 8388608 | tf_op jit(solution)/shard_map/forward_rows/pallas_call | solution.py:112
  5.7 0.5 collective-permute-start
  6.3 1.9 %collective-permute-done.got_ref = bf16[4,2,2,64,384]{4,3,2,1,0:T(8,128)(2,1)S(1)} collective-permute-done((bf16[4,2,2,64,384]{4,3,2,1,0:T(8,128)(2,1)S(1)}, bf16[4,2,2,64,384]{4,3,2,1,0:T(8,128)(2,1)S(1)}, u32[]{:S(2)}, u32[]{:S(2)}) %collective-permute-start) | collective-permute-done | bytes 786464 | tf_op jit(solution)/shard_map/ppermute | solution.py:447
  8.2 0.7 %spread_rows.1 = (bf16[5,128,384]{2,1,0:T(8,128)(2,1)S(1)}, f32[4,128,384]{2,1,0:T(8,128)S(1)}, bf16[656,384]{1,0:T(8,128)(2,1)S(1)}, f32[4,128,384]{2,1,0:T(8,128)S(1)}) custom-call(f32[4,128]{1,0:T(4,128)S(1)} %pad_add_fusion.meta_ref, bf16[4,2,2,64,384]{4,3,2,1,0:T(8,128)(2,1)S(1)} %get-tuple-element.32.keep_ref, ...), custom_call_target="tpu_custom_call" | custom-call | flops 201326592 | bytes 4718592 | tf_op jit(solution)/shard_map/spread_rows/pallas_call | solution.py:182
  8.9 3.0 %collective-permute-start.2 = (bf16[656,384]{1,0:T(8,128)(2,1)S(1)}, bf16[656,384]{1,0:T(8,128)(2,1)S(1)}, u32[]{:S(2)}, u32[]{:S(2)}) collective-permute-start(bf16[656,384]{1,0:T(8,128)(2,1)S(1)} %get-tuple-element.39), channel_id=1, source_target_pairs={{0,16},{1,17},{2,18},{3,19},{4,20},{5,21},{6,22},{7,23},{8,24},{9,... | collective-permute-start | bytes 1511432 | tf_op jit(solution)/shard_map/ppermute | solution.py:447
  11.9 1.5 %collective-permute-start.1 = (bf16[5,128,384]{2,1,0:T(8,128)(2,1)S(1)}, bf16[5,128,384]{2,1,0:T(8,128)(2,1)S(1)}, u32[]{:S(2)}, u32[]{:S(2)}) collective-permute-start(bf16[5,128,384]{2,1,0:T(8,128)(2,1)S(1)} %get-tuple-element.37), channel_id=1, source_target_pairs={{0,1},{1,0},{2,3},{3,2},{4,5},{5,4},{6,7},{7,6},{8,9},{9,8},{10,11... | collective-permute-start | bytes 1474568 | tf_op jit(solution)/shard_map/ppermute | solution.py:447
  13.4 3.6 %collective-permute-start.12 = (bf16[128,384]{1,0:T(8,128)(2,1)S(1)}, bf16[128,384]{1,0:T(8,128)(2,1)S(1)}, u32[]{:S(2)}, u32[]{:S(2)}) collective-permute-start(bf16[128,384]{1,0:T(8,128)(2,1)S(1)} %copy-done.1), channel_id=1, source_target_pairs={{0,6},{1,7},{2,0},{3,1},{4,2},{5,3},{6,4},{7,5},{8,14},{9,15},{10,... | collective-permute-start | bytes 294920 | tf_op jit(solution)/shard_map/ppermute | solution.py:450
  17.0 1.0 %collective-permute-start.10 = (bf16[128,384]{1,0:T(8,128)(2,1)S(1)}, bf16[128,384]{1,0:T(8,128)(2,1)S(1)}, u32[]{:S(2)}, u32[]{:S(2)}) collective-permute-start(bf16[128,384]{1,0:T(8,128)(2,1)S(1)} %copy-done.1), channel_id=1, source_target_pairs={{0,2},{1,3},{2,4},{3,5},{4,6},{5,7},{6,0},{7,1},{8,10},{9,11},{10,... | collective-permute-start | bytes 294920 | tf_op jit(solution)/shard_map/ppermute | solution.py:450
  18.0 6.9 %collective-permute-done.1.x_got = bf16[5,128,384]{2,1,0:T(8,128)(2,1)S(1)} collective-permute-done((bf16[5,128,384]{2,1,0:T(8,128)(2,1)S(1)}, bf16[5,128,384]{2,1,0:T(8,128)(2,1)S(1)}, u32[]{:S(2)}, u32[]{:S(2)}) %collective-permute-start.1) | collective-permute-done | bytes 491552 | tf_op jit(solution)/shard_map/ppermute | solution.py:447
  24.9 0.6 %first_sum.1 = (f32[2,128,384]{2,1,0:T(8,128)S(1)}, bf16[320,384]{1,0:T(8,128)(2,1)S(1)}, f32[2,128,384]{2,1,0:T(8,128)S(1)}, bf16[320,384]{1,0:T(8,128)(2,1)S(1...) custom-call(bf16[128,384]{1,0:T(8,128)(2,1)S(1)} %copy-done.1, f32[4,128]{1,0:T(4,128)S(1)} %pad_add_fusion.meta_ref, ...), custom_call_target="tpu_custom_call" | custom-call | flops 1000000000 | tf_op jit(solution)/shard_map/first_sum/pallas_call | solution.py:233
  25.5 0.6 %collective-permute-start.5 = (bf16[320,384]{1,0:T(8,128)(2,1)S(1)}, bf16[320,384]{1,0:T(8,128)(2,1)S(1)}, u32[]{:S(2)}, u32[]{:S(2)}) collective-permute-start(bf16[320,384]{1,0:T(8,128)(2,1)S(1)} %get-tuple-element.44), channel_id=1, source_target_pairs={{0,16},{1,17},{2,18},{3,19},{4,20},{5,21},{6,22},{7,23},{8,24},{9,... | collective-permute-start | bytes 737288 | tf_op jit(solution)/shard_map/ppermute | solution.py:447
  26.1 1.5 %collective-permute-start.6 = (bf16[320,384]{1,0:T(8,128)(2,1)S(1)}, bf16[320,384]{1,0:T(8,128)(2,1)S(1)}, u32[]{:S(2)}, u32[]{:S(2)}) collective-permute-start(bf16[320,384]{1,0:T(8,128)(2,1)S(1)} %get-tuple-element.45), channel_id=1, source_target_pairs={{0,1},{1,0},{2,3},{3,2},{4,5},{5,4},{6,7},{7,6},{8,9},{9,8},{10,11... | collective-permute-start | bytes 737288 | tf_op jit(solution)/shard_map/ppermute | solution.py:447
  27.6 0.6 %collective-permute-start.13 = (bf16[3,128,384]{2,1,0:T(8,128)(2,1)S(1)}, bf16[3,128,384]{2,1,0:T(8,128)(2,1)S(1)}, u32[]{:S(2)}, u32[]{:S(2)}) collective-permute-start(bf16[3,128,384]{2,1,0:T(8,128)(2,1)S(1)} %stack_blocks.1.refs_0_), channel_id=1, source_target_pairs={{0,1},{1,0},{2,3},{3,2},{4,5},{5,4},{6,7},{7,6},{8,9},{9,8},{10,11... | collective-permute-start | bytes 884744 | tf_op jit(solution)/shard_map/ppermute | solution.py:447
  28.2 1.5 %collective-permute-start.14 = (bf16[3,128,384]{2,1,0:T(8,128)(2,1)S(1)}, bf16[3,128,384]{2,1,0:T(8,128)(2,1)S(1)}, u32[]{:S(2)}, u32[]{:S(2)}) collective-permute-start(bf16[3,128,384]{2,1,0:T(8,128)(2,1)S(1)} %stack_blocks.1.refs_0_), channel_id=1, source_target_pairs={{0,16},{1,17},{2,18},{3,19},{4,20},{5,21},{6,22},{7,23},{8,24},{9,... | collective-permute-start | bytes 884744 | tf_op jit(solution)/shard_map/ppermute | solution.py:447
  29.7 4.7 %collective-permute-done.5.by_y = bf16[320,384]{1,0:T(8,128)(2,1)S(1)} collective-permute-done((bf16[320,384]{1,0:T(8,128)(2,1)S(1)}, bf16[320,384]{1,0:T(8,128)(2,1)S(1)}, u32[]{:S(2)}, u32[]{:S(2)}) %collective-permute-start.5) | collective-permute-done | bytes 245792 | tf_op jit(solution)/shard_map/ppermute | solution.py:447
  34.4 0.5 collective-permute-done.6.by_x
  35.0 0.5 second_sum.1
  35.5 1.6 %collective-permute-start.8 = (bf16[128,384]{1,0:T(8,128)(2,1)S(1)}, bf16[128,384]{1,0:T(8,128)(2,1)S(1)}, u32[]{:S(2)}, u32[]{:S(2)}) collective-permute-start(bf16[128,384]{1,0:T(8,128)(2,1)S(1)} %get-tuple-element.47), channel_id=1, source_target_pairs={{0,2},{1,3},{2,4},{3,5},{4,6},{5,7},{6,0},{7,1},{8,10},{9,11},{10,... | collective-permute-start | bytes 294920 | tf_op jit(solution)/shard_map/ppermute | solution.py:450
  37.1 2.2 %collective-permute-start.9 = (bf16[128,384]{1,0:T(8,128)(2,1)S(1)}, bf16[128,384]{1,0:T(8,128)(2,1)S(1)}, u32[]{:S(2)}, u32[]{:S(2)}) collective-permute-start(bf16[128,384]{1,0:T(8,128)(2,1)S(1)} %get-tuple-element.48), channel_id=1, source_target_pairs={{0,6},{1,7},{2,0},{3,1},{4,2},{5,3},{6,4},{7,5},{8,14},{9,15},{10,... | collective-permute-start | bytes 294920 | tf_op jit(solution)/shard_map/ppermute | solution.py:450
  39.4 1.5 %collective-permute-start.15 = (bf16[2,128,384]{2,1,0:T(8,128)(2,1)S(1)}, bf16[2,128,384]{2,1,0:T(8,128)(2,1)S(1)}, u32[]{:S(2)}, u32[]{:S(2)}) collective-permute-start(bf16[2,128,384]{2,1,0:T(8,128)(2,1)S(1)} %slice.8), channel_id=1, source_target_pairs={{0,16},{1,17},{2,18},{3,19},{4,20},{5,21},{6,22},{7,23},{8,24},{9,... | collective-permute-start | bytes 589832 | tf_op jit(solution)/shard_map/ppermute | solution.py:447
  41.0 0.3 collective-permute-start.17
  41.3 1.5 %collective-permute-done.8.refs_4_.refs_0_ = bf16[128,384]{1,0:T(8,128)(2,1)S(1)} collective-permute-done((bf16[128,384]{1,0:T(8,128)(2,1)S(1)}, bf16[128,384]{1,0:T(8,128)(2,1)S(1)}, u32[]{:S(2)}, u32[]{:S(2)}) %collective-permute-start.8) | collective-permute-done | bytes 98336 | tf_op jit(solution)/shard_map/ppermute | solution.py:450
  42.8 1.5 %collective-permute-start.16 = (bf16[1,128,384]{2,1,0:T(8,128)(2,1)S(1)}, bf16[1,128,384]{2,1,0:T(8,128)(2,1)S(1)}, u32[]{:S(2)}, u32[]{:S(2)}) collective-permute-start(bf16[1,128,384]{2,1,0:T(8,128)(2,1)S(1)} %slice.9), channel_id=1, source_target_pairs={{0,1},{1,0},{2,3},{3,2},{4,5},{5,4},{6,7},{7,6},{8,9},{9,8},{10,11... | collective-permute-start | bytes 294920 | tf_op jit(solution)/shard_map/ppermute | solution.py:447
  44.3 0.5 collective-permute-start.18
  44.8 2.4 %backward_here.1 = (f32[256,1024]{1,0:T(8,128)S(1)}, bf16[1,1024,3072]{2,1,0:T(8,128)(2,1)}, bf16[1024,256]{1,0:T(8,128)(2,1)S(1)}, bf16[4,64,128]{2,1,0:T(8,128)(2,1)S(1)}, f32[4,64,128]{2,1,0:T(8,128)S(1)}) custom-call(bf16[1,256,1024]{2,1,0:T(8,128)(2,1)S(1)} %copy-done, bf16[1,1024,3072]{2,1,0:T(8,128)(2,1)S(1)} %bitcast.4, ...), custom_call_target="tpu_custom_call" | custom-call | flops 2000000000 | tf_op jit(solution)/shard_map/backward_here/pallas_call | solution.py:337
  47.2 0.1 collective-permute-start.20
  47.4 0.4 collective-permute-start.21
  47.8 2.0 %collective-permute-start.22 = (bf16[128,384]{1,0:T(8,128)(2,1)S(1)}, bf16[128,384]{1,0:T(8,128)(2,1)S(1)}, u32[]{:S(2)}, u32[]{:S(2)}) collective-permute-start(bf16[128,384]{1,0:T(8,128)(2,1)S(1)} %get-tuple-element.58), channel_id=1, source_target_pairs={{0,4},{1,5},{2,6},{3,7},{4,0},{5,1},{6,2},{7,3},{8,12},{9,13},{10,... | collective-permute-start | bytes 294920 | tf_op jit(solution)/shard_map/ppermute | solution.py:450
  49.8 4.8 %backward_rows.1 = (bf16[1,256,1024]{2,1,0:T(8,128)(2,1)}, bf16[1,1024,3072]{2,1,0:T(8,128)(2,1)}, f32[8,128]{1,0:T(8,128)S(1)}) custom-call(bf16[1,1024,3072]{2,1,0:T(8,128)(2,1)S(1)} %bitcast.4, f32[256,1024]{1,0:T(8,128)S(1)} %get-tuple-element.49.part_ref, bf16[1024,256]{1,0:T(8,128)(2,1)S(1)} %get-tuple-element.50.turned, ...), custom_call_target="tpu_custom_call", output_to_operand_aliasing={{1}: (15, {})} | custom-call | flops 100000000 | tf_op jit(solution)/shard_map/backward_rows/pallas_call | solution.py:393
  54.6 1.0 %collective-permute-done.22.refs_1_ = bf16[128,384]{1,0:T(8,128)(2,1)S(1)} collective-permute-done((bf16[128,384]{1,0:T(8,128)(2,1)S(1)}, bf16[128,384]{1,0:T(8,128)(2,1)S(1)}, u32[]{:S(2)}, u32[]{:S(2)}) %collective-permute-start.22) | collective-permute-done | bytes 98336 | tf_op jit(solution)/shard_map/ppermute | solution.py:450
  55.6 0.7 %last_sum.1 = bf16[128,384]{1,0:T(8,128)(2,1)} custom-call(f32[8,128]{1,0:T(8,128)S(1)} %get-tuple-element.56._, f32[128,384]{1,0:T(8,128)S(1)} %get-tuple-element.57.first_ref, bf16[128,384]{1,0:T(8,128)(2,1)S(1)} %collective-permute-done.8.refs_4_.refs_0_, bf16[128,384]{1,0:T(8,128)(2,1)S(1)} %collective-permute-done.22.refs_1_, ...), custom_call_target="tpu_custom_call" | custom-call | flops 1000000000 | tf_op jit(solution)/shard_map/last_sum/pallas_call | solution.py:425
  (39 shorter events, 0.2 us)
Async XLA Ops:
  0.6 1.0 %copy-start = (bf16[1,256,1024]{2,1,0:T(8,128)(2,1)S(1)}, bf16[1,256,1024]{2,1,0:T(8,128)(2,1)}, u32[]{:S(2)}) copy-start(bf16[1,256,1024]{2,1,0:T(8,128)(2,1)} %hidden_ref.3) | copy-start | bytes 1572868
  1.7 4.6 %copy-start.2 = (s32[128,2]{0,1:T(2,128)S(1)}, s32[128,2]{0,1:T(2,128)}, u32[]{:S(2)}) copy-start(s32[128,2]{0,1:T(2,128)} %param.7) | copy-start | bytes 3076
  1.7 4.6 %copy-start.3 = (f32[128,2]{0,1:T(2,128)S(1)}, f32[128,2]{0,1:T(2,128)}, u32[]{:S(2)}) copy-start(f32[128,2]{0,1:T(2,128)} %param.8) | copy-start | bytes 3076
  1.7 6.5 %copy-start.1 = (bf16[128,384]{1,0:T(8,128)(2,1)S(1)}, bf16[128,384]{1,0:T(8,128)(2,1)}, u32[]{:S(2)}) copy-start(bf16[128,384]{1,0:T(8,128)(2,1)} %grad_ref.3) | copy-start | bytes 294916
  5.7 2.4 %collective-permute-start = (bf16[4,2,2,64,384]{4,3,2,1,0:T(8,128)(2,1)S(1)}, bf16[4,2,2,64,384]{4,3,2,1,0:T(8,128)(2,1)S(1)}, u32[]{:S(2)}, u32[]{:S(2)}) collective-permute-start(bf16[4,2,2,64,384]{4,3,2,1,0:T(8,128)(2,1)S(1)} %get-tuple-element.35), channel_id=1, source_target_pairs={{0,8},{1,9},{2,10},{3,11},{4,12},{5,13},{6,14},{7,15},{8,0},{9,1},... | collective-permute-start | bytes 2359304 | tf_op jit(solution)/shard_map/ppermute | solution.py:447
  6.3 38.5 %slice-start = ((s8[6291456]{0:T(1024)(128)(4,1)}), s8[4194304]{0:T(1024)(128)(4,1)S(1)}, s32[]{:S(2)}) async-start(s8[6291456]{0:T(1024)(128)(4,1)} %bitcast.3), calls=%async_computation | async-start | bytes 8388608
  8.9 15.9 %collective-permute-start.2 = (bf16[656,384]{1,0:T(8,128)(2,1)S(1)}, bf16[656,384]{1,0:T(8,128)(2,1)S(1)}, u32[]{:S(2)}, u32[]{:S(2)}) collective-permute-start(bf16[656,384]{1,0:T(8,128)(2,1)S(1)} %get-tuple-element.39), channel_id=1, source_target_pairs={{0,16},{1,17},{2,18},{3,19},{4,20},{5,21},{6,22},{7,23},{8,24},{9,... | collective-permute-start | bytes 1511432 | tf_op jit(solution)/shard_map/ppermute | solution.py:447
  11.9 13.0 %collective-permute-start.1 = (bf16[5,128,384]{2,1,0:T(8,128)(2,1)S(1)}, bf16[5,128,384]{2,1,0:T(8,128)(2,1)S(1)}, u32[]{:S(2)}, u32[]{:S(2)}) collective-permute-start(bf16[5,128,384]{2,1,0:T(8,128)(2,1)S(1)} %get-tuple-element.37), channel_id=1, source_target_pairs={{0,1},{1,0},{2,3},{3,2},{4,5},{5,4},{6,7},{7,6},{8,9},{9,8},{10,11... | collective-permute-start | bytes 1474568 | tf_op jit(solution)/shard_map/ppermute | solution.py:447
  13.4 14.2 %collective-permute-start.12 = (bf16[128,384]{1,0:T(8,128)(2,1)S(1)}, bf16[128,384]{1,0:T(8,128)(2,1)S(1)}, u32[]{:S(2)}, u32[]{:S(2)}) collective-permute-start(bf16[128,384]{1,0:T(8,128)(2,1)S(1)} %copy-done.1), channel_id=1, source_target_pairs={{0,6},{1,7},{2,0},{3,1},{4,2},{5,3},{6,4},{7,5},{8,14},{9,15},{10,... | collective-permute-start | bytes 294920 | tf_op jit(solution)/shard_map/ppermute | solution.py:450
  17.0 10.6 %collective-permute-start.11 = (bf16[128,384]{1,0:T(8,128)(2,1)S(1)}, bf16[128,384]{1,0:T(8,128)(2,1)S(1)}, u32[]{:S(2)}, u32[]{:S(2)}) collective-permute-start(bf16[128,384]{1,0:T(8,128)(2,1)S(1)} %copy-done.1), channel_id=1, source_target_pairs={{0,4},{1,5},{2,6},{3,7},{4,0},{5,1},{6,2},{7,3},{8,12},{9,13},{10,... | collective-permute-start | bytes 294920 | tf_op jit(solution)/shard_map/ppermute | solution.py:450
  17.0 10.6 %collective-permute-start.10 = (bf16[128,384]{1,0:T(8,128)(2,1)S(1)}, bf16[128,384]{1,0:T(8,128)(2,1)S(1)}, u32[]{:S(2)}, u32[]{:S(2)}) collective-permute-start(bf16[128,384]{1,0:T(8,128)(2,1)S(1)} %copy-done.1), channel_id=1, source_target_pairs={{0,2},{1,3},{2,4},{3,5},{4,6},{5,7},{6,0},{7,1},{8,10},{9,11},{10,... | collective-permute-start | bytes 294920 | tf_op jit(solution)/shard_map/ppermute | solution.py:450
  25.5 9.0 %collective-permute-start.5 = (bf16[320,384]{1,0:T(8,128)(2,1)S(1)}, bf16[320,384]{1,0:T(8,128)(2,1)S(1)}, u32[]{:S(2)}, u32[]{:S(2)}) collective-permute-start(bf16[320,384]{1,0:T(8,128)(2,1)S(1)} %get-tuple-element.44), channel_id=1, source_target_pairs={{0,16},{1,17},{2,18},{3,19},{4,20},{5,21},{6,22},{7,23},{8,24},{9,... | collective-permute-start | bytes 737288 | tf_op jit(solution)/shard_map/ppermute | solution.py:447
  26.1 8.9 %collective-permute-start.6 = (bf16[320,384]{1,0:T(8,128)(2,1)S(1)}, bf16[320,384]{1,0:T(8,128)(2,1)S(1)}, u32[]{:S(2)}, u32[]{:S(2)}) collective-permute-start(bf16[320,384]{1,0:T(8,128)(2,1)S(1)} %get-tuple-element.45), channel_id=1, source_target_pairs={{0,1},{1,0},{2,3},{3,2},{4,5},{5,4},{6,7},{7,6},{8,9},{9,8},{10,11... | collective-permute-start | bytes 737288 | tf_op jit(solution)/shard_map/ppermute | solution.py:447
  27.6 17.2 %slice-start.1 = ((s8[6291456]{0:T(1024)(128)(4,1)}), s8[2097152]{0:T(1024)(128)(4,1)S(1)}, s32[]{:S(2)}) async-start(s8[6291456]{0:T(1024)(128)(4,1)} %bitcast.3), calls=%async_computation.1 | async-start | bytes 4194304
  27.6 11.8 %collective-permute-start.13 = (bf16[3,128,384]{2,1,0:T(8,128)(2,1)S(1)}, bf16[3,128,384]{2,1,0:T(8,128)(2,1)S(1)}, u32[]{:S(2)}, u32[]{:S(2)}) collective-permute-start(bf16[3,128,384]{2,1,0:T(8,128)(2,1)S(1)} %stack_blocks.1.refs_0_), channel_id=1, source_target_pairs={{0,1},{1,0},{2,3},{3,2},{4,5},{5,4},{6,7},{7,6},{8,9},{9,8},{10,11... | collective-permute-start | bytes 884744 | tf_op jit(solution)/shard_map/ppermute | solution.py:447
  28.2 11.2 %collective-permute-start.14 = (bf16[3,128,384]{2,1,0:T(8,128)(2,1)S(1)}, bf16[3,128,384]{2,1,0:T(8,128)(2,1)S(1)}, u32[]{:S(2)}, u32[]{:S(2)}) collective-permute-start(bf16[3,128,384]{2,1,0:T(8,128)(2,1)S(1)} %stack_blocks.1.refs_0_), channel_id=1, source_target_pairs={{0,16},{1,17},{2,18},{3,19},{4,20},{5,21},{6,22},{7,23},{8,24},{9,... | collective-permute-start | bytes 884744 | tf_op jit(solution)/shard_map/ppermute | solution.py:447
  29.7 11.3 %collective-permute-start.4 = (bf16[3,128,384]{2,1,0:T(8,128)(2,1)S(1)}, bf16[3,128,384]{2,1,0:T(8,128)(2,1)S(1)}, u32[]{:S(2)}, u32[]{:S(2)}) collective-permute-start(bf16[3,128,384]{2,1,0:T(8,128)(2,1)S(1)} %get-tuple-element.41.refs_0_), channel_id=1, source_target_pairs={{0,8},{1,9},{2,10},{3,11},{4,12},{5,13},{6,14},{7,15},{8,0},{9,1},... | collective-permute-start | bytes 884744 | tf_op jit(solution)/shard_map/ppermute | solution.py:447
  34.4 2.7 %collective-permute-start.3 = (f32[2,4,128]{2,1,0:T(4,128)S(1)}, f32[2,4,128]{2,1,0:T(4,128)S(1)}, u32[]{:S(2)}, u32[]{:S(2)}) collective-permute-start(f32[2,4,128]{2,1,0:T(4,128)S(1)} %get-tuple-element.40.metas), channel_id=1, source_target_pairs={{0,8},{1,9},{2,10},{3,11},{4,12},{5,13},{6,14},{7,15},{8,0},{9,1},... | collective-permute-start | bytes 12296 | tf_op jit(solution)/shard_map/ppermute | solution.py:447
  35.5 7.3 %collective-permute-start.8 = (bf16[128,384]{1,0:T(8,128)(2,1)S(1)}, bf16[128,384]{1,0:T(8,128)(2,1)S(1)}, u32[]{:S(2)}, u32[]{:S(2)}) collective-permute-start(bf16[128,384]{1,0:T(8,128)(2,1)S(1)} %get-tuple-element.47), channel_id=1, source_target_pairs={{0,2},{1,3},{2,4},{3,5},{4,6},{5,7},{6,0},{7,1},{8,10},{9,11},{10,... | collective-permute-start | bytes 294920 | tf_op jit(solution)/shard_map/ppermute | solution.py:450
  37.1 7.2 %collective-permute-start.9 = (bf16[128,384]{1,0:T(8,128)(2,1)S(1)}, bf16[128,384]{1,0:T(8,128)(2,1)S(1)}, u32[]{:S(2)}, u32[]{:S(2)}) collective-permute-start(bf16[128,384]{1,0:T(8,128)(2,1)S(1)} %get-tuple-element.48), channel_id=1, source_target_pairs={{0,6},{1,7},{2,0},{3,1},{4,2},{5,3},{6,4},{7,5},{8,14},{9,15},{10,... | collective-permute-start | bytes 294920 | tf_op jit(solution)/shard_map/ppermute | solution.py:450
  39.4 4.9 %collective-permute-start.7 = (bf16[128,384]{1,0:T(8,128)(2,1)S(1)}, bf16[128,384]{1,0:T(8,128)(2,1)S(1)}, u32[]{:S(2)}, u32[]{:S(2)}) collective-permute-start(bf16[128,384]{1,0:T(8,128)(2,1)S(1)} %get-tuple-element.46.refs_2_), channel_id=1, source_target_pairs={{0,8},{1,9},{2,10},{3,11},{4,12},{5,13},{6,14},{7,15},{8,0},{9,1},... | collective-permute-start | bytes 294920 | tf_op jit(solution)/shard_map/ppermute | solution.py:447
  39.4 7.8 %collective-permute-start.15 = (bf16[2,128,384]{2,1,0:T(8,128)(2,1)S(1)}, bf16[2,128,384]{2,1,0:T(8,128)(2,1)S(1)}, u32[]{:S(2)}, u32[]{:S(2)}) collective-permute-start(bf16[2,128,384]{2,1,0:T(8,128)(2,1)S(1)} %slice.8), channel_id=1, source_target_pairs={{0,16},{1,17},{2,18},{3,19},{4,20},{5,21},{6,22},{7,23},{8,24},{9,... | collective-permute-start | bytes 589832 | tf_op jit(solution)/shard_map/ppermute | solution.py:447
  41.0 6.8 %collective-permute-start.17 = (bf16[3,128,384]{2,1,0:T(8,128)(2,1)S(1)}, bf16[3,128,384]{2,1,0:T(8,128)(2,1)S(1)}, u32[]{:S(2)}, u32[]{:S(2)}) collective-permute-start(bf16[3,128,384]{2,1,0:T(8,128)(2,1)S(1)} %stack_blocks.1.refs_0_), channel_id=1, source_target_pairs={{0,8},{1,9},{2,10},{3,11},{4,12},{5,13},{6,14},{7,15},{8,0},{9,1},... | collective-permute-start | bytes 884744 | tf_op jit(solution)/shard_map/ppermute | solution.py:447
  42.8 4.6 %collective-permute-start.16 = (bf16[1,128,384]{2,1,0:T(8,128)(2,1)S(1)}, bf16[1,128,384]{2,1,0:T(8,128)(2,1)S(1)}, u32[]{:S(2)}, u32[]{:S(2)}) collective-permute-start(bf16[1,128,384]{2,1,0:T(8,128)(2,1)S(1)} %slice.9), channel_id=1, source_target_pairs={{0,1},{1,0},{2,3},{3,2},{4,5},{5,4},{6,7},{7,6},{8,9},{9,8},{10,11... | collective-permute-start | bytes 294920 | tf_op jit(solution)/shard_map/ppermute | solution.py:447
  44.3 5.5 %collective-permute-start.19 = (bf16[3,128,384]{2,1,0:T(8,128)(2,1)S(1)}, bf16[3,128,384]{2,1,0:T(8,128)(2,1)S(1)}, u32[]{:S(2)}, u32[]{:S(2)}) collective-permute-start(bf16[3,128,384]{2,1,0:T(8,128)(2,1)S(1)} %collective-permute-done.14.refs_2_), channel_id=1, source_target_pairs={{0,8},{1,9},{2,10},{3,11},{4,12},{5,13},{6,14},{7,15},{8,0},{9,1},... | collective-permute-start | bytes 884744 | tf_op jit(solution)/shard_map/ppermute | solution.py:447
  44.3 5.5 %collective-permute-start.18 = (bf16[3,128,384]{2,1,0:T(8,128)(2,1)S(1)}, bf16[3,128,384]{2,1,0:T(8,128)(2,1)S(1)}, u32[]{:S(2)}, u32[]{:S(2)}) collective-permute-start(bf16[3,128,384]{2,1,0:T(8,128)(2,1)S(1)} %collective-permute-done.13.refs_1_), channel_id=1, source_target_pairs={{0,8},{1,9},{2,10},{3,11},{4,12},{5,13},{6,14},{7,15},{8,0},{9,1},... | collective-permute-start | bytes 884744 | tf_op jit(solution)/shard_map/ppermute | solution.py:447
  47.2 2.6 %collective-permute-start.20 = (bf16[2,128,384]{2,1,0:T(8,128)(2,1)S(1)}, bf16[2,128,384]{2,1,0:T(8,128)(2,1)S(1)}, u32[]{:S(2)}, u32[]{:S(2)}) collective-permute-start(bf16[2,128,384]{2,1,0:T(8,128)(2,1)S(1)} %collective-permute-done.15.refs_3_), channel_id=1, source_target_pairs={{0,8},{1,9},{2,10},{3,11},{4,12},{5,13},{6,14},{7,15},{8,0},{9,1},... | collective-permute-start | bytes 589832 | tf_op jit(solution)/shard_map/ppermute | solution.py:447
  47.4 2.4 %collective-permute-start.21 = (bf16[1,128,384]{2,1,0:T(8,128)(2,1)S(1)}, bf16[1,128,384]{2,1,0:T(8,128)(2,1)S(1)}, u32[]{:S(2)}, u32[]{:S(2)}) collective-permute-start(bf16[1,128,384]{2,1,0:T(8,128)(2,1)S(1)} %collective-permute-done.16.refs_4_), channel_id=1, source_target_pairs={{0,8},{1,9},{2,10},{3,11},{4,12},{5,13},{6,14},{7,15},{8,0},{9,1},... | collective-permute-start | bytes 294920 | tf_op jit(solution)/shard_map/ppermute | solution.py:447
  47.8 7.9 %collective-permute-start.22 = (bf16[128,384]{1,0:T(8,128)(2,1)S(1)}, bf16[128,384]{1,0:T(8,128)(2,1)S(1)}, u32[]{:S(2)}, u32[]{:S(2)}) collective-permute-start(bf16[128,384]{1,0:T(8,128)(2,1)S(1)} %get-tuple-element.58), channel_id=1, source_target_pairs={{0,4},{1,5},{2,6},{3,7},{4,0},{5,1},{6,2},{7,3},{8,12},{9,13},{10,... | collective-permute-start | bytes 294920 | tf_op jit(solution)/shard_map/ppermute | solution.py:450

commit v7 on v6

--- a/solution.py
+++ b/solution.py
@@ -322,11 +322,16 @@
         for j in range(4):
             put(rows_ref, hots, cols, j % 2, 2 * (j // 2) + dc, grads[dc][j] if j < 3 else grads[2 + dc][...])
     rows, column = rows_ref[...], columns(nz, 0, feat)
-    made[...] = jnp.dot(turned[...], rows, preferred_element_type=F32).astype(BF)
-    copy = pltpu.make_async_copy(made, down_out.at[0, :, column], sem)
-    copy.start()
+    mid, copies = made.shape[0] // 2, []
+    for i in range(2):
+        upper = slice(i * mid, (i + 1) * mid)
+        made[upper] = jnp.dot(turned[upper], rows, preferred_element_type=F32).astype(BF)
+        strip = pl.ds(i * mid, mid)
+        copies.append(pltpu.make_async_copy(made.at[strip], down_out.at[0, strip, column], sem.at[i]))
+        copies[i].start()
     part[...] = times_transposed(rows, weight_ref[0, :, column])
-    copy.wait()
+    for copy in copies:
+        copy.wait()
 
 
 def backward_here(hidden, weight, metas, other_metas, near_by, cross, after=()):
@@ -341,7 +346,7 @@
         scratch_shapes=[
             pltpu.VMEM((ff, 2 * feat), BF),
             pltpu.VMEM((slots, 2 * feat), BF),
-            pltpu.SemaphoreType.DMA,
+            pltpu.SemaphoreType.DMA((2,)),
         ],
         out_shape=[
             jax.ShapeDtypeStruct((slots, ff), F32),

time: 56.5 us -> 56.5 us (level)
  transfers between devices with their start and end apart: 23 -> 23, of which waited for: 7 -> 7; matrix products, arithmetic and copies ran while one was open for 0% -> 0% of each run, Pallas kernels for 15% -> 14%
where the time goes in v7:
time: 56.5 us; the launch traced here: 56.3 us
  starting transfers between devices  24 us (42%)
  waiting for transfers between devices  16.9 us (30%)
  Pallas kernels  13.6 us (24%)
  local copies, waits for them, and re-layouts  1.09 us (2%)
  between operations  0.79 us (1%)
    ppermute x17, waiting for transfers between devices, send(): return lax.ppermute(value, ('dp', 'cuts'), pairs)  14.4 us
    ppermute x17, starting transfers between devices, send(): return lax.ppermute(value, ('dp', 'cuts'), pairs)  13.2 us
    ppermute x6, starting transfers between devices, along(): lax.ppermute(value, 'cuts', [(c, (c + 2 * k) % cut_count) for c in range(...  10.7 us
    pallas_call x1, Pallas kernels, backward(): pl.pallas_call(functools.partial(backward_kernel, weight.shape[2] // (2 *...  4.8 us
    pallas_call x1, Pallas kernels, forward(): pl.pallas_call(functools.partial(forward_kernel, nz, capacity), in_specs=...  4.04 us
    ppermute x6, waiting for transfers between devices, along(): lax.ppermute(value, 'cuts', [(c, (c + 2 * k) % cut_count) for c in range(...  2.54 us
    pallas_call x1, Pallas kernels, backward_here(): pl.pallas_call(functools.partial(backward_here_kernel, weight.shape[2] //...  2.13 us
  transfers between devices with their start and end apart: 23, of which 7 were waited for; matrix products, arithmetic and copies ran while one was open for 0% of the time, Pallas kernels for 14%

profile of v7, /device:TPU:0, one launch (start us, length us, event | category | flops | bytes accessed | tf_op | source)
XLA Modules:
  0.0 56.3 jit_solution(14957317084191990828)
XLA Ops:
  0.6 1.0 %copy-done = bf16[1,256,1024]{2,1,0:T(8,128)(2,1)S(1)} copy-done((bf16[1,256,1024]{2,1,0:T(8,128)(2,1)S(1)}, bf16[1,256,1024]{2,1,0:T(8,128)(2,1)}, u32[]{:S(2)}) %copy-start) | copy-done | bytes 524312
  1.7 4.0 %forward_rows.1 = (bf16[4,2,2,64,384]{4,3,2,1,0:T(8,128)(2,1)S(1)}, bf16[4,2,2,64,384]{4,3,2,1,0:T(8,128)(2,1)S(1)}) custom-call(bf16[1,256,1024]{2,1,0:T(8,128)(2,1)S(1)} %copy-done, bf16[1,1024,3072]{2,1,0:T(8,128)(2,1)} %weight_ref.5), custom_call_target="tpu_custom_call" | custom-call | flops 1610612736 | bytes 8388608 | tf_op jit(solution)/shard_map/forward_rows/pallas_call | solution.py:112
  5.7 0.5 collective-permute-start
  6.3 1.9 %collective-permute-done.got_ref = bf16[4,2,2,64,384]{4,3,2,1,0:T(8,128)(2,1)S(1)} collective-permute-done((bf16[4,2,2,64,384]{4,3,2,1,0:T(8,128)(2,1)S(1)}, bf16[4,2,2,64,384]{4,3,2,1,0:T(8,128)(2,1)S(1)}, u32[]{:S(2)}, u32[]{:S(2)}) %collective-permute-start) | collective-permute-done | bytes 786464 | tf_op jit(solution)/shard_map/ppermute | solution.py:452
  8.2 0.7 %spread_rows.1 = (bf16[5,128,384]{2,1,0:T(8,128)(2,1)S(1)}, f32[4,128,384]{2,1,0:T(8,128)S(1)}, bf16[656,384]{1,0:T(8,128)(2,1)S(1)}, f32[4,128,384]{2,1,0:T(8,128)S(1)}) custom-call(f32[4,128]{1,0:T(4,128)S(1)} %pad_add_fusion.meta_ref, bf16[4,2,2,64,384]{4,3,2,1,0:T(8,128)(2,1)S(1)} %get-tuple-element.32.keep_ref, ...), custom_call_target="tpu_custom_call" | custom-call | flops 201326592 | bytes 4718592 | tf_op jit(solution)/shard_map/spread_rows/pallas_call | solution.py:182
  8.9 3.0 %collective-permute-start.2 = (bf16[656,384]{1,0:T(8,128)(2,1)S(1)}, bf16[656,384]{1,0:T(8,128)(2,1)S(1)}, u32[]{:S(2)}, u32[]{:S(2)}) collective-permute-start(bf16[656,384]{1,0:T(8,128)(2,1)S(1)} %get-tuple-element.39), channel_id=1, source_target_pairs={{0,16},{1,17},{2,18},{3,19},{4,20},{5,21},{6,22},{7,23},{8,24},{9,... | collective-permute-start | bytes 1511432 | tf_op jit(solution)/shard_map/ppermute | solution.py:452
  11.9 1.5 %collective-permute-start.1 = (bf16[5,128,384]{2,1,0:T(8,128)(2,1)S(1)}, bf16[5,128,384]{2,1,0:T(8,128)(2,1)S(1)}, u32[]{:S(2)}, u32[]{:S(2)}) collective-permute-start(bf16[5,128,384]{2,1,0:T(8,128)(2,1)S(1)} %get-tuple-element.37), channel_id=1, source_target_pairs={{0,1},{1,0},{2,3},{3,2},{4,5},{5,4},{6,7},{7,6},{8,9},{9,8},{10,11... | collective-permute-start | bytes 1474568 | tf_op jit(solution)/shard_map/ppermute | solution.py:452
  13.4 3.6 %collective-permute-start.12 = (bf16[128,384]{1,0:T(8,128)(2,1)S(1)}, bf16[128,384]{1,0:T(8,128)(2,1)S(1)}, u32[]{:S(2)}, u32[]{:S(2)}) collective-permute-start(bf16[128,384]{1,0:T(8,128)(2,1)S(1)} %copy-done.1), channel_id=1, source_target_pairs={{0,6},{1,7},{2,0},{3,1},{4,2},{5,3},{6,4},{7,5},{8,14},{9,15},{10,... | collective-permute-start | bytes 294920 | tf_op jit(solution)/shard_map/ppermute | solution.py:455
  17.0 1.0 %collective-permute-start.10 = (bf16[128,384]{1,0:T(8,128)(2,1)S(1)}, bf16[128,384]{1,0:T(8,128)(2,1)S(1)}, u32[]{:S(2)}, u32[]{:S(2)}) collective-permute-start(bf16[128,384]{1,0:T(8,128)(2,1)S(1)} %copy-done.1), channel_id=1, source_target_pairs={{0,2},{1,3},{2,4},{3,5},{4,6},{5,7},{6,0},{7,1},{8,10},{9,11},{10,... | collective-permute-start | bytes 294920 | tf_op jit(solution)/shard_map/ppermute | solution.py:455
  18.0 6.9 %collective-permute-done.1.x_got = bf16[5,128,384]{2,1,0:T(8,128)(2,1)S(1)} collective-permute-done((bf16[5,128,384]{2,1,0:T(8,128)(2,1)S(1)}, bf16[5,128,384]{2,1,0:T(8,128)(2,1)S(1)}, u32[]{:S(2)}, u32[]{:S(2)}) %collective-permute-start.1) | collective-permute-done | bytes 491552 | tf_op jit(solution)/shard_map/ppermute | solution.py:452
  24.9 0.6 %first_sum.1 = (f32[2,128,384]{2,1,0:T(8,128)S(1)}, bf16[320,384]{1,0:T(8,128)(2,1)S(1)}, f32[2,128,384]{2,1,0:T(8,128)S(1)}, bf16[320,384]{1,0:T(8,128)(2,1)S(1...) custom-call(bf16[128,384]{1,0:T(8,128)(2,1)S(1)} %copy-done.1, f32[4,128]{1,0:T(4,128)S(1)} %pad_add_fusion.meta_ref, ...), custom_call_target="tpu_custom_call" | custom-call | flops 1000000000 | tf_op jit(solution)/shard_map/first_sum/pallas_call | solution.py:233
  25.5 0.6 %collective-permute-start.5 = (bf16[320,384]{1,0:T(8,128)(2,1)S(1)}, bf16[320,384]{1,0:T(8,128)(2,1)S(1)}, u32[]{:S(2)}, u32[]{:S(2)}) collective-permute-start(bf16[320,384]{1,0:T(8,128)(2,1)S(1)} %get-tuple-element.44), channel_id=1, source_target_pairs={{0,16},{1,17},{2,18},{3,19},{4,20},{5,21},{6,22},{7,23},{8,24},{9,... | collective-permute-start | bytes 737288 | tf_op jit(solution)/shard_map/ppermute | solution.py:452
  26.1 1.5 %collective-permute-start.6 = (bf16[320,384]{1,0:T(8,128)(2,1)S(1)}, bf16[320,384]{1,0:T(8,128)(2,1)S(1)}, u32[]{:S(2)}, u32[]{:S(2)}) collective-permute-start(bf16[320,384]{1,0:T(8,128)(2,1)S(1)} %get-tuple-element.45), channel_id=1, source_target_pairs={{0,1},{1,0},{2,3},{3,2},{4,5},{5,4},{6,7},{7,6},{8,9},{9,8},{10,11... | collective-permute-start | bytes 737288 | tf_op jit(solution)/shard_map/ppermute | solution.py:452
  27.6 0.6 %collective-permute-start.13 = (bf16[3,128,384]{2,1,0:T(8,128)(2,1)S(1)}, bf16[3,128,384]{2,1,0:T(8,128)(2,1)S(1)}, u32[]{:S(2)}, u32[]{:S(2)}) collective-permute-start(bf16[3,128,384]{2,1,0:T(8,128)(2,1)S(1)} %stack_blocks.1.refs_0_), channel_id=1, source_target_pairs={{0,1},{1,0},{2,3},{3,2},{4,5},{5,4},{6,7},{7,6},{8,9},{9,8},{10,11... | collective-permute-start | bytes 884744 | tf_op jit(solution)/shard_map/ppermute | solution.py:452
  28.2 1.5 %collective-permute-start.14 = (bf16[3,128,384]{2,1,0:T(8,128)(2,1)S(1)}, bf16[3,128,384]{2,1,0:T(8,128)(2,1)S(1)}, u32[]{:S(2)}, u32[]{:S(2)}) collective-permute-start(bf16[3,128,384]{2,1,0:T(8,128)(2,1)S(1)} %stack_blocks.1.refs_0_), channel_id=1, source_target_pairs={{0,16},{1,17},{2,18},{3,19},{4,20},{5,21},{6,22},{7,23},{8,24},{9,... | collective-permute-start | bytes 884744 | tf_op jit(solution)/shard_map/ppermute | solution.py:452
  29.7 4.7 %collective-permute-done.5.by_y = bf16[320,384]{1,0:T(8,128)(2,1)S(1)} collective-permute-done((bf16[320,384]{1,0:T(8,128)(2,1)S(1)}, bf16[320,384]{1,0:T(8,128)(2,1)S(1)}, u32[]{:S(2)}, u32[]{:S(2)}) %collective-permute-start.5) | collective-permute-done | bytes 245792 | tf_op jit(solution)/shard_map/ppermute | solution.py:452
  34.4 0.5 collective-permute-done.6.by_x
  35.0 0.5 second_sum.1
  35.5 1.6 %collective-permute-start.8 = (bf16[128,384]{1,0:T(8,128)(2,1)S(1)}, bf16[128,384]{1,0:T(8,128)(2,1)S(1)}, u32[]{:S(2)}, u32[]{:S(2)}) collective-permute-start(bf16[128,384]{1,0:T(8,128)(2,1)S(1)} %get-tuple-element.47), channel_id=1, source_target_pairs={{0,2},{1,3},{2,4},{3,5},{4,6},{5,7},{6,0},{7,1},{8,10},{9,11},{10,... | collective-permute-start | bytes 294920 | tf_op jit(solution)/shard_map/ppermute | solution.py:455
  37.1 2.2 %collective-permute-start.9 = (bf16[128,384]{1,0:T(8,128)(2,1)S(1)}, bf16[128,384]{1,0:T(8,128)(2,1)S(1)}, u32[]{:S(2)}, u32[]{:S(2)}) collective-permute-start(bf16[128,384]{1,0:T(8,128)(2,1)S(1)} %get-tuple-element.48), channel_id=1, source_target_pairs={{0,6},{1,7},{2,0},{3,1},{4,2},{5,3},{6,4},{7,5},{8,14},{9,15},{10,... | collective-permute-start | bytes 294920 | tf_op jit(solution)/shard_map/ppermute | solution.py:455
  39.4 1.5 %collective-permute-start.15 = (bf16[2,128,384]{2,1,0:T(8,128)(2,1)S(1)}, bf16[2,128,384]{2,1,0:T(8,128)(2,1)S(1)}, u32[]{:S(2)}, u32[]{:S(2)}) collective-permute-start(bf16[2,128,384]{2,1,0:T(8,128)(2,1)S(1)} %slice.8), channel_id=1, source_target_pairs={{0,16},{1,17},{2,18},{3,19},{4,20},{5,21},{6,22},{7,23},{8,24},{9,... | collective-permute-start | bytes 589832 | tf_op jit(solution)/shard_map/ppermute | solution.py:452
  41.0 0.3 collective-permute-start.17
  41.3 1.5 %collective-permute-done.8.refs_4_.refs_0_ = bf16[128,384]{1,0:T(8,128)(2,1)S(1)} collective-permute-done((bf16[128,384]{1,0:T(8,128)(2,1)S(1)}, bf16[128,384]{1,0:T(8,128)(2,1)S(1)}, u32[]{:S(2)}, u32[]{:S(2)}) %collective-permute-start.8) | collective-permute-done | bytes 98336 | tf_op jit(solution)/shard_map/ppermute | solution.py:455
  42.8 1.5 %collective-permute-start.16 = (bf16[1,128,384]{2,1,0:T(8,128)(2,1)S(1)}, bf16[1,128,384]{2,1,0:T(8,128)(2,1)S(1)}, u32[]{:S(2)}, u32[]{:S(2)}) collective-permute-start(bf16[1,128,384]{2,1,0:T(8,128)(2,1)S(1)} %slice.9), channel_id=1, source_target_pairs={{0,1},{1,0},{2,3},{3,2},{4,5},{5,4},{6,7},{7,6},{8,9},{9,8},{10,11... | collective-permute-start | bytes 294920 | tf_op jit(solution)/shard_map/ppermute | solution.py:452
  44.3 0.5 collective-permute-start.18
  44.8 2.1 %backward_here.1 = (f32[256,1024]{1,0:T(8,128)S(1)}, bf16[1,1024,3072]{2,1,0:T(8,128)(2,1)}, bf16[1024,256]{1,0:T(8,128)(2,1)S(1)}, bf16[4,64,128]{2,1,0:T(8,128)(2,1)S(1)}, f32[4,64,128]{2,1,0:T(8,128)S(1)}) custom-call(bf16[1,256,1024]{2,1,0:T(8,128)(2,1)S(1)} %copy-done, bf16[1,1024,3072]{2,1,0:T(8,128)(2,1)S(1)} %bitcast.4, ...), custom_call_target="tpu_custom_call" | custom-call | flops 2000000000 | tf_op jit(solution)/shard_map/backward_here/pallas_call | solution.py:342
  47.0 0.1 collective-permute-start.20
  47.1 0.3 collective-permute-done.16.refs_4_
  47.6 2.2 %collective-permute-start.22 = (bf16[128,384]{1,0:T(8,128)(2,1)S(1)}, bf16[128,384]{1,0:T(8,128)(2,1)S(1)}, u32[]{:S(2)}, u32[]{:S(2)}) collective-permute-start(bf16[128,384]{1,0:T(8,128)(2,1)S(1)} %get-tuple-element.58), channel_id=1, source_target_pairs={{0,4},{1,5},{2,6},{3,7},{4,0},{5,1},{6,2},{7,3},{8,12},{9,13},{10,... | collective-permute-start | bytes 294920 | tf_op jit(solution)/shard_map/ppermute | solution.py:455
  49.8 4.8 %backward_rows.1 = (bf16[1,256,1024]{2,1,0:T(8,128)(2,1)}, bf16[1,1024,3072]{2,1,0:T(8,128)(2,1)}, f32[8,128]{1,0:T(8,128)S(1)}) custom-call(bf16[1,1024,3072]{2,1,0:T(8,128)(2,1)S(1)} %bitcast.4, f32[256,1024]{1,0:T(8,128)S(1)} %get-tuple-element.49.part_ref, bf16[1024,256]{1,0:T(8,128)(2,1)S(1)} %get-tuple-element.50.turned, ...), custom_call_target="tpu_custom_call", output_to_operand_aliasing={{1}: (15, {})} | custom-call | flops 100000000 | tf_op jit(solution)/shard_map/backward_rows/pallas_call | solution.py:398
  54.6 1.0 %collective-permute-done.22.refs_1_ = bf16[128,384]{1,0:T(8,128)(2,1)S(1)} collective-permute-done((bf16[128,384]{1,0:T(8,128)(2,1)S(1)}, bf16[128,384]{1,0:T(8,128)(2,1)S(1)}, u32[]{:S(2)}, u32[]{:S(2)}) %collective-permute-start.22) | collective-permute-done | bytes 98336 | tf_op jit(solution)/shard_map/ppermute | solution.py:455
  55.6 0.7 %last_sum.1 = bf16[128,384]{1,0:T(8,128)(2,1)} custom-call(f32[8,128]{1,0:T(8,128)S(1)} %get-tuple-element.56._, f32[128,384]{1,0:T(8,128)S(1)} %get-tuple-element.57.first_ref, bf16[128,384]{1,0:T(8,128)(2,1)S(1)} %collective-permute-done.8.refs_4_.refs_0_, bf16[128,384]{1,0:T(8,128)(2,1)S(1)} %collective-permute-done.22.refs_1_, ...), custom_call_target="tpu_custom_call" | custom-call | flops 1000000000 | tf_op jit(solution)/shard_map/last_sum/pallas_call | solution.py:430
  (39 shorter events, 0.3 us)
Async XLA Ops:
  0.6 1.0 %copy-start = (bf16[1,256,1024]{2,1,0:T(8,128)(2,1)S(1)}, bf16[1,256,1024]{2,1,0:T(8,128)(2,1)}, u32[]{:S(2)}) copy-start(bf16[1,256,1024]{2,1,0:T(8,128)(2,1)} %hidden_ref.3) | copy-start | bytes 1572868
  1.7 4.6 %copy-start.2 = (s32[128,2]{0,1:T(2,128)S(1)}, s32[128,2]{0,1:T(2,128)}, u32[]{:S(2)}) copy-start(s32[128,2]{0,1:T(2,128)} %param.7) | copy-start | bytes 3076
  1.7 4.6 %copy-start.3 = (f32[128,2]{0,1:T(2,128)S(1)}, f32[128,2]{0,1:T(2,128)}, u32[]{:S(2)}) copy-start(f32[128,2]{0,1:T(2,128)} %param.8) | copy-start | bytes 3076
  1.7 6.5 %copy-start.1 = (bf16[128,384]{1,0:T(8,128)(2,1)S(1)}, bf16[128,384]{1,0:T(8,128)(2,1)}, u32[]{:S(2)}) copy-start(bf16[128,384]{1,0:T(8,128)(2,1)} %grad_ref.3) | copy-start | bytes 294916
  5.7 2.4 %collective-permute-start = (bf16[4,2,2,64,384]{4,3,2,1,0:T(8,128)(2,1)S(1)}, bf16[4,2,2,64,384]{4,3,2,1,0:T(8,128)(2,1)S(1)}, u32[]{:S(2)}, u32[]{:S(2)}) collective-permute-start(bf16[4,2,2,64,384]{4,3,2,1,0:T(8,128)(2,1)S(1)} %get-tuple-element.35), channel_id=1, source_target_pairs={{0,8},{1,9},{2,10},{3,11},{4,12},{5,13},{6,14},{7,15},{8,0},{9,1},... | collective-permute-start | bytes 2359304 | tf_op jit(solution)/shard_map/ppermute | solution.py:452
  6.3 38.5 %slice-start = ((s8[6291456]{0:T(1024)(128)(4,1)}), s8[4194304]{0:T(1024)(128)(4,1)S(1)}, s32[]{:S(2)}) async-start(s8[6291456]{0:T(1024)(128)(4,1)} %bitcast.3), calls=%async_computation | async-start | bytes 8388608
  8.9 15.9 %collective-permute-start.2 = (bf16[656,384]{1,0:T(8,128)(2,1)S(1)}, bf16[656,384]{1,0:T(8,128)(2,1)S(1)}, u32[]{:S(2)}, u32[]{:S(2)}) collective-permute-start(bf16[656,384]{1,0:T(8,128)(2,1)S(1)} %get-tuple-element.39), channel_id=1, source_target_pairs={{0,16},{1,17},{2,18},{3,19},{4,20},{5,21},{6,22},{7,23},{8,24},{9,... | collective-permute-start | bytes 1511432 | tf_op jit(solution)/shard_map/ppermute | solution.py:452
  11.9 13.0 %collective-permute-start.1 = (bf16[5,128,384]{2,1,0:T(8,128)(2,1)S(1)}, bf16[5,128,384]{2,1,0:T(8,128)(2,1)S(1)}, u32[]{:S(2)}, u32[]{:S(2)}) collective-permute-start(bf16[5,128,384]{2,1,0:T(8,128)(2,1)S(1)} %get-tuple-element.37), channel_id=1, source_target_pairs={{0,1},{1,0},{2,3},{3,2},{4,5},{5,4},{6,7},{7,6},{8,9},{9,8},{10,11... | collective-permute-start | bytes 1474568 | tf_op jit(solution)/shard_map/ppermute | solution.py:452
  13.4 14.2 %collective-permute-start.12 = (bf16[128,384]{1,0:T(8,128)(2,1)S(1)}, bf16[128,384]{1,0:T(8,128)(2,1)S(1)}, u32[]{:S(2)}, u32[]{:S(2)}) collective-permute-start(bf16[128,384]{1,0:T(8,128)(2,1)S(1)} %copy-done.1), channel_id=1, source_target_pairs={{0,6},{1,7},{2,0},{3,1},{4,2},{5,3},{6,4},{7,5},{8,14},{9,15},{10,... | collective-permute-start | bytes 294920 | tf_op jit(solution)/shard_map/ppermute | solution.py:455
  17.0 10.6 %collective-permute-start.11 = (bf16[128,384]{1,0:T(8,128)(2,1)S(1)}, bf16[128,384]{1,0:T(8,128)(2,1)S(1)}, u32[]{:S(2)}, u32[]{:S(2)}) collective-permute-start(bf16[128,384]{1,0:T(8,128)(2,1)S(1)} %copy-done.1), channel_id=1, source_target_pairs={{0,4},{1,5},{2,6},{3,7},{4,0},{5,1},{6,2},{7,3},{8,12},{9,13},{10,... | collective-permute-start | bytes 294920 | tf_op jit(solution)/shard_map/ppermute | solution.py:455
  17.0 10.6 %collective-permute-start.10 = (bf16[128,384]{1,0:T(8,128)(2,1)S(1)}, bf16[128,384]{1,0:T(8,128)(2,1)S(1)}, u32[]{:S(2)}, u32[]{:S(2)}) collective-permute-start(bf16[128,384]{1,0:T(8,128)(2,1)S(1)} %copy-done.1), channel_id=1, source_target_pairs={{0,2},{1,3},{2,4},{3,5},{4,6},{5,7},{6,0},{7,1},{8,10},{9,11},{10,... | collective-permute-start | bytes 294920 | tf_op jit(solution)/shard_map/ppermute | solution.py:455
  25.5 9.0 %collective-permute-start.5 = (bf16[320,384]{1,0:T(8,128)(2,1)S(1)}, bf16[320,384]{1,0:T(8,128)(2,1)S(1)}, u32[]{:S(2)}, u32[]{:S(2)}) collective-permute-start(bf16[320,384]{1,0:T(8,128)(2,1)S(1)} %get-tuple-element.44), channel_id=1, source_target_pairs={{0,16},{1,17},{2,18},{3,19},{4,20},{5,21},{6,22},{7,23},{8,24},{9,... | collective-permute-start | bytes 737288 | tf_op jit(solution)/shard_map/ppermute | solution.py:452
  26.1 8.9 %collective-permute-start.6 = (bf16[320,384]{1,0:T(8,128)(2,1)S(1)}, bf16[320,384]{1,0:T(8,128)(2,1)S(1)}, u32[]{:S(2)}, u32[]{:S(2)}) collective-permute-start(bf16[320,384]{1,0:T(8,128)(2,1)S(1)} %get-tuple-element.45), channel_id=1, source_target_pairs={{0,1},{1,0},{2,3},{3,2},{4,5},{5,4},{6,7},{7,6},{8,9},{9,8},{10,11... | collective-permute-start | bytes 737288 | tf_op jit(solution)/shard_map/ppermute | solution.py:452
  27.6 17.2 %slice-start.1 = ((s8[6291456]{0:T(1024)(128)(4,1)}), s8[2097152]{0:T(1024)(128)(4,1)S(1)}, s32[]{:S(2)}) async-start(s8[6291456]{0:T(1024)(128)(4,1)} %bitcast.3), calls=%async_computation.1 | async-start | bytes 4194304
  27.6 11.8 %collective-permute-start.13 = (bf16[3,128,384]{2,1,0:T(8,128)(2,1)S(1)}, bf16[3,128,384]{2,1,0:T(8,128)(2,1)S(1)}, u32[]{:S(2)}, u32[]{:S(2)}) collective-permute-start(bf16[3,128,384]{2,1,0:T(8,128)(2,1)S(1)} %stack_blocks.1.refs_0_), channel_id=1, source_target_pairs={{0,1},{1,0},{2,3},{3,2},{4,5},{5,4},{6,7},{7,6},{8,9},{9,8},{10,11... | collective-permute-start | bytes 884744 | tf_op jit(solution)/shard_map/ppermute | solution.py:452
  28.2 11.2 %collective-permute-start.14 = (bf16[3,128,384]{2,1,0:T(8,128)(2,1)S(1)}, bf16[3,128,384]{2,1,0:T(8,128)(2,1)S(1)}, u32[]{:S(2)}, u32[]{:S(2)}) collective-permute-start(bf16[3,128,384]{2,1,0:T(8,128)(2,1)S(1)} %stack_blocks.1.refs_0_), channel_id=1, source_target_pairs={{0,16},{1,17},{2,18},{3,19},{4,20},{5,21},{6,22},{7,23},{8,24},{9,... | collective-permute-start | bytes 884744 | tf_op jit(solution)/shard_map/ppermute | solution.py:452
  29.7 11.3 %collective-permute-start.4 = (bf16[3,128,384]{2,1,0:T(8,128)(2,1)S(1)}, bf16[3,128,384]{2,1,0:T(8,128)(2,1)S(1)}, u32[]{:S(2)}, u32[]{:S(2)}) collective-permute-start(bf16[3,128,384]{2,1,0:T(8,128)(2,1)S(1)} %get-tuple-element.41.refs_0_), channel_id=1, source_target_pairs={{0,8},{1,9},{2,10},{3,11},{4,12},{5,13},{6,14},{7,15},{8,0},{9,1},... | collective-permute-start | bytes 884744 | tf_op jit(solution)/shard_map/ppermute | solution.py:452
  34.4 2.7 %collective-permute-start.3 = (f32[2,4,128]{2,1,0:T(4,128)S(1)}, f32[2,4,128]{2,1,0:T(4,128)S(1)}, u32[]{:S(2)}, u32[]{:S(2)}) collective-permute-start(f32[2,4,128]{2,1,0:T(4,128)S(1)} %get-tuple-element.40.metas), channel_id=1, source_target_pairs={{0,8},{1,9},{2,10},{3,11},{4,12},{5,13},{6,14},{7,15},{8,0},{9,1},... | collective-permute-start | bytes 12296 | tf_op jit(solution)/shard_map/ppermute | solution.py:452
  35.5 7.3 %collective-permute-start.8 = (bf16[128,384]{1,0:T(8,128)(2,1)S(1)}, bf16[128,384]{1,0:T(8,128)(2,1)S(1)}, u32[]{:S(2)}, u32[]{:S(2)}) collective-permute-start(bf16[128,384]{1,0:T(8,128)(2,1)S(1)} %get-tuple-element.47), channel_id=1, source_target_pairs={{0,2},{1,3},{2,4},{3,5},{4,6},{5,7},{6,0},{7,1},{8,10},{9,11},{10,... | collective-permute-start | bytes 294920 | tf_op jit(solution)/shard_map/ppermute | solution.py:455
  37.1 7.2 %collective-permute-start.9 = (bf16[128,384]{1,0:T(8,128)(2,1)S(1)}, bf16[128,384]{1,0:T(8,128)(2,1)S(1)}, u32[]{:S(2)}, u32[]{:S(2)}) collective-permute-start(bf16[128,384]{1,0:T(8,128)(2,1)S(1)} %get-tuple-element.48), channel_id=1, source_target_pairs={{0,6},{1,7},{2,0},{3,1},{4,2},{5,3},{6,4},{7,5},{8,14},{9,15},{10,... | collective-permute-start | bytes 294920 | tf_op jit(solution)/shard_map/ppermute | solution.py:455
  39.4 4.9 %collective-permute-start.7 = (bf16[128,384]{1,0:T(8,128)(2,1)S(1)}, bf16[128,384]{1,0:T(8,128)(2,1)S(1)}, u32[]{:S(2)}, u32[]{:S(2)}) collective-permute-start(bf16[128,384]{1,0:T(8,128)(2,1)S(1)} %get-tuple-element.46.refs_2_), channel_id=1, source_target_pairs={{0,8},{1,9},{2,10},{3,11},{4,12},{5,13},{6,14},{7,15},{8,0},{9,1},... | collective-permute-start | bytes 294920 | tf_op jit(solution)/shard_map/ppermute | solution.py:452
  39.4 7.5 %collective-permute-start.15 = (bf16[2,128,384]{2,1,0:T(8,128)(2,1)S(1)}, bf16[2,128,384]{2,1,0:T(8,128)(2,1)S(1)}, u32[]{:S(2)}, u32[]{:S(2)}) collective-permute-start(bf16[2,128,384]{2,1,0:T(8,128)(2,1)S(1)} %slice.8), channel_id=1, source_target_pairs={{0,16},{1,17},{2,18},{3,19},{4,20},{5,21},{6,22},{7,23},{8,24},{9,... | collective-permute-start | bytes 589832 | tf_op jit(solution)/shard_map/ppermute | solution.py:452
  41.0 6.5 %collective-permute-start.17 = (bf16[3,128,384]{2,1,0:T(8,128)(2,1)S(1)}, bf16[3,128,384]{2,1,0:T(8,128)(2,1)S(1)}, u32[]{:S(2)}, u32[]{:S(2)}) collective-permute-start(bf16[3,128,384]{2,1,0:T(8,128)(2,1)S(1)} %stack_blocks.1.refs_0_), channel_id=1, source_target_pairs={{0,8},{1,9},{2,10},{3,11},{4,12},{5,13},{6,14},{7,15},{8,0},{9,1},... | collective-permute-start | bytes 884744 | tf_op jit(solution)/shard_map/ppermute | solution.py:452
  42.8 4.6 %collective-permute-start.16 = (bf16[1,128,384]{2,1,0:T(8,128)(2,1)S(1)}, bf16[1,128,384]{2,1,0:T(8,128)(2,1)S(1)}, u32[]{:S(2)}, u32[]{:S(2)}) collective-permute-start(bf16[1,128,384]{2,1,0:T(8,128)(2,1)S(1)} %slice.9), channel_id=1, source_target_pairs={{0,1},{1,0},{2,3},{3,2},{4,5},{5,4},{6,7},{7,6},{8,9},{9,8},{10,11... | collective-permute-start | bytes 294920 | tf_op jit(solution)/shard_map/ppermute | solution.py:452
  44.3 5.5 %collective-permute-start.19 = (bf16[3,128,384]{2,1,0:T(8,128)(2,1)S(1)}, bf16[3,128,384]{2,1,0:T(8,128)(2,1)S(1)}, u32[]{:S(2)}, u32[]{:S(2)}) collective-permute-start(bf16[3,128,384]{2,1,0:T(8,128)(2,1)S(1)} %collective-permute-done.14.refs_2_), channel_id=1, source_target_pairs={{0,8},{1,9},{2,10},{3,11},{4,12},{5,13},{6,14},{7,15},{8,0},{9,1},... | collective-permute-start | bytes 884744 | tf_op jit(solution)/shard_map/ppermute | solution.py:452
  44.3 5.5 %collective-permute-start.18 = (bf16[3,128,384]{2,1,0:T(8,128)(2,1)S(1)}, bf16[3,128,384]{2,1,0:T(8,128)(2,1)S(1)}, u32[]{:S(2)}, u32[]{:S(2)}) collective-permute-start(bf16[3,128,384]{2,1,0:T(8,128)(2,1)S(1)} %collective-permute-done.13.refs_1_), channel_id=1, source_target_pairs={{0,8},{1,9},{2,10},{3,11},{4,12},{5,13},{6,14},{7,15},{8,0},{9,1},... | collective-permute-start | bytes 884744 | tf_op jit(solution)/shard_map/ppermute | solution.py:452
  47.0 2.8 %collective-permute-start.20 = (bf16[2,128,384]{2,1,0:T(8,128)(2,1)S(1)}, bf16[2,128,384]{2,1,0:T(8,128)(2,1)S(1)}, u32[]{:S(2)}, u32[]{:S(2)}) collective-permute-start(bf16[2,128,384]{2,1,0:T(8,128)(2,1)S(1)} %collective-permute-done.15.refs_3_), channel_id=1, source_target_pairs={{0,8},{1,9},{2,10},{3,11},{4,12},{5,13},{6,14},{7,15},{8,0},{9,1},... | collective-permute-start | bytes 589832 | tf_op jit(solution)/shard_map/ppermute | solution.py:452
  47.4 2.4 %collective-permute-start.21 = (bf16[1,128,384]{2,1,0:T(8,128)(2,1)S(1)}, bf16[1,128,384]{2,1,0:T(8,128)(2,1)S(1)}, u32[]{:S(2)}, u32[]{:S(2)}) collective-permute-start(bf16[1,128,384]{2,1,0:T(8,128)(2,1)S(1)} %collective-permute-done.16.refs_4_), channel_id=1, source_target_pairs={{0,8},{1,9},{2,10},{3,11},{4,12},{5,13},{6,14},{7,15},{8,0},{9,1},... | collective-permute-start | bytes 294920 | tf_op jit(solution)/shard_map/ppermute | solution.py:452
  47.6 8.1 %collective-permute-start.22 = (bf16[128,384]{1,0:T(8,128)(2,1)S(1)}, bf16[128,384]{1,0:T(8,128)(2,1)S(1)}, u32[]{:S(2)}, u32[]{:S(2)}) collective-permute-start(bf16[128,384]{1,0:T(8,128)(2,1)S(1)} %get-tuple-element.58), channel_id=1, source_target_pairs={{0,4},{1,5},{2,6},{3,7},{4,0},{5,1},{6,2},{7,3},{8,12},{9,13},{10,... | collective-permute-start | bytes 294920 | tf_op jit(solution)/shard_map/ppermute | solution.py:455
